TPU v7x, 32 devices: a whole 2x2x4 slice. The times are simulated.
32 devices in a mesh: layer: 4 (over y, x), tok: 8 (over z, core).
Axes of the slice: x: 2, y: 2, z: 4, core: 2. Of those that a mesh axis runs over, the one named last changes fastest.
Arguments:
- layer_inputs: bfloat16 [4, 256, 2048], P('layer', 'tok'), may hold values from -6 to 6
- layer_targets: bfloat16 [4, 256, 2048], P('layer', 'tok'), may hold values from -12 to 12
- row_order: int32 [256], replicated, may hold values from 0 to 255, each once
- encoder_weight: bfloat16 [4, 2048, 4096], P('layer', None, 'tok'), may hold values from -0.125 to 0.125
- encoder_bias: float32 [4, 4096], P('layer', 'tok'), may hold values from -3 to 3
- decoder_weight: bfloat16 [4, 4, 4096, 2048], P('layer', None, 'tok'), may hold values from -1 to 1
- decoder_bias: float32 [4, 2048], P('layer'), may hold values from -0.6 to 0.6
Outputs:
- encoder_grad: bfloat16 [4, 2048, 4096], P('layer', None, 'tok')
- feature_grad: float32 [4, 4096], P('layer', 'tok')
- decoder_grad: bfloat16 [4, 4, 4096, 2048], P('layer', None, 'tok')
- output_grad: float32 [4, 2048], P('layer')
Inputs may be any that keep to these rules, and one draw needn't show every extreme that they name: Row i of layer_targets belongs to the token in row row_order[i] of layer_inputs, in every layer; each row index appears once.
All inputs are finite; a program needn't handle non-finite values.
Results may differ from a plain program's by a relative error of at most 0.015.
Values may be sent and summed in bfloat16 or wider, within the bound.
No kernel may reach another device: no remote copies, remote signals or barrier semaphores. Data moves between devices by JAX's collectives and lax.ppermute only.
A program may use at most 128 MiB of HBM per device.

v0:
```python
import math

import jax
import jax.numpy as jnp
from jax import lax
from jax.sharding import PartitionSpec as P


def on_device(
    layer_inputs,
    layer_targets,
    row_order,
    encoder_weight,
    encoder_bias,
    decoder_weight,
    decoder_bias,
):
    layers = decoder_weight.shape[1]
    row_total = row_order.shape[0]
    loss_scale = 1.0 / math.sqrt(row_total)
    target = lax.axis_index("layer")
    weights = decoder_weight[0]
    width = weights.shape[2]
    features = weights.shape[1]
    contract_rows = (((0,), (0,)), ((), ()))
    contract_cols = (((1,), (1,)), ((), ()))
    squares = jnp.sum(jnp.square(weights.astype(jnp.float32)), axis=2)
    active = (jnp.arange(layers) <= target)[:, None]
    norm_sq = lax.psum(jnp.where(active, squares, 0.0), "layer")
    feature_norms = jnp.sqrt(norm_sq + 1e-06)
    gathered = lax.all_gather(layer_inputs[0], "tok", axis=0, tiled=True)
    ordered = jnp.take(gathered, row_order, axis=0)
    pre_act = (
        jnp.dot(ordered, encoder_weight[0], preferred_element_type=jnp.float32) + encoder_bias[0]
    )
    own_acts = jnp.maximum(pre_act, 0.0).astype(jnp.bfloat16)
    sources = lax.all_gather(own_acts[None], "layer", axis=0, tiled=True)

    def add_source(source, partial_value):
        act_block = lax.dynamic_index_in_dim(sources, source, 0, keepdims=False)
        chosen_weights = lax.dynamic_index_in_dim(weights, source, 0, keepdims=False)
        return partial_value + jnp.dot(
            act_block, chosen_weights, preferred_element_type=jnp.float32
        )

    local_sum = lax.psum_scatter(
        lax.fori_loop(
            0,
            target + 1,
            add_source,
            jnp.zeros((layer_targets.shape[1] * lax.axis_size("tok"), width), jnp.float32),
        ),
        "tok",
        scatter_dimension=0,
        tiled=True,
    )
    resid_full = (local_sum + decoder_bias[0] - layer_targets[0].astype(jnp.float32)) * loss_scale
    bias_grad = lax.psum(jnp.sum(resid_full, axis=0), "tok")
    residual = lax.all_gather(resid_full.astype(jnp.bfloat16), "tok", axis=0, tiled=True)

    def source_term(source):

        def source_compute():
            chosen_weights = lax.dynamic_index_in_dim(weights, source, 0, keepdims=False)
            return lax.dot_general(
                residual, chosen_weights, contract_cols, preferred_element_type=jnp.float32
            )

        def source_nothing():
            return jnp.zeros((row_total, features), jnp.float32)

        return lax.cond(source <= target, source_compute, source_nothing)

    grad_acts = lax.psum_scatter(
        lax.map(source_term, jnp.arange(1 * lax.axis_size("layer"), dtype=jnp.int32)),
        "layer",
        scatter_dimension=0,
        tiled=True,
    )[0]
    own_norm = lax.dynamic_index_in_dim(feature_norms, target, 0, keepdims=False)
    grad_pre = jnp.where(pre_act > 0, grad_acts + own_norm * loss_scale, 0.0)
    grad_low = grad_pre.astype(jnp.bfloat16)
    encoder_grad = lax.dot_general(
        ordered, grad_low, contract_rows, preferred_element_type=jnp.float32
    ).astype(jnp.bfloat16)
    feature_grad = jnp.sum(grad_pre, axis=0)
    act_sums = jnp.sum(sources.astype(jnp.float32), axis=1)

    def block_grad(source):

        def block_compute():
            chosen_acts = lax.dynamic_index_in_dim(sources, source, 0, keepdims=False)
            chosen_weights = lax.dynamic_index_in_dim(weights, source, 0, keepdims=False)
            chosen_sums = lax.dynamic_index_in_dim(act_sums, source, 0, keepdims=False)
            chosen_norms = lax.dynamic_index_in_dim(feature_norms, source, 0, keepdims=False)
            factor = chosen_sums * loss_scale / chosen_norms
            product = lax.dot_general(
                chosen_acts, residual, contract_rows, preferred_element_type=jnp.float32
            )
            return (product + factor[:, None] * chosen_weights.astype(jnp.float32)).astype(
                jnp.bfloat16
            )

        def block_nothing():
            return jnp.zeros((features, width), jnp.bfloat16)

        return lax.cond(source <= target, block_compute, block_nothing)

    decoder_grad = lax.map(block_grad, jnp.arange(layers, dtype=jnp.int32))
    return (encoder_grad[None], feature_grad[None], decoder_grad[None], bias_grad[None])


def solution(mesh):
    placed = (
        P("layer", "tok", None),
        P("layer", "tok", None),
        P(),
        P("layer", None, "tok"),
        P("layer", "tok"),
        P("layer", None, "tok", None),
        P("layer", None),
    )
    return jax.shard_map(
        on_device,
        mesh=mesh,
        in_specs=placed,
        out_specs=(
            P("layer", None, "tok"),
            P("layer", "tok"),
            P("layer", None, "tok", None),
            P("layer", None),
        ),
        check_vma=False,
    )
```

profile of v0, /device:TPU:7, one launch (start us, length us, event | category | flops | bytes accessed | tf_op | source)
XLA Modules:
  0.0 249.2 jit_solution(15499355788157247148)
XLA Ops:
  7.2 0.7 all-gather.8.cloned.1.call-update
  8.0 0.7 compare_select_fusion
  8.7 0.7 compare_and_fusion
  9.3 24.0 %all-gather.8.cloned.1.call-done = bf16[1,256,2048]{2,1,0:T(8,128)(2,1)} async-done(((bf16[1,32,2048]{2,1,0:T(8,128)(2,1)}), bf16[1,256,2048]{2,1,0:T(8,128)(2,1)}) %all-gather.8.cloned.1.call-update) | async-done | bytes 1048592 | tf_op jit(solution)/shard_map/all_gather | solution.py:31
  33.3 3.7 %gather_fusion = bf16[256,2048]{1,0:T(8,128)(2,1)S(1)} fusion(bf16[256,2048]{1,0:T(8,128)(2,1)} %bitcast.72, s32[1024]{0:T(1024)S(1)} %pad_clamp_fusion), kind=kCustom, calls=%fused_computation | custom fusion | bytes 2098176 | tf_op jit(solution)/shard_map/jit(_take)/gather | solution.py:32
  37.1 1.6 maximum_convert_fusion
  38.7 0.0 reduce-scatter.5.cloned.1.call-start
  38.8 25.1 %all-gather.10.cloned.1.call-done = bf16[1024,512]{1,0:T(8,128)(2,1)} async-done(((bf16[256,512]{1,0:T(8,128)(2,1)}), bf16[1024,512]{1,0:T(8,128)(2,1)}) %all-gather.10.cloned.1.call-update) | async-done | bytes 1048592 | tf_op jit(solution)/shard_map/all_gather | solution.py:37
  63.9 1.6 broadcast_in_dim.73
  65.4 17.3 %while.30 = (s32[]{:T(128)}, f32[256,2048]{1,0:T(8,128)}, s32[]{:T(128)}, bf16[4,256,512]{2,1,0:T(8,128)(2,1)}, bf16[4,512,2048]{2,1,0:T(8,128)(2,1)}, /*index=5*/s32[]{:T(128)}, s32[]{:T(128)}, s32[]{:T(128)}) while((s32[]{:T(128)}, f32[256,2048]{1,0:T(8,128)}, s32[]{:T(128)}, bf16[4,256,512]{2,1,0:T(8,128)(2,1)}, ...), condition=%wide.region_1.2_spmd, body=%wide.region_0.0_spmd.sunk | while | flops 537395200 | bytes 6554743 | solution.py:47
  65.4 4.3 %convolution_add_fusion.2 = f32[256,2048]{1,0:T(8,128)} fusion(f32[256,2048]{1,0:T(8,128)} %get-tuple-element.326, bf16[4,512,2048]{2,1,0:T(8,128)(2,1)} %get-tuple-element.337, s32[]{:T(128)S(6)} %select_n.59, bf16[4,256,512]{2,1,0:T(8,128)(2,1)} %get-tuple-element.336), kind=kOutput, calls=%fused_computation.1.clone.1 | convolution fusion | flops 537395200 | bytes 6554624 | tf_op jit(solution)/shard_map/while/body/dot_general | solution.py:42
  69.8 4.3 %convolution_add_fusion.2 = f32[256,2048]{1,0:T(8,128)} fusion(f32[256,2048]{1,0:T(8,128)} %get-tuple-element.326, bf16[4,512,2048]{2,1,0:T(8,128)(2,1)} %get-tuple-element.337, s32[]{:T(128)S(6)} %select_n.59, bf16[4,256,512]{2,1,0:T(8,128)(2,1)} %get-tuple-element.336), kind=kOutput, calls=%fused_computation.1.clone.1 | convolution fusion | flops 537395200 | bytes 6554624 | tf_op jit(solution)/shard_map/while/body/dot_general | solution.py:42
  74.1 4.3 %convolution_add_fusion.2 = f32[256,2048]{1,0:T(8,128)} fusion(f32[256,2048]{1,0:T(8,128)} %get-tuple-element.326, bf16[4,512,2048]{2,1,0:T(8,128)(2,1)} %get-tuple-element.337, s32[]{:T(128)S(6)} %select_n.59, bf16[4,256,512]{2,1,0:T(8,128)(2,1)} %get-tuple-element.336), kind=kOutput, calls=%fused_computation.1.clone.1 | convolution fusion | flops 537395200 | bytes 6554624 | tf_op jit(solution)/shard_map/while/body/dot_general | solution.py:42
  78.4 4.3 %convolution_add_fusion.2 = f32[256,2048]{1,0:T(8,128)} fusion(f32[256,2048]{1,0:T(8,128)} %get-tuple-element.326, bf16[4,512,2048]{2,1,0:T(8,128)(2,1)} %get-tuple-element.337, s32[]{:T(128)S(6)} %select_n.59, bf16[4,256,512]{2,1,0:T(8,128)(2,1)} %get-tuple-element.336), kind=kOutput, calls=%fused_computation.1.clone.1 | convolution fusion | flops 537395200 | bytes 6554624 | tf_op jit(solution)/shard_map/while/body/dot_general | solution.py:42
  82.8 0.0 all-gather.6.cloned.1.call-start
  82.8 33.9 %reduce-scatter.5.cloned.1.call-done = f32[32,2048]{1,0:T(8,128)} async-done(((f32[256,2048]{1,0:T(8,128)}), f32[32,2048]{1,0:T(8,128)}) %reduce-scatter.5.cloned.1.call-update) | async-done | bytes 262160 | tf_op jit(solution)/shard_map/reduce_scatter | solution.py:46
  116.8 1.7 fusion.29
  118.5 0.0 reduce-scatter.7.cloned.1.call-start
  118.5 24.3 %all-gather.6.cloned.1.call-done = bf16[256,2048]{1,0:T(8,128)(2,1)} async-done(((bf16[32,2048]{1,0:T(8,128)(2,1)}), bf16[256,2048]{1,0:T(8,128)(2,1)}) %all-gather.6.cloned.1.call-update) | async-done | bytes 1048592 | tf_op jit(solution)/shard_map/all_gather | solution.py:59
  142.8 27.4 %while.31 = (s32[]{:T(128)}, f32[4,256,512]{2,1,0:T(8,128)}, s32[4]{0:T(128)S(1)}, s32[]{:T(128)}, bf16[4,512,2048]{2,1,0:T(8,128)(2,1)}, /*index=5*/bf16[256,2048]{1,0:T(8,128)(2,1)}, s32[]{:T(128)}) while((s32[]{:T(128)}, f32[4,256,512]{2,1,0:T(8,128)}, s32[4]{0:T(128)S(1)}, s32[]{:T(128)}, bf16[4,512,2048]{2,1,0:T(8,128)(2,1)}, ...), condition=%wide.region_6.7_spmd, body=%wide.region_3.6_spmd.sunk | while | flops 536870912 | bytes 5767853 | solution.py:75
  142.8 0.6 dynamic_slice.65
  144.0 4.6 %conditional.4 = (f32[1,256,512]{1,2,0:T(8,128)S(1)}) conditional(s32[]{:T(128)} %convert_element_type.63, () %tuple.69, (s32[]{:T(128)}, bf16[4,512,2048]{2,1,0:T(8,128)(2,1)}, bf16[256,2048]{1,0:T(8,128)(2,1)}) %tuple.70), branch_computations={%region_4.4_spmd, %region_5.5_spmd} | conditional | flops 536870912 | bytes 3670062 | solution.py:72
  146.0 2.6 %fusion.8 = f32[1,256,512]{1,2,0:T(8,128)S(1)} fusion(bf16[256,2048]{1,0:T(8,128)(2,1)} %get-tuple-element.115, bf16[4,512,2048]{2,1,0:T(8,128)(2,1)} %get-tuple-element.113, s32[]{:T(128)S(6)} %select_n.31), kind=kOutput, calls=%fused_computation.10 | convolution fusion | flops 536870912 | bytes 3670020 | tf_op jit(solution)/shard_map/while/body/eval_jaxpr/cond/branch_1_fun/dot_general | solution.py:65
  148.6 0.2 copy.20
  148.8 0.8 constant_dynamic-update-slice_fusion.4
  149.6 0.6 dynamic_slice.65
  150.9 4.6 %conditional.4 = (f32[1,256,512]{1,2,0:T(8,128)S(1)}) conditional(s32[]{:T(128)} %convert_element_type.63, () %tuple.69, (s32[]{:T(128)}, bf16[4,512,2048]{2,1,0:T(8,128)(2,1)}, bf16[256,2048]{1,0:T(8,128)(2,1)}) %tuple.70), branch_computations={%region_4.4_spmd, %region_5.5_spmd} | conditional | flops 536870912 | bytes 3670062 | solution.py:72
  152.8 2.6 %fusion.8 = f32[1,256,512]{1,2,0:T(8,128)S(1)} fusion(bf16[256,2048]{1,0:T(8,128)(2,1)} %get-tuple-element.115, bf16[4,512,2048]{2,1,0:T(8,128)(2,1)} %get-tuple-element.113, s32[]{:T(128)S(6)} %select_n.31), kind=kOutput, calls=%fused_computation.10 | convolution fusion | flops 536870912 | bytes 3670020 | tf_op jit(solution)/shard_map/while/body/eval_jaxpr/cond/branch_1_fun/dot_general | solution.py:65
  155.4 0.2 copy.20
  155.6 0.8 constant_dynamic-update-slice_fusion.4
  156.5 0.6 dynamic_slice.65
  157.7 4.6 %conditional.4 = (f32[1,256,512]{1,2,0:T(8,128)S(1)}) conditional(s32[]{:T(128)} %convert_element_type.63, () %tuple.69, (s32[]{:T(128)}, bf16[4,512,2048]{2,1,0:T(8,128)(2,1)}, bf16[256,2048]{1,0:T(8,128)(2,1)}) %tuple.70), branch_computations={%region_4.4_spmd, %region_5.5_spmd} | conditional | flops 536870912 | bytes 3670062 | solution.py:72
  159.7 2.6 %fusion.8 = f32[1,256,512]{1,2,0:T(8,128)S(1)} fusion(bf16[256,2048]{1,0:T(8,128)(2,1)} %get-tuple-element.115, bf16[4,512,2048]{2,1,0:T(8,128)(2,1)} %get-tuple-element.113, s32[]{:T(128)S(6)} %select_n.31), kind=kOutput, calls=%fused_computation.10 | convolution fusion | flops 536870912 | bytes 3670020 | tf_op jit(solution)/shard_map/while/body/eval_jaxpr/cond/branch_1_fun/dot_general | solution.py:65
  162.3 0.2 copy.20
  162.5 0.8 constant_dynamic-update-slice_fusion.4
  163.3 0.6 dynamic_slice.65
  164.6 4.6 %conditional.4 = (f32[1,256,512]{1,2,0:T(8,128)S(1)}) conditional(s32[]{:T(128)} %convert_element_type.63, () %tuple.69, (s32[]{:T(128)}, bf16[4,512,2048]{2,1,0:T(8,128)(2,1)}, bf16[256,2048]{1,0:T(8,128)(2,1)}) %tuple.70), branch_computations={%region_4.4_spmd, %region_5.5_spmd} | conditional | flops 536870912 | bytes 3670062 | solution.py:72
  166.5 2.6 %fusion.8 = f32[1,256,512]{1,2,0:T(8,128)S(1)} fusion(bf16[256,2048]{1,0:T(8,128)(2,1)} %get-tuple-element.115, bf16[4,512,2048]{2,1,0:T(8,128)(2,1)} %get-tuple-element.113, s32[]{:T(128)S(6)} %select_n.31), kind=kOutput, calls=%fused_computation.10 | convolution fusion | flops 536870912 | bytes 3670020 | tf_op jit(solution)/shard_map/while/body/eval_jaxpr/cond/branch_1_fun/dot_general | solution.py:65
  169.1 0.2 copy.20
  169.3 0.8 constant_dynamic-update-slice_fusion.4
  170.2 5.2 %multiply_reduce_fusion = f32[4,512]{1,0:T(4,128)S(1)} fusion(bf16[1,4,512,2048]{3,2,1,0:T(8,128)(2,1)} %bitcast.71), kind=kLoop, calls=%fused_computation.22 | loop fusion | flops 12580864 | bytes 8396800 | tf_op jit(solution)/shard_map/reduce_sum | solution.py:27
  175.4 0.1 broadcast_select_fusion.3
  175.5 6.0 %psum.14 = f32[4,512]{1,0:T(4,128)S(1)} all-reduce(f32[4,512]{1,0:T(4,128)S(1)} %broadcast_select_fusion.3), channel_id=1, replica_groups=mesh['layer'=4,'tok'=8] {'layer'}, use_global_device_ids=true, to_apply=%region_9.10 | all-reduce | flops 2048 | bytes 16384 | tf_op jit(solution)/shard_map/psum | solution.py:29
  181.5 1.4 convert_reduce_fusion
  182.9 15.8 %psum.15 = f32[1,2048]{1,0:T(1,128)} all-reduce(f32[1,2048]{1,0:T(1,128)S(1)} %bitcast.76), channel_id=1, replica_groups=mesh['layer'=4,'tok'=8] {'tok'}, use_global_device_ids=true, to_apply=%region_17.18 | all-reduce | flops 2048 | bytes 16384 | tf_op jit(solution)/shard_map/psum | solution.py:58
  198.7 39.5 %while.32 = (s32[]{:T(128)}, bf16[4,512,2048]{2,1,0:T(8,128)(2,1)}, s32[4]{0:T(128)S(1)}, s32[]{:T(128)}, bf16[4,256,512]{2,1,0:T(8,128)(2,1)}, /*index=5*/bf16[...) while((s32[]{:T(128)}, bf16[4,512,2048]{2,1,0:T(8,128)(2,1)}, ...), condition=%wide.region_15.16_spmd, body=%wide.region_12.15_spmd.sunk | while | flops 541066240 | bytes 9709277 | solution.py:109
  198.7 0.6 dynamic_slice.66
  199.9 5.6 %conditional.5 = (bf16[1,512,2048]{2,1,0:T(8,128)(2,1)}) conditional(s32[]{:T(128)} %convert_element_type.64, () %tuple.72, (s32[]{:T(128)}, bf16[4,256,512]{2,1,0:T(8,128)(2,1)}, bf16[256,2048]{1,0:T(8,128)(2,1)S(1)}, f32[4,512]{1,0:T(4,128)S(1)}, f32[4,512]{1,0:T(4,128)S(1)}, /*index=5*/bf16[4,512,2048]{2,1,0:T(8,128)(2,1)}) %tuple.73), branch_computations={%region_13.13_spmd, %region_14.14_spmd} | conditional | flops 541066240 | bytes 5514286 | solution.py:107
  201.6 3.8 %fusion.14 = bf16[1,512,2048]{2,1,0:T(8,128)(2,1)} fusion(bf16[256,2048]{1,0:T(8,128)(2,1)S(1)} %get-tuple-element.125, bf16[4,512,2048]{2,1,0:T(8,128)(2,1)} %get-tuple-element.128, s32[]{:T(128)S(6)} %select_n.32, f32[512]{0:T(512)S(1)} %bitcast.75, bf16[4,256,512]{2,1,0:T(8,128)(2,1)} %get-tuple-element.123), kind=kOutput, calls=%fused_computation.16 | convolution fusion | flops 541065216 | bytes 5508096 | tf_op jit(solution)/shard_map/while/body/eval_jaxpr/cond/branch_1_fun/dot_general | solution.py:97
  205.5 3.2 %constant_dynamic-update-slice_fusion.5 = bf16[4,512,2048]{2,1,0:T(8,128)(2,1)} fusion(bf16[4,512,2048]{2,1,0:T(8,128)(2,1)} %get-tuple-element.373, bf16[1,512,2048]{2,1,0:T(8,128)(2,1)} %get-tuple-element.393, s32[]{:T(128)} %get-tuple-element.372), kind=kLoop, calls=%fused_computation.21.clone.1 | loop fusion | bytes 4194816 | tf_op jit(solution)/shard_map/while/body/jit(dynamic_update_index_in_dim)/dynamic_update_slice | solution.py:109
  208.6 0.6 dynamic_slice.66
  209.8 5.5 %conditional.5 = (bf16[1,512,2048]{2,1,0:T(8,128)(2,1)}) conditional(s32[]{:T(128)} %convert_element_type.64, () %tuple.72, (s32[]{:T(128)}, bf16[4,256,512]{2,1,0:T(8,128)(2,1)}, bf16[256,2048]{1,0:T(8,128)(2,1)S(1)}, f32[4,512]{1,0:T(4,128)S(1)}, f32[4,512]{1,0:T(4,128)S(1)}, /*index=5*/bf16[4,512,2048]{2,1,0:T(8,128)(2,1)}) %tuple.73), branch_computations={%region_13.13_spmd, %region_14.14_spmd} | conditional | flops 541066240 | bytes 5514286 | solution.py:107
  211.5 3.8 %fusion.14 = bf16[1,512,2048]{2,1,0:T(8,128)(2,1)} fusion(bf16[256,2048]{1,0:T(8,128)(2,1)S(1)} %get-tuple-element.125, bf16[4,512,2048]{2,1,0:T(8,128)(2,1)} %get-tuple-element.128, s32[]{:T(128)S(6)} %select_n.32, f32[512]{0:T(512)S(1)} %bitcast.75, bf16[4,256,512]{2,1,0:T(8,128)(2,1)} %get-tuple-element.123), kind=kOutput, calls=%fused_computation.16 | convolution fusion | flops 541065216 | bytes 5508096 | tf_op jit(solution)/shard_map/while/body/eval_jaxpr/cond/branch_1_fun/dot_general | solution.py:97
  215.3 3.2 %constant_dynamic-update-slice_fusion.5 = bf16[4,512,2048]{2,1,0:T(8,128)(2,1)} fusion(bf16[4,512,2048]{2,1,0:T(8,128)(2,1)} %get-tuple-element.373, bf16[1,512,2048]{2,1,0:T(8,128)(2,1)} %get-tuple-element.393, s32[]{:T(128)} %get-tuple-element.372), kind=kLoop, calls=%fused_computation.21.clone.1 | loop fusion | bytes 4194816 | tf_op jit(solution)/shard_map/while/body/jit(dynamic_update_index_in_dim)/dynamic_update_slice | solution.py:109
  218.5 0.6 dynamic_slice.66
  219.7 5.6 %conditional.5 = (bf16[1,512,2048]{2,1,0:T(8,128)(2,1)}) conditional(s32[]{:T(128)} %convert_element_type.64, () %tuple.72, (s32[]{:T(128)}, bf16[4,256,512]{2,1,0:T(8,128)(2,1)}, bf16[256,2048]{1,0:T(8,128)(2,1)S(1)}, f32[4,512]{1,0:T(4,128)S(1)}, f32[4,512]{1,0:T(4,128)S(1)}, /*index=5*/bf16[4,512,2048]{2,1,0:T(8,128)(2,1)}) %tuple.73), branch_computations={%region_13.13_spmd, %region_14.14_spmd} | conditional | flops 541066240 | bytes 5514286 | solution.py:107
  221.4 3.8 %fusion.14 = bf16[1,512,2048]{2,1,0:T(8,128)(2,1)} fusion(bf16[256,2048]{1,0:T(8,128)(2,1)S(1)} %get-tuple-element.125, bf16[4,512,2048]{2,1,0:T(8,128)(2,1)} %get-tuple-element.128, s32[]{:T(128)S(6)} %select_n.32, f32[512]{0:T(512)S(1)} %bitcast.75, bf16[4,256,512]{2,1,0:T(8,128)(2,1)} %get-tuple-element.123), kind=kOutput, calls=%fused_computation.16 | convolution fusion | flops 541065216 | bytes 5508096 | tf_op jit(solution)/shard_map/while/body/eval_jaxpr/cond/branch_1_fun/dot_general | solution.py:97
  225.2 3.2 %constant_dynamic-update-slice_fusion.5 = bf16[4,512,2048]{2,1,0:T(8,128)(2,1)} fusion(bf16[4,512,2048]{2,1,0:T(8,128)(2,1)} %get-tuple-element.373, bf16[1,512,2048]{2,1,0:T(8,128)(2,1)} %get-tuple-element.393, s32[]{:T(128)} %get-tuple-element.372), kind=kLoop, calls=%fused_computation.21.clone.1 | loop fusion | bytes 4194816 | tf_op jit(solution)/shard_map/while/body/jit(dynamic_update_index_in_dim)/dynamic_update_slice | solution.py:109
  228.4 0.6 dynamic_slice.66
  229.5 5.5 %conditional.5 = (bf16[1,512,2048]{2,1,0:T(8,128)(2,1)}) conditional(s32[]{:T(128)} %convert_element_type.64, () %tuple.72, (s32[]{:T(128)}, bf16[4,256,512]{2,1,0:T(8,128)(2,1)}, bf16[256,2048]{1,0:T(8,128)(2,1)S(1)}, f32[4,512]{1,0:T(4,128)S(1)}, f32[4,512]{1,0:T(4,128)S(1)}, /*index=5*/bf16[4,512,2048]{2,1,0:T(8,128)(2,1)}) %tuple.73), branch_computations={%region_13.13_spmd, %region_14.14_spmd} | conditional | flops 541066240 | bytes 5514286 | solution.py:107
  231.3 3.8 %fusion.14 = bf16[1,512,2048]{2,1,0:T(8,128)(2,1)} fusion(bf16[256,2048]{1,0:T(8,128)(2,1)S(1)} %get-tuple-element.125, bf16[4,512,2048]{2,1,0:T(8,128)(2,1)} %get-tuple-element.128, s32[]{:T(128)S(6)} %select_n.32, f32[512]{0:T(512)S(1)} %bitcast.75, bf16[4,256,512]{2,1,0:T(8,128)(2,1)} %get-tuple-element.123), kind=kOutput, calls=%fused_computation.16 | convolution fusion | flops 541065216 | bytes 5508096 | tf_op jit(solution)/shard_map/while/body/eval_jaxpr/cond/branch_1_fun/dot_general | solution.py:97
  235.1 3.2 %constant_dynamic-update-slice_fusion.5 = bf16[4,512,2048]{2,1,0:T(8,128)(2,1)} fusion(bf16[4,512,2048]{2,1,0:T(8,128)(2,1)} %get-tuple-element.373, bf16[1,512,2048]{2,1,0:T(8,128)(2,1)} %get-tuple-element.393, s32[]{:T(128)} %get-tuple-element.372), kind=kLoop, calls=%fused_computation.21.clone.1 | loop fusion | bytes 4194816 | tf_op jit(solution)/shard_map/while/body/jit(dynamic_update_index_in_dim)/dynamic_update_slice | solution.py:109
  238.3 3.8 %fusion.18 = bf16[1,2048,512]{2,1,0:T(8,128)(2,1)} fusion(bf16[256,2048]{1,0:T(8,128)(2,1)} %copy-done.2, pred[256]{0:T(512)(128)(4,1)S(1)} %compare_and_fusion, f32[1,256,512]{2,1,0:T(8,128)} %reduce-scatter.7.cloned.1.call-done, f32[256,512]{1,0:T(8,128)} %get-tuple-element.192, f32[512]{0:T(512)S(1)} %bitcast.77), kind=kOutput, calls=%fused_computation.24 | convolution fusion | flops 538968064 | bytes 4196608 | tf_op jit(solution)/shard_map/dot_general | solution.py:83
  242.0 0.7 fusion.27
  (35 shorter events, 0.3 us)
Async XLA Ops:
  7.2 29.9 %copy-start = (bf16[1,2048,512]{2,1,0:T(8,128)(2,1)S(1)}, bf16[1,2048,512]{2,1,0:T(8,128)(2,1)}, u32[]{:S(2)}) copy-start(bf16[1,2048,512]{2,1,0:T(8,128)(2,1)} %param.20) | copy-start | bytes 6291460
  7.2 26.1 %all-gather.8.cloned.1.call-start = ((), (), s32[]{:S(2)}) async-start(), calls=%async_computation.4 | async-start | bytes 1179648 | tf_op jit(solution)/shard_map/all_gather | solution.py:31
  7.9 55.9 %all-gather.10.cloned.1.call-start = ((), (), s32[]{:S(2)}) async-start(), calls=%async_computation.5 | async-start | bytes 1310720 | tf_op jit(solution)/shard_map/all_gather | solution.py:37
  33.3 3.8 %copy-start.7 = (f32[1,512]{1,0:T(1,128)S(1)}, f32[1,512]{1,0:T(1,128)}, u32[]{:S(2)}) copy-start(f32[1,512]{1,0:T(1,128)} %param.21) | copy-start | bytes 6148
  37.1 1.7 copy-start.2
  38.7 78.0 %reduce-scatter.5.cloned.1.call-start = ((), (), s32[]{:S(2)}) async-start(), calls=%async_computation.2 | async-start | bytes 2359296 | tf_op jit(solution)/shard_map/reduce_scatter | solution.py:46
  82.8 34.0 %copy-start.5 = (bf16[1,32,2048]{2,1,0:T(8,128)(2,1)S(1)}, bf16[1,32,2048]{2,1,0:T(8,128)(2,1)}, u32[]{:S(2)}) copy-start(bf16[1,32,2048]{2,1,0:T(8,128)(2,1)} %param.18) | copy-start | bytes 393220
  82.8 34.0 %copy-start.6 = (f32[1,2048]{1,0:T(1,128)S(1)}, f32[1,2048]{1,0:T(1,128)}, u32[]{:S(2)}) copy-start(f32[1,2048]{1,0:T(1,128)} %param.23) | copy-start | bytes 24580
  82.8 60.0 %all-gather.6.cloned.1.call-start = ((), (), s32[]{:S(2)}) async-start(), calls=%async_computation.3 | async-start | bytes 1179648 | tf_op jit(solution)/shard_map/all_gather | solution.py:59
  118.5 119.8 %reduce-scatter.7.cloned.1.call-start = ((), (), s32[]{:S(2)}) async-start(), calls=%async_computation.6 | async-start | bytes 2621440
  170.2 28.5 %copy-start.1 = (bf16[256,2048]{1,0:T(8,128)(2,1)S(1)}, bf16[256,2048]{1,0:T(8,128)(2,1)}, u32[]{:S(2)}) copy-start(bf16[256,2048]{1,0:T(8,128)(2,1)} %get-tuple-element.405) | copy-start | bytes 3145732
  238.2 3.8 %copy-start.3 = (f32[256,512]{1,0:T(8,128)S(1)}, f32[256,512]{1,0:T(8,128)}, u32[]{:S(2)}) copy-start(f32[256,512]{1,0:T(8,128)} %get-tuple-element.192) | copy-start | bytes 1572868
  238.3 3.8 %copy-start.4 = (f32[1,256,512]{2,1,0:T(8,128)S(1)}, f32[1,256,512]{2,1,0:T(8,128)}, u32[]{:S(2)}) copy-start(f32[1,256,512]{2,1,0:T(8,128)} %reduce-scatter.7.cloned.1.call-done) | copy-start | bytes 1572868
Sparse Core Ops, SparseCore 0:
  9.6 23.6 all-gather.7
  38.9 24.9 all-gather.9
  82.9 33.8 reduce-scatter.4
  118.8 23.9 all-gather.5
  170.3 33.9 reduce-scatter.6
where the time goes:
time: 250 us; the launch traced here: 249 us
  waiting for transfers between devices  108 us (43%)
  matrix products  48.3 us (19%)
  local copies, waits for them, and re-layouts  26.8 us (11%)
  blocking collectives  21.8 us (9%)
  loops' own time  19.8 us (8%)
  between operations  13.9 us (6%)
  other arithmetic  10.4 us (4%)
    reduce_scatter x1, waiting for transfers between devices, on_device(): lax.psum_scatter(lax.fori_loop(0, target + 1, add_source, jnp.zeros((laye...  33.9 us
    all_gather x1, waiting for transfers between devices, on_device(): sources = lax.all_gather(own_acts[None], 'layer', axis=0, tiled=True)  25.1 us
    all_gather x1, waiting for transfers between devices, on_device(): lax.all_gather(resid_full.astype(jnp.bfloat16), 'tok', axis=0, tiled=True)  24.3 us
    all_gather x1, waiting for transfers between devices, on_device(): gathered = lax.all_gather(layer_inputs[0], 'tok', axis=0, tiled=True)  24 us
    dot_general x4, matrix products, add_source(): jnp.dot(act_block, chosen_weights, preferred_element_type=jnp.float32)  17.3 us
    psum x1, blocking collectives, on_device(): bias_grad = lax.psum(jnp.sum(resid_full, axis=0), 'tok')  15.8 us
    dot_general x4, matrix products, block_compute(): lax.dot_general(chosen_acts, residual, contract_rows, preferred_element_t...  15.2 us
    dynamic_update_slice x4, local copies, waits for them, and re-layouts, on_device(): decoder_grad = lax.map(block_grad, jnp.arange(layers, dtype=jnp.int32))  12.6 us
  transfers between devices with their start and end apart: 5, of which 4 were waited for; matrix products, arithmetic and copies ran while one was open for 15% of the time, Pallas kernels for 0%

commit v1 on v0

v1 whole, which is shorter than its diff:
```python
import functools
import math

import jax
import jax.numpy as jnp
from jax import lax
from jax.experimental import pallas as pl
from jax.experimental.pallas import tpu as pltpu
from jax.sharding import PartitionSpec as P

BF16 = jnp.bfloat16
F32 = jnp.float32
VMEM_LIMIT = 48 * 1024 * 1024


def whole(count):
    return [pl.BlockSpec(memory_space=pltpu.VMEM)] * count


def call(kernel, out_shape, in_specs, out_specs, scratch, flops, moved):
    return pl.pallas_call(
        kernel,
        out_shape=out_shape,
        in_specs=in_specs,
        out_specs=out_specs,
        scratch_shapes=scratch,
        compiler_params=pltpu.CompilerParams(vmem_limit_bytes=VMEM_LIMIT),
        cost_estimate=pl.CostEstimate(flops=flops, bytes_accessed=moved, transcendentals=0),
    )


def encode_kernel(count, *refs):
    pieces, (weight, bias, out, rows) = refs[:count], refs[count:]
    height = pieces[0].shape[0]
    for index, piece in enumerate(pieces):
        rows[pl.ds(index * height, height), :] = piece[...]
    value = jnp.dot(rows[...], weight[...], preferred_element_type=F32) + bias[...]
    out[...] = jnp.maximum(value, 0.0).astype(BF16)


def decode_kernel(layers, pieces, columns, target_ref, order_ref, *refs):
    acts = refs[: 2 * layers]
    weights, order_out, keep, send, buffer, sems = refs[2 * layers :]
    target = target_ref[0]
    features = acts[0].shape[1]
    half = acts[0].shape[0]
    width = weights.shape[2]
    copies = []
    for part in range(width // columns):
        copy = pltpu.make_async_copy(
            weights.at[:, :, pl.ds(part * columns, columns)],
            buffer.at[:, :, pl.ds(part * columns, columns)],
            sems.at[part],
        )
        copy.start()
        copies.append(copy)
    order = order_ref[...]
    for offset in range(layers):
        source = target ^ offset
        place = pl.ds(pl.multiple_of(source * features, features), features)
        low = jnp.dot(order[:, :half], acts[2 * offset][...], preferred_element_type=F32)
        high = jnp.dot(order[:, half:], acts[2 * offset + 1][...], preferred_element_type=F32)
        used = jnp.where(source <= target, 1.0, 0.0)
        order_out[:, place] = ((low + high) * used).astype(BF16)
    quarter = half // 2
    for part, copy in enumerate(copies):
        copy.wait()
        lanes = pl.ds(part * columns, columns)
        block = buffer[:, :, lanes].reshape(layers * features, columns)
        value = jnp.dot(order_out[...], block, preferred_element_type=F32).astype(BF16)
        keep[pl.ds(0, quarter), lanes] = value[:quarter]
        send[pl.ds(0, quarter), lanes] = value[quarter : 2 * quarter]
        keep[pl.ds(quarter, quarter), lanes] = value[2 * quarter : 3 * quarter]
        send[pl.ds(quarter, quarter), lanes] = value[3 * quarter :]


def grad_kernel(layers, count, target_ref, *refs):
    pieces = refs[:count]
    weights = refs[count]
    outs = refs[count + 1 : count + 1 + layers]
    rows, buffer, sems = refs[count + 1 + layers :]
    target = target_ref[0]
    sequence = list(range(1, layers)) + [0]
    copies = {}
    for offset in sequence:
        copy = pltpu.make_async_copy(
            weights.at[target ^ offset], buffer.at[offset], sems.at[offset]
        )
        copy.start()
        copies[offset] = copy
    height = pieces[0].shape[0]
    for index, piece in enumerate(pieces):
        rows[pl.ds(index * height, height), :] = piece[...]
    for offset in sequence:
        copies[offset].wait()
        value = lax.dot_general(
            rows[...], buffer[offset], (((1,), (1,)), ((), ())), preferred_element_type=F32
        )
        used = (target ^ offset) <= target
        outs[offset][...] = jnp.where(used, value, 0.0).astype(outs[offset].dtype)


def decoder_grad_kernel(count, loss_scale, target_ref, acts, norms, *refs):
    pieces = refs[:count]
    weights, out, rows = refs[count:]
    source = pl.program_id(0)
    height = pieces[0].shape[0]

    @pl.when(jnp.logical_and(source == 0, pl.program_id(1) == 0))
    def _():
        for index, piece in enumerate(pieces):
            rows[pl.ds(index * height, height), :] = piece[...]

    @pl.when(source <= target_ref[0])
    def _():
        columns = out.shape[2]
        lanes = pl.ds(pl.multiple_of(pl.program_id(1) * columns, columns), columns)
        block = acts[...]
        product = lax.dot_general(
            block, rows[:, lanes], (((0,), (0,)), ((), ())), preferred_element_type=F32
        )
        ones = jnp.ones((block.shape[0], 128), BF16)
        sums = lax.dot_general(block, ones, (((0,), (0,)), ((), ())), preferred_element_type=F32)
        norm = jnp.broadcast_to(norms[0], (128, norms.shape[2])).T
        factor = sums * loss_scale / norm
        for part in range(columns // 128):
            cut = slice(part * 128, part * 128 + 128)
            out[0, :, cut] = (
                product[:, cut] + factor * weights[0, :, cut].astype(F32)
            ).astype(BF16)

    @pl.when(source > target_ref[0])
    def _():
        out[...] = jnp.zeros(out.shape, out.dtype)


def on_device(
    layer_inputs,
    layer_targets,
    row_order,
    encoder_weight,
    encoder_bias,
    decoder_weight,
    decoder_bias,
):
    layers = lax.axis_size("layer")
    ranks = lax.axis_size("tok")
    lines = ranks // 2
    row_total = row_order.shape[0]
    height = row_total // ranks
    loss_scale = 1.0 / math.sqrt(row_total)
    target = lax.axis_index("layer")
    rank = lax.axis_index("tok")
    target_id = target.astype(jnp.int32).reshape(1)
    weights = decoder_weight[0]
    features, width = weights.shape[1:]
    half = row_total // 2

    def swap_tok(value, step):
        return lax.ppermute(value, "tok", [(i, i ^ step) for i in range(ranks)])

    def swap_layer(value, step):
        return lax.ppermute(value, "layer", [(i, i ^ step) for i in range(layers)])

    def gather_lines(own):
        lane = {0: own}
        for line in sorted(range(1, lines), key=lambda j: (bin(j).count("1"), j)):
            low = line & -line
            lane[line] = swap_tok(lane[line ^ low], 2 * low)
        other = {line: swap_tok(lane[line], 1) for line in range(lines)}
        first, last = range(lines // 2), range(lines // 2, lines)
        return [
            [lane[j] for j in group] + [other[j] for j in group] for group in (first, last)
        ]

    relative = []
    for group in (range(lines // 2), range(lines // 2, lines)):
        for core in range(2):
            relative += [2 * j + core for j in group]
    ordered_ranks = row_order.reshape(ranks, height)
    wanted = jnp.concatenate(
        [lax.dynamic_index_in_dim(ordered_ranks, rank ^ j, 0, keepdims=False) for j in relative]
    )
    held = (
        (rank ^ jnp.array(relative, jnp.int32))[:, None] * height
        + jnp.arange(height, dtype=jnp.int32)[None, :]
    ).reshape(row_total)
    order = (wanted[:, None] == held[None, :]).astype(BF16)

    inputs = gather_lines(layer_inputs[0])
    acts = []
    for pieces in inputs:
        own = call(
            functools.partial(encode_kernel, len(pieces)),
            jax.ShapeDtypeStruct((half, features), BF16),
            whole(len(pieces) + 2),
            pl.BlockSpec(memory_space=pltpu.VMEM),
            [pltpu.VMEM((half, width), BF16)],
            2 * half * width * features,
            2 * width * features,
        )(*pieces, encoder_weight[0], encoder_bias)
        acts.append([own] + [swap_layer(own, step) for step in range(1, layers)])

    squares = jnp.sum(jnp.square(weights.astype(F32)), axis=2)
    active = (jnp.arange(layers) <= target)[:, None]
    squares = jnp.where(active, squares, 0.0)
    norm_sq = squares
    for step in range(1, layers):
        norm_sq = norm_sq + swap_layer(squares, step)
    norms = jnp.sqrt(norm_sq + 1e-06)

    columns = min(512, width)
    any_space = pl.BlockSpec(memory_space=pl.ANY)
    scalar = pl.BlockSpec(memory_space=pltpu.SMEM)
    flat_acts = [acts[part][step] for step in range(layers) for part in range(2)]
    acts_all, keep, send = call(
        functools.partial(decode_kernel, layers, lines, columns),
        (
            jax.ShapeDtypeStruct((row_total, layers * features), BF16),
            jax.ShapeDtypeStruct((half, width), BF16),
            jax.ShapeDtypeStruct((half, width), BF16),
        ),
        [scalar] + whole(1 + 2 * layers) + [any_space],
        tuple(whole(3)),
        [
            pltpu.VMEM((layers, features, width), BF16),
            pltpu.SemaphoreType.DMA((width // columns,)),
        ],
        2 * row_total * layers * features * width,
        2 * layers * features * width,
    )(target_id, order, *flat_acts, weights)

    received = swap_tok(send, 1).astype(F32).reshape(lines, height, width)
    kept = keep.astype(F32).reshape(lines, height, width)
    parts = {j: kept[j] + received[j] for j in range(lines)}
    after = None
    for line in reversed(range(1, lines)):
        low = line & -line
        block = parts[line].astype(BF16)
        if after is not None:
            block, after = lax.optimization_barrier((block, after))
        after = swap_tok(block, 2 * low)
        parts[line ^ low] = parts[line ^ low] + after.astype(F32)
    resid_full = (
        parts[0] + decoder_bias[0] - layer_targets[0].astype(F32)
    ) * loss_scale
    resid = gather_lines(resid_full.astype(BF16))

    own_acts = [acts_all_part for acts_all_part in (acts_all[:half], acts_all[half:])]
    grads = []
    for pieces in resid:
        outs = call(
            functools.partial(grad_kernel, layers, len(pieces)),
            tuple(
                jax.ShapeDtypeStruct((half, features), BF16 if step else F32)
                for step in range(layers)
            ),
            [scalar] + whole(len(pieces)) + [any_space],
            tuple(whole(layers)),
            [
                pltpu.VMEM((half, width), BF16),
                pltpu.VMEM((layers, features, width), BF16),
                pltpu.SemaphoreType.DMA((layers,)),
            ],
            2 * half * layers * features * width,
            2 * layers * features * width,
        )(target_id, *pieces, weights)
        total = outs[0]
        for step in range(1, layers):
            total = total + swap_layer(outs[step], step).astype(F32)
        grads.append(total)

    all_pieces = resid[0] + resid[1]
    cut = min(1024, width)
    decoder_grad = pl.pallas_call(
        functools.partial(decoder_grad_kernel, len(all_pieces), loss_scale),
        out_shape=jax.ShapeDtypeStruct((layers, features, width), BF16),
        grid=(layers, width // cut),
        in_specs=[
            scalar,
            pl.BlockSpec((row_total, features), lambda s, n: (0, s)),
            pl.BlockSpec((1, 1, features), lambda s, n: (s, 0, 0)),
            *[pl.BlockSpec((height, width), lambda s, n: (0, 0)) for _ in all_pieces],
            pl.BlockSpec((1, features, cut), lambda s, n: (s, 0, n)),
        ],
        out_specs=pl.BlockSpec((1, features, cut), lambda s, n: (s, 0, n)),
        scratch_shapes=[pltpu.VMEM((row_total, width), BF16)],
        compiler_params=pltpu.CompilerParams(
            vmem_limit_bytes=VMEM_LIMIT, dimension_semantics=("arbitrary", "arbitrary")
        ),
        cost_estimate=pl.CostEstimate(
            flops=2 * row_total * layers * features * width,
            bytes_accessed=4 * layers * features * width,
            transcendentals=0,
        ),
    )(target_id, acts_all, norms[:, None, :], *all_pieces, weights)
    bias_grad = sum(jnp.sum(piece.astype(F32), axis=0) for piece in all_pieces)

    own_norm = lax.dynamic_index_in_dim(norms, target, 0, keepdims=False)
    ordered = lax.dot_general(
        jnp.concatenate(inputs[0] + inputs[1]),
        order,
        (((0,), (1,)), ((), ())),
        preferred_element_type=F32,
    ).astype(BF16)
    own_all = lax.dynamic_slice_in_dim(acts_all, target * features, features, axis=1)
    grad_pre = jnp.where(
        own_all > 0, jnp.concatenate(grads) + own_norm * loss_scale, 0.0
    )
    encoder_grad = jnp.dot(
        ordered, grad_pre.astype(BF16), preferred_element_type=F32
    ).astype(BF16)
    feature_grad = jnp.sum(grad_pre, axis=0)
    return (encoder_grad[None], feature_grad[None], decoder_grad[None], bias_grad[None])


def solution(mesh):
    placed = (
        P("layer", "tok", None),
        P("layer", "tok", None),
        P(),
        P("layer", None, "tok"),
        P("layer", "tok"),
        P("layer", None, "tok", None),
        P("layer", None),
    )
    return jax.shard_map(
        on_device,
        mesh=mesh,
        in_specs=placed,
        out_specs=(
            P("layer", None, "tok"),
            P("layer", "tok"),
            P("layer", None, "tok", None),
            P("layer", None),
        ),
        check_vma=False,
    )
```

time: 250 us -> 110 us (0.44)
  the two profiles are of different devices: /device:TPU:7 before, /device:TPU:0 now
where the time goes in v1:
time: 110 us
  waiting for transfers between devices  41.7 us (38%)
  starting transfers between devices  30.3 us (28%)
  Pallas kernels  25.1 us (23%)
  other arithmetic  7.77 us (7%)
  matrix products  2.79 us (3%)
    ppermute x18, waiting for transfers between devices, swap_tok(): return lax.ppermute(value, 'tok', [(i, i ^ step) for i in range(ranks)])  35.3 us
    ppermute x15, starting transfers between devices, swap_layer(): return lax.ppermute(value, 'layer', [(i, i ^ step) for i in range(layers)])  19.6 us
    ppermute x18, starting transfers between devices, swap_tok(): return lax.ppermute(value, 'tok', [(i, i ^ step) for i in range(ranks)])  10.7 us
    pallas_call x2, Pallas kernels, on_device(): call(functools.partial(grad_kernel, layers, len(pieces)), tuple((jax.Shap...  9.83 us
    pallas_call x1, Pallas kernels, on_device(): pl.pallas_call(functools.partial(decoder_grad_kernel, len(all_pieces), lo...  9.28 us
    ppermute x15, waiting for transfers between devices, swap_layer(): return lax.ppermute(value, 'layer', [(i, i ^ step) for i in range(layers)])  6.41 us
    reduce_sum x1, other arithmetic, on_device(): squares = jnp.sum(jnp.square(weights.astype(F32)), axis=2)  5.31 us
    pallas_call x1, Pallas kernels, on_device(): call(functools.partial(decode_kernel, layers, lines, columns), (jax.Shape...  5.04 us
  transfers between devices with their start and end apart: 33, of which 15 were waited for; matrix products, arithmetic and copies ran while one was open for 2% of the time, Pallas kernels for 18%

profile of v1, /device:TPU:0, one launch (start us, length us, event | category | flops | bytes accessed | tf_op | source)
XLA Modules:
  0.0 109.7 jit_solution(17327147856595244647)
XLA Ops:
  0.7 5.3 %multiply_reduce_fusion = f32[4,512]{1,0:T(4,128)S(1)} fusion(bf16[1,4,512,2048]{3,2,1,0:T(8,128)(2,1)} %param.13), kind=kLoop, calls=%fused_computation | loop fusion | flops 12580864 | bytes 8396800 | tf_op jit(solution)/shard_map/reduce_sum | solution.py:204
  6.0 0.1 broadcast_select_fusion
  6.1 3.0 %collective-permute-start.31 = (f32[4,512]{1,0:T(4,128)S(1)}, f32[4,512]{1,0:T(4,128)S(1)}, u32[]{:S(2)}, u32[]{:S(2)}) collective-permute-start(f32[4,512]{1,0:T(4,128)S(1)} %broadcast_select_fusion), channel_id=1, source_target_pairs={{0,16},{8,24},{16,0},{24,8},{1,17},{9,25},{17,1},{25,9},{2,18},{10... | collective-permute-start | bytes 24584 | tf_op jit(solution)/shard_map/ppermute | solution.py:163
  9.1 1.4 %collective-permute-start.32 = (f32[4,512]{1,0:T(4,128)S(1)}, f32[4,512]{1,0:T(4,128)S(1)}, u32[]{:S(2)}, u32[]{:S(2)}) collective-permute-start(f32[4,512]{1,0:T(4,128)S(1)} %broadcast_select_fusion), channel_id=1, source_target_pairs={{0,24},{8,16},{16,8},{24,0},{1,25},{9,17},{17,9},{25,1},{2,26},{10... | collective-permute-start | bytes 24584 | tf_op jit(solution)/shard_map/ppermute | solution.py:163
  10.5 2.6 %collective-permute-start.3 = (bf16[32,2048]{1,0:T(8,128)(2,1)S(1)}, bf16[32,2048]{1,0:T(8,128)(2,1)S(1)}, u32[]{:S(2)}, u32[]{:S(2)}) collective-permute-start(bf16[32,2048]{1,0:T(8,128)(2,1)S(1)} %bitcast.36), channel_id=1, source_target_pairs={{0,4},{1,5},{2,6},{3,7},{4,0},{5,1},{6,2},{7,3},{8,12},{9,13},{10,... | collective-permute-start | bytes 393224 | tf_op jit(solution)/shard_map/ppermute | solution.py:160
  13.1 1.6 %collective-permute-start = (bf16[32,2048]{1,0:T(8,128)(2,1)S(1)}, bf16[32,2048]{1,0:T(8,128)(2,1)S(1)}, u32[]{:S(2)}, u32[]{:S(2)}) collective-permute-start(bf16[32,2048]{1,0:T(8,128)(2,1)S(1)} %bitcast.38), channel_id=1, source_target_pairs={{0,2},{1,3},{2,0},{3,1},{4,6},{5,7},{6,4},{7,5},{8,10},{9,11},{10,... | collective-permute-start | bytes 393224 | tf_op jit(solution)/shard_map/ppermute | solution.py:160
  14.7 0.7 constant_dynamic-update-slice_fusion.7
  15.3 5.1 %collective-permute-done.refs_1_ = bf16[32,2048]{1,0:T(8,128)(2,1)S(1)} collective-permute-done((bf16[32,2048]{1,0:T(8,128)(2,1)S(1)}, bf16[32,2048]{1,0:T(8,128)(2,1)S(1)}, u32[]{:S(2)}, u32[]{:S(2)}) %collective-permute-start) | collective-permute-done | bytes 131104 | tf_op jit(solution)/shard_map/ppermute | solution.py:160
  20.5 0.1 add.213
  20.6 0.1 reshape.112
  20.6 0.5 collective-permute-start.4
  21.2 0.1 concatenate.10
  21.2 0.3 collective-permute-start.5
  21.5 0.2 collective-permute-done.2.refs_3_
  21.7 0.5 shard_map.111.refs_0_
  22.2 1.6 %collective-permute-start.11 = (bf16[128,512]{1,0:T(8,128)(2,1)S(1)}, bf16[128,512]{1,0:T(8,128)(2,1)S(1)}, u32[]{:S(2)}, u32[]{:S(2)}) collective-permute-start(bf16[128,512]{1,0:T(8,128)(2,1)S(1)} %shard_map.111.refs_0_), channel_id=1, source_target_pairs={{0,24},{8,16},{16,8},{24,0},{1,25},{9,17},{17,9},{25,1},{2,26},{10... | collective-permute-start | bytes 393224 | tf_op jit(solution)/shard_map/ppermute | solution.py:163
  23.8 2.8 %collective-permute-done.4.refs_1_ = bf16[32,2048]{1,0:T(8,128)(2,1)S(1)} collective-permute-done((bf16[32,2048]{1,0:T(8,128)(2,1)S(1)}, bf16[32,2048]{1,0:T(8,128)(2,1)S(1)}, u32[]{:S(2)}, u32[]{:S(2)}) %collective-permute-start.4) | collective-permute-done | bytes 131104 | tf_op jit(solution)/shard_map/ppermute | solution.py:160
  26.6 0.1 compare_convert_fusion.order_ref
  26.7 0.5 collective-permute-start.30
  27.3 0.7 collective-permute-done.6.refs_3_
  27.9 1.5 %collective-permute-start.9 = (bf16[128,512]{1,0:T(8,128)(2,1)S(1)}, bf16[128,512]{1,0:T(8,128)(2,1)S(1)}, u32[]{:S(2)}, u32[]{:S(2)}) collective-permute-start(bf16[128,512]{1,0:T(8,128)(2,1)S(1)} %shard_map.111.refs_0_), channel_id=1, source_target_pairs={{0,16},{8,24},{16,0},{24,8},{1,17},{9,25},{17,1},{25,9},{2,18},{10... | collective-permute-start | bytes 393224 | tf_op jit(solution)/shard_map/ppermute | solution.py:163
  29.5 0.5 shard_map.112.refs_1_
  30.0 0.9 collective-permute-start.7
  30.9 1.1 collective-permute-start.12
  32.0 1.5 %collective-permute-start.10 = (bf16[128,512]{1,0:T(8,128)(2,1)S(1)}, bf16[128,512]{1,0:T(8,128)(2,1)S(1)}, u32[]{:S(2)}, u32[]{:S(2)}) collective-permute-start(bf16[128,512]{1,0:T(8,128)(2,1)S(1)} %shard_map.112.refs_1_), channel_id=1, source_target_pairs={{0,16},{8,24},{16,0},{24,8},{1,17},{9,25},{17,1},{25,9},{2,18},{10... | collective-permute-start | bytes 393224 | tf_op jit(solution)/shard_map/ppermute | solution.py:163
  33.5 0.9 collective-permute-start.8
  34.4 0.1 add_sqrt_fusion
  34.5 1.9 %collective-permute-done.7.refs_2_ = bf16[128,512]{1,0:T(8,128)(2,1)S(1)} collective-permute-done((bf16[128,512]{1,0:T(8,128)(2,1)S(1)}, bf16[128,512]{1,0:T(8,128)(2,1)S(1)}, u32[]{:S(2)}, u32[]{:S(2)}) %collective-permute-start.7) | collective-permute-done | bytes 131104 | tf_op jit(solution)/shard_map/ppermute | solution.py:163
  36.4 2.8 %collective-permute-done.12.refs_7_ = bf16[128,512]{1,0:T(8,128)(2,1)S(1)} collective-permute-done((bf16[128,512]{1,0:T(8,128)(2,1)S(1)}, bf16[128,512]{1,0:T(8,128)(2,1)S(1)}, u32[]{:S(2)}, u32[]{:S(2)}) %collective-permute-start.12) | collective-permute-done | bytes 131104 | tf_op jit(solution)/shard_map/ppermute | solution.py:163
  39.2 0.4 collective-permute-done.10.refs_5_
  39.5 1.4 %collective-permute-done.8.refs_3_ = bf16[128,512]{1,0:T(8,128)(2,1)S(1)} collective-permute-done((bf16[128,512]{1,0:T(8,128)(2,1)S(1)}, bf16[128,512]{1,0:T(8,128)(2,1)S(1)}, u32[]{:S(2)}, u32[]{:S(2)}) %collective-permute-start.8) | collective-permute-done | bytes 131104 | tf_op jit(solution)/shard_map/ppermute | solution.py:163
  40.9 5.0 %shard_map.113 = (bf16[256,2048]{1,0:T(8,128)(2,1)S(1)}, bf16[128,2048]{1,0:T(8,128)(2,1)S(1)}, bf16[128,2048]{1,0:T(8,128)(2,1)S(1)}) custom-call(s32[1]{0:T(128)} %bitcast.9.target_ref, bf16[256,256]{1,0:T(8,128)(2,1)S(1)} %compare_convert_fusion.order_ref, bf16[128,512]{1,0:T(8,128)(2,1)S(1)} %shard_map.111.refs_0_, ...), custom_call_target="tpu_custom_call" | custom-call | flops 2147483648 | bytes 8388608 | tf_op jit(solution)/shard_map/pallas_call | solution.py:216
  46.0 0.1 collective-permute-start.13
  46.1 0.1 convert_element_type.92
  46.2 1.7 %collective-permute-done.13 = bf16[128,2048]{1,0:T(8,128)(2,1)S(1)} collective-permute-done((bf16[128,2048]{1,0:T(8,128)(2,1)S(1)}, bf16[128,2048]{1,0:T(8,128)(2,1)S(1)}, u32[]{:S(2)}, u32[]{:S(2)}) %collective-permute-start.13) | collective-permute-done | bytes 524320 | tf_op jit(solution)/shard_map/ppermute | solution.py:160
  47.9 0.1 convert_element_type.93
  48.1 0.5 collective-permute-start.14
  48.6 5.1 %collective-permute-done.14 = bf16[32,2048]{1,0:T(8,128)(2,1)S(1)} collective-permute-done((bf16[32,2048]{1,0:T(8,128)(2,1)S(1)}, bf16[32,2048]{1,0:T(8,128)(2,1)S(1)}, u32[]{:S(2)}, u32[]{:S(2)}) %collective-permute-start.14) | collective-permute-done | bytes 131104 | tf_op jit(solution)/shard_map/ppermute | solution.py:160
  53.7 0.1 fusion.7
  53.8 1.6 %collective-permute-start.15 = (bf16[32,2048]{1,0:T(8,128)(2,1)S(1)}, bf16[32,2048]{1,0:T(8,128)(2,1)S(1)}, u32[]{:S(2)}, u32[]{:S(2)}) collective-permute-start(bf16[32,2048]{1,0:T(8,128)(2,1)S(1)} %get-tuple-element.20), channel_id=1, source_target_pairs={{0,4},{1,5},{2,6},{3,7},{4,0},{5,1},{6,2},{7,3},{8,12},{9,13},{10,... | collective-permute-start | bytes 393224 | tf_op jit(solution)/shard_map/ppermute | solution.py:160
  55.3 6.9 %collective-permute-done.15 = bf16[32,2048]{1,0:T(8,128)(2,1)S(1)} collective-permute-done((bf16[32,2048]{1,0:T(8,128)(2,1)S(1)}, bf16[32,2048]{1,0:T(8,128)(2,1)S(1)}, u32[]{:S(2)}, u32[]{:S(2)}) %collective-permute-start.15) | collective-permute-done | bytes 131104 | tf_op jit(solution)/shard_map/ppermute | solution.py:160
  62.3 5.3 %collective-permute-done.16 = bf16[32,2048]{1,0:T(8,128)(2,1)S(1)} collective-permute-done((bf16[32,2048]{1,0:T(8,128)(2,1)S(1)}, bf16[32,2048]{1,0:T(8,128)(2,1)S(1)}, u32[]{:S(2)}, u32[]{:S(2)}) %collective-permute-start.16) | collective-permute-done | bytes 131104 | tf_op jit(solution)/shard_map/ppermute | solution.py:160
  67.6 0.1 convert_reduce_fusion.7
  67.7 1.2 %collective-permute-start.23 = (bf16[32,2048]{1,0:T(8,128)(2,1)S(1)}, bf16[32,2048]{1,0:T(8,128)(2,1)S(1)}, u32[]{:S(2)}, u32[]{:S(2)}) collective-permute-start(bf16[32,2048]{1,0:T(8,128)(2,1)S(1)} %get-tuple-element.31.refs_0_), channel_id=1, source_target_pairs={{0,4},{1,5},{2,6},{3,7},{4,0},{5,1},{6,2},{7,3},{8,12},{9,13},{10,... | collective-permute-start | bytes 393224 | tf_op jit(solution)/shard_map/ppermute | solution.py:160
  68.9 1.7 %collective-permute-start.17 = (bf16[32,2048]{1,0:T(8,128)(2,1)S(1)}, bf16[32,2048]{1,0:T(8,128)(2,1)S(1)}, u32[]{:S(2)}, u32[]{:S(2)}) collective-permute-start(bf16[32,2048]{1,0:T(8,128)(2,1)S(1)} %get-tuple-element.31.refs_0_), channel_id=1, source_target_pairs={{0,2},{1,3},{2,0},{3,1},{4,6},{5,7},{6,4},{7,5},{8,10},{9,11},{10,... | collective-permute-start | bytes 393224 | tf_op jit(solution)/shard_map/ppermute | solution.py:160
  70.7 0.1 collective-permute-start.18
  70.8 5.3 %collective-permute-done.23.refs_0_.refs_4_ = bf16[32,2048]{1,0:T(8,128)(2,1)S(1)} collective-permute-done((bf16[32,2048]{1,0:T(8,128)(2,1)S(1)}, bf16[32,2048]{1,0:T(8,128)(2,1)S(1)}, u32[]{:S(2)}, u32[]{:S(2)}) %collective-permute-start.23) | collective-permute-done | bytes 131104 | tf_op jit(solution)/shard_map/ppermute | solution.py:160
  76.2 0.1 collective-permute-start.24
  76.3 0.4 collective-permute-start.19
  76.8 0.9 collective-permute-done.19.refs_3_
  77.7 4.9 %shard_map.114 = (f32[128,512]{1,0:T(8,128)S(1)}, bf16[128,512]{1,0:T(8,128)(2,1)S(1)}, bf16[128,512]{1,0:T(8,128)(2,1)S(1)}, bf16[128,512]{1,0:T(8,128)(2,1)S(1)}) custom-call(s32[1]{0:T(128)} %bitcast.9.target_ref, bf16[32,2048]{1,0:T(8,128)(2,1)S(1)} %get-tuple-element.31.refs_0_, bf16[32,2048]{1,0:T(8,128)(2,1)S(1)} %collective-permute-done.17.refs_1_, ...), custom_call_target="tpu_custom_call" | custom-call | flops 1073741824 | bytes 8388608 | tf_op jit(solution)/shard_map/pallas_call | solution.py:252
  82.6 1.0 collective-permute-start.20
  83.6 0.5 collective-permute-start.21
  84.1 2.1 %collective-permute-start.22 = (bf16[128,512]{1,0:T(8,128)(2,1)S(1)}, bf16[128,512]{1,0:T(8,128)(2,1)S(1)}, u32[]{:S(2)}, u32[]{:S(2)}) collective-permute-start(bf16[128,512]{1,0:T(8,128)(2,1)S(1)} %get-tuple-element.25), channel_id=1, source_target_pairs={{0,24},{8,16},{16,8},{24,0},{1,25},{9,17},{17,9},{25,1},{2,26},{10... | collective-permute-start | bytes 393224 | tf_op jit(solution)/shard_map/ppermute | solution.py:163
  86.2 0.1 collective-permute-start.26
  86.4 1.2 %collective-permute-done.26.refs_3_.refs_7_ = bf16[32,2048]{1,0:T(8,128)(2,1)S(1)} collective-permute-done((bf16[32,2048]{1,0:T(8,128)(2,1)S(1)}, bf16[32,2048]{1,0:T(8,128)(2,1)S(1)}, u32[]{:S(2)}, u32[]{:S(2)}) %collective-permute-start.26) | collective-permute-done | bytes 131104 | tf_op jit(solution)/shard_map/ppermute | solution.py:160
  87.6 4.9 %shard_map.115 = (f32[128,512]{1,0:T(8,128)S(1)}, bf16[128,512]{1,0:T(8,128)(2,1)S(1)}, bf16[128,512]{1,0:T(8,128)(2,1)S(1)}, bf16[128,512]{1,0:T(8,128)(2,1)S(1)}) custom-call(s32[1]{0:T(128)} %bitcast.9.target_ref, bf16[32,2048]{1,0:T(8,128)(2,1)S(1)} %collective-permute-done.23.refs_0_.refs_4_, ...), custom_call_target="tpu_custom_call" | custom-call | flops 1073741824 | bytes 8388608 | tf_op jit(solution)/shard_map/pallas_call | solution.py:252
  92.6 1.0 collective-permute-start.27
  93.5 0.5 collective-permute-start.28
  94.1 0.6 add_add_fusion
  94.7 2.1 %collective-permute-start.29 = (bf16[128,512]{1,0:T(8,128)(2,1)S(1)}, bf16[128,512]{1,0:T(8,128)(2,1)S(1)}, u32[]{:S(2)}, u32[]{:S(2)}) collective-permute-start(bf16[128,512]{1,0:T(8,128)(2,1)S(1)} %get-tuple-element.29), channel_id=1, source_target_pairs={{0,24},{8,16},{16,8},{24,0},{1,25},{9,17},{17,9},{25,1},{2,26},{10... | collective-permute-start | bytes 393224 | tf_op jit(solution)/shard_map/ppermute | solution.py:163
  96.9 9.3 %shard_map.116 = bf16[4,512,2048]{2,1,0:T(8,128)(2,1)} custom-call(s32[1]{0:T(128)} %bitcast.9.target_ref, bf16[256,2048]{1,0:T(8,128)(2,1)S(1)} %get-tuple-element.17.acts, f32[4,1,512]{2,1,0:T(1,128)S(1)} %broadcast_in_dim.39.norms, bf16[32,2048]{1,0:T(8,128)(2,1)S(1)} %get-tuple-element.31.refs_0_, bf16[32,2048]{1,0:T(8,128)(2,1)S(1)} %collective-permute-done.17.refs_1_, ...), custom_call_target="tpu_custom_call" | custom-call | flops 2147483648 | bytes 16777216 | tf_op jit(solution)/shard_map/pallas_call | solution.py:275
  106.2 0.7 fusion.15
  106.9 2.8 %fusion = bf16[1,2048,512]{2,1,0:T(8,128)(2,1)} fusion(bf16[256,2048]{1,0:T(8,128)(2,1)S(1)} %copy-done.5, f32[128,512]{1,0:T(8,128)S(1)} %convert_add_fusion, f32[128,512]{1,0:T(8,128)S(1)} %convert_add_fusion.1, f32[512]{0:T(512)S(1)} %bitcast.46, bf16[256,2048]{1,0:T(8,128)(2,1)S(1)} %get-tuple-element.17.acts, s32[]{:T(128)S(6)} %select_n.48, ...), kind=kOutput, calls=%fused_computation.2 | convolution fusion | flops 807862272 | bytes 3936260 | tf_op jit(solution)/shard_map/dot_general | solution.py:310
  (66 shorter events, 0.8 us)
Async XLA Ops:
  0.6 14.7 %copy-start.9 = (s32[8]{0:T(128)S(1)}, s32[8]{0:T(128)}, u32[]{:S(2)}) copy-start(s32[8]{0:T(128)} %constant.64.clone) | copy-start | bytes 100
  0.6 9.8 %copy-start.1 = (bf16[1,32,2048]{2,1,0:T(8,128)(2,1)S(1)}, bf16[1,32,2048]{2,1,0:T(8,128)(2,1)}, u32[]{:S(2)}) copy-start(bf16[1,32,2048]{2,1,0:T(8,128)(2,1)} %param.8) | copy-start | bytes 393220
  0.7 19.9 %copy-start.8 = (s32[256]{0:T(256)S(1)}, s32[256]{0:T(256)}, u32[]{:S(2)}) copy-start(s32[256]{0:T(256)} %param.10) | copy-start | bytes 3076
  0.7 21.1 %copy-start.2 = (f32[1,512]{1,0:T(1,128)S(1)}, f32[1,512]{1,0:T(1,128)}, u32[]{:S(2)}) copy-start(f32[1,512]{1,0:T(1,128)} %refs_5_.3) | copy-start | bytes 6148
  0.7 21.1 %copy-start = (bf16[1,2048,512]{2,1,0:T(8,128)(2,1)S(1)}, bf16[1,2048,512]{2,1,0:T(8,128)(2,1)}, u32[]{:S(2)}) copy-start(bf16[1,2048,512]{2,1,0:T(8,128)(2,1)} %param.11) | copy-start | bytes 6291460
  6.1 23.9 %collective-permute-start.31 = (f32[4,512]{1,0:T(4,128)S(1)}, f32[4,512]{1,0:T(4,128)S(1)}, u32[]{:S(2)}, u32[]{:S(2)}) collective-permute-start(f32[4,512]{1,0:T(4,128)S(1)} %broadcast_select_fusion), channel_id=1, source_target_pairs={{0,16},{8,24},{16,0},{24,8},{1,17},{9,25},{17,1},{25,9},{2,18},{10... | collective-permute-start | bytes 24584 | tf_op jit(solution)/shard_map/ppermute | solution.py:163
  9.1 21.8 %collective-permute-start.32 = (f32[4,512]{1,0:T(4,128)S(1)}, f32[4,512]{1,0:T(4,128)S(1)}, u32[]{:S(2)}, u32[]{:S(2)}) collective-permute-start(f32[4,512]{1,0:T(4,128)S(1)} %broadcast_select_fusion), channel_id=1, source_target_pairs={{0,24},{8,16},{16,8},{24,0},{1,25},{9,17},{17,9},{25,1},{2,26},{10... | collective-permute-start | bytes 24584 | tf_op jit(solution)/shard_map/ppermute | solution.py:163
  10.5 10.1 %collective-permute-start.3 = (bf16[32,2048]{1,0:T(8,128)(2,1)S(1)}, bf16[32,2048]{1,0:T(8,128)(2,1)S(1)}, u32[]{:S(2)}, u32[]{:S(2)}) collective-permute-start(bf16[32,2048]{1,0:T(8,128)(2,1)S(1)} %bitcast.36), channel_id=1, source_target_pairs={{0,4},{1,5},{2,6},{3,7},{4,0},{5,1},{6,2},{7,3},{8,12},{9,13},{10,... | collective-permute-start | bytes 393224 | tf_op jit(solution)/shard_map/ppermute | solution.py:160
  13.1 8.2 %collective-permute-start.1 = (bf16[32,2048]{1,0:T(8,128)(2,1)S(1)}, bf16[32,2048]{1,0:T(8,128)(2,1)S(1)}, u32[]{:S(2)}, u32[]{:S(2)}) collective-permute-start(bf16[32,2048]{1,0:T(8,128)(2,1)S(1)} %bitcast.37), channel_id=1, source_target_pairs={{0,1},{1,0},{2,3},{3,2},{4,5},{5,4},{6,7},{7,6},{8,9},{9,8},{10,11... | collective-permute-start | bytes 393224 | tf_op jit(solution)/shard_map/ppermute | solution.py:160
  13.1 7.3 %collective-permute-start = (bf16[32,2048]{1,0:T(8,128)(2,1)S(1)}, bf16[32,2048]{1,0:T(8,128)(2,1)S(1)}, u32[]{:S(2)}, u32[]{:S(2)}) collective-permute-start(bf16[32,2048]{1,0:T(8,128)(2,1)S(1)} %bitcast.38), channel_id=1, source_target_pairs={{0,2},{1,3},{2,0},{3,1},{4,6},{5,7},{6,4},{7,5},{8,10},{9,11},{10,... | collective-permute-start | bytes 393224 | tf_op jit(solution)/shard_map/ppermute | solution.py:160
  20.4 1.3 %collective-permute-start.2 = (bf16[32,2048]{1,0:T(8,128)(2,1)S(1)}, bf16[32,2048]{1,0:T(8,128)(2,1)S(1)}, u32[]{:S(2)}, u32[]{:S(2)}) collective-permute-start(bf16[32,2048]{1,0:T(8,128)(2,1)S(1)} %collective-permute-done.refs_1_), channel_id=1, source_target_pairs={{0,1},{1,0},{2,3},{3,2},{4,5},{5,4},{6,7},{7,6},{8,9},{9,8},{10,11... | collective-permute-start | bytes 393224 | tf_op jit(solution)/shard_map/ppermute | solution.py:160
  20.6 6.0 %collective-permute-start.4 = (bf16[32,2048]{1,0:T(8,128)(2,1)S(1)}, bf16[32,2048]{1,0:T(8,128)(2,1)S(1)}, u32[]{:S(2)}, u32[]{:S(2)}) collective-permute-start(bf16[32,2048]{1,0:T(8,128)(2,1)S(1)} %collective-permute-done.3.refs_0_), channel_id=1, source_target_pairs={{0,2},{1,3},{2,0},{3,1},{4,6},{5,7},{6,4},{7,5},{8,10},{9,11},{10,... | collective-permute-start | bytes 393224 | tf_op jit(solution)/shard_map/ppermute | solution.py:160
  21.2 5.5 %collective-permute-start.5 = (bf16[32,2048]{1,0:T(8,128)(2,1)S(1)}, bf16[32,2048]{1,0:T(8,128)(2,1)S(1)}, u32[]{:S(2)}, u32[]{:S(2)}) collective-permute-start(bf16[32,2048]{1,0:T(8,128)(2,1)S(1)} %collective-permute-done.3.refs_0_), channel_id=1, source_target_pairs={{0,1},{1,0},{2,3},{3,2},{4,5},{5,4},{6,7},{7,6},{8,9},{9,8},{10,11... | collective-permute-start | bytes 393224 | tf_op jit(solution)/shard_map/ppermute | solution.py:160
  22.2 11.3 %collective-permute-start.11 = (bf16[128,512]{1,0:T(8,128)(2,1)S(1)}, bf16[128,512]{1,0:T(8,128)(2,1)S(1)}, u32[]{:S(2)}, u32[]{:S(2)}) collective-permute-start(bf16[128,512]{1,0:T(8,128)(2,1)S(1)} %shard_map.111.refs_0_), channel_id=1, source_target_pairs={{0,24},{8,16},{16,8},{24,0},{1,25},{9,17},{17,9},{25,1},{2,26},{10... | collective-permute-start | bytes 393224 | tf_op jit(solution)/shard_map/ppermute | solution.py:163
  26.6 1.3 %collective-permute-start.6 = (bf16[32,2048]{1,0:T(8,128)(2,1)S(1)}, bf16[32,2048]{1,0:T(8,128)(2,1)S(1)}, u32[]{:S(2)}, u32[]{:S(2)}) collective-permute-start(bf16[32,2048]{1,0:T(8,128)(2,1)S(1)} %collective-permute-done.4.refs_1_), channel_id=1, source_target_pairs={{0,1},{1,0},{2,3},{3,2},{4,5},{5,4},{6,7},{7,6},{8,9},{9,8},{10,11... | collective-permute-start | bytes 393224 | tf_op jit(solution)/shard_map/ppermute | solution.py:160
  26.7 19.3 %copy-start.3 = (bf16[256,2048]{1,0:T(8,128)(2,1)S(1)}, bf16[256,2048]{1,0:T(8,128)(2,1)}, u32[]{:S(2)}) copy-start(bf16[256,2048]{1,0:T(8,128)(2,1)} %constant_dynamic-update-slice_fusion.7) | copy-start | bytes 3145732
  26.7 5.3 %collective-permute-start.30 = (f32[4,512]{1,0:T(4,128)S(1)}, f32[4,512]{1,0:T(4,128)S(1)}, u32[]{:S(2)}, u32[]{:S(2)}) collective-permute-start(f32[4,512]{1,0:T(4,128)S(1)} %broadcast_select_fusion), channel_id=1, source_target_pairs={{0,8},{8,0},{16,24},{24,16},{1,9},{9,1},{17,25},{25,17},{2,10},{10... | collective-permute-start | bytes 24584 | tf_op jit(solution)/shard_map/ppermute | solution.py:163
  27.9 6.6 %collective-permute-start.9 = (bf16[128,512]{1,0:T(8,128)(2,1)S(1)}, bf16[128,512]{1,0:T(8,128)(2,1)S(1)}, u32[]{:S(2)}, u32[]{:S(2)}) collective-permute-start(bf16[128,512]{1,0:T(8,128)(2,1)S(1)} %shard_map.111.refs_0_), channel_id=1, source_target_pairs={{0,16},{8,24},{16,0},{24,8},{1,17},{9,25},{17,1},{25,9},{2,18},{10... | collective-permute-start | bytes 393224 | tf_op jit(solution)/shard_map/ppermute | solution.py:163
  29.9 37.7 %copy-start.6 = (bf16[1,32,2048]{2,1,0:T(8,128)(2,1)S(1)}, bf16[1,32,2048]{2,1,0:T(8,128)(2,1)}, u32[]{:S(2)}) copy-start(bf16[1,32,2048]{2,1,0:T(8,128)(2,1)} %param.9) | copy-start | bytes 393220
  29.9 37.7 %copy-start.7 = (f32[1,2048]{1,0:T(1,128)S(1)}, f32[1,2048]{1,0:T(1,128)}, u32[]{:S(2)}) copy-start(f32[1,2048]{1,0:T(1,128)} %param.14) | copy-start | bytes 24580
  30.0 6.4 %collective-permute-start.7 = (bf16[128,512]{1,0:T(8,128)(2,1)S(1)}, bf16[128,512]{1,0:T(8,128)(2,1)S(1)}, u32[]{:S(2)}, u32[]{:S(2)}) collective-permute-start(bf16[128,512]{1,0:T(8,128)(2,1)S(1)} %shard_map.111.refs_0_), channel_id=1, source_target_pairs={{0,8},{8,0},{16,24},{24,16},{1,9},{9,1},{17,25},{25,17},{2,10},{10... | collective-permute-start | bytes 393224 | tf_op jit(solution)/shard_map/ppermute | solution.py:163
  30.9 8.3 %collective-permute-start.12 = (bf16[128,512]{1,0:T(8,128)(2,1)S(1)}, bf16[128,512]{1,0:T(8,128)(2,1)S(1)}, u32[]{:S(2)}, u32[]{:S(2)}) collective-permute-start(bf16[128,512]{1,0:T(8,128)(2,1)S(1)} %shard_map.112.refs_1_), channel_id=1, source_target_pairs={{0,24},{8,16},{16,8},{24,0},{1,25},{9,17},{17,9},{25,1},{2,26},{10... | collective-permute-start | bytes 393224 | tf_op jit(solution)/shard_map/ppermute | solution.py:163
  32.0 7.5 %collective-permute-start.10 = (bf16[128,512]{1,0:T(8,128)(2,1)S(1)}, bf16[128,512]{1,0:T(8,128)(2,1)S(1)}, u32[]{:S(2)}, u32[]{:S(2)}) collective-permute-start(bf16[128,512]{1,0:T(8,128)(2,1)S(1)} %shard_map.112.refs_1_), channel_id=1, source_target_pairs={{0,16},{8,24},{16,0},{24,8},{1,17},{9,25},{17,1},{25,9},{2,18},{10... | collective-permute-start | bytes 393224 | tf_op jit(solution)/shard_map/ppermute | solution.py:163
  33.5 7.4 %collective-permute-start.8 = (bf16[128,512]{1,0:T(8,128)(2,1)S(1)}, bf16[128,512]{1,0:T(8,128)(2,1)S(1)}, u32[]{:S(2)}, u32[]{:S(2)}) collective-permute-start(bf16[128,512]{1,0:T(8,128)(2,1)S(1)} %shard_map.112.refs_1_), channel_id=1, source_target_pairs={{0,8},{8,0},{16,24},{24,16},{1,9},{9,1},{17,25},{25,17},{2,10},{10... | collective-permute-start | bytes 393224 | tf_op jit(solution)/shard_map/ppermute | solution.py:163
  46.0 2.0 %collective-permute-start.13 = (bf16[128,2048]{1,0:T(8,128)(2,1)S(1)}, bf16[128,2048]{1,0:T(8,128)(2,1)S(1)}, u32[]{:S(2)}, u32[]{:S(2)}) collective-permute-start(bf16[128,2048]{1,0:T(8,128)(2,1)S(1)} %get-tuple-element.19), channel_id=1, source_target_pairs={{0,1},{1,0},{2,3},{3,2},{4,5},{5,4},{6,7},{7,6},{8,9},{9,8},{10,11... | collective-permute-start | bytes 1572872 | tf_op jit(solution)/shard_map/ppermute | solution.py:160
  48.1 5.6 %collective-permute-start.14 = (bf16[32,2048]{1,0:T(8,128)(2,1)S(1)}, bf16[32,2048]{1,0:T(8,128)(2,1)S(1)}, u32[]{:S(2)}, u32[]{:S(2)}) collective-permute-start(bf16[32,2048]{1,0:T(8,128)(2,1)S(1)} %fusion.5), channel_id=1, source_target_pairs={{0,2},{1,3},{2,0},{3,1},{4,6},{5,7},{6,4},{7,5},{8,10},{9,11},{10,... | collective-permute-start | bytes 393224 | tf_op jit(solution)/shard_map/ppermute | solution.py:160
  53.8 8.5 %collective-permute-start.15 = (bf16[32,2048]{1,0:T(8,128)(2,1)S(1)}, bf16[32,2048]{1,0:T(8,128)(2,1)S(1)}, u32[]{:S(2)}, u32[]{:S(2)}) collective-permute-start(bf16[32,2048]{1,0:T(8,128)(2,1)S(1)} %get-tuple-element.20), channel_id=1, source_target_pairs={{0,4},{1,5},{2,6},{3,7},{4,0},{5,1},{6,2},{7,3},{8,12},{9,13},{10,... | collective-permute-start | bytes 393224 | tf_op jit(solution)/shard_map/ppermute | solution.py:160
  62.2 5.4 %collective-permute-start.16 = (bf16[32,2048]{1,0:T(8,128)(2,1)S(1)}, bf16[32,2048]{1,0:T(8,128)(2,1)S(1)}, u32[]{:S(2)}, u32[]{:S(2)}) collective-permute-start(bf16[32,2048]{1,0:T(8,128)(2,1)S(1)} %get-tuple-element.21), channel_id=1, source_target_pairs={{0,2},{1,3},{2,0},{3,1},{4,6},{5,7},{6,4},{7,5},{8,10},{9,11},{10,... | collective-permute-start | bytes 393224 | tf_op jit(solution)/shard_map/ppermute | solution.py:160
  67.7 8.3 %collective-permute-start.23 = (bf16[32,2048]{1,0:T(8,128)(2,1)S(1)}, bf16[32,2048]{1,0:T(8,128)(2,1)S(1)}, u32[]{:S(2)}, u32[]{:S(2)}) collective-permute-start(bf16[32,2048]{1,0:T(8,128)(2,1)S(1)} %get-tuple-element.31.refs_0_), channel_id=1, source_target_pairs={{0,4},{1,5},{2,6},{3,7},{4,0},{5,1},{6,2},{7,3},{8,12},{9,13},{10,... | collective-permute-start | bytes 393224 | tf_op jit(solution)/shard_map/ppermute | solution.py:160
  68.9 7.3 %collective-permute-start.17 = (bf16[32,2048]{1,0:T(8,128)(2,1)S(1)}, bf16[32,2048]{1,0:T(8,128)(2,1)S(1)}, u32[]{:S(2)}, u32[]{:S(2)}) collective-permute-start(bf16[32,2048]{1,0:T(8,128)(2,1)S(1)} %get-tuple-element.31.refs_0_), channel_id=1, source_target_pairs={{0,2},{1,3},{2,0},{3,1},{4,6},{5,7},{6,4},{7,5},{8,10},{9,11},{10,... | collective-permute-start | bytes 393224 | tf_op jit(solution)/shard_map/ppermute | solution.py:160
  70.7 15.7 %copy-start.4 = (bf16[256,2048]{1,0:T(8,128)(2,1)}, bf16[256,2048]{1,0:T(8,128)(2,1)S(1)}, u32[]{:S(2)}) copy-start(bf16[256,2048]{1,0:T(8,128)(2,1)S(1)} %constant_dynamic-update-slice_fusion) | copy-start | bytes 3145732
  70.7 6.0 %collective-permute-start.18 = (bf16[32,2048]{1,0:T(8,128)(2,1)S(1)}, bf16[32,2048]{1,0:T(8,128)(2,1)S(1)}, u32[]{:S(2)}, u32[]{:S(2)}) collective-permute-start(bf16[32,2048]{1,0:T(8,128)(2,1)S(1)} %get-tuple-element.31.refs_0_), channel_id=1, source_target_pairs={{0,1},{1,0},{2,3},{3,2},{4,5},{5,4},{6,7},{7,6},{8,9},{9,8},{10,11... | collective-permute-start | bytes 393224 | tf_op jit(solution)/shard_map/ppermute | solution.py:160
  76.1 10.2 %collective-permute-start.25 = (bf16[32,2048]{1,0:T(8,128)(2,1)S(1)}, bf16[32,2048]{1,0:T(8,128)(2,1)S(1)}, u32[]{:S(2)}, u32[]{:S(2)}) collective-permute-start(bf16[32,2048]{1,0:T(8,128)(2,1)S(1)} %collective-permute-done.23.refs_0_.refs_4_), channel_id=1, source_target_pairs={{0,1},{1,0},{2,3},{3,2},{4,5},{5,4},{6,7},{7,6},{8,9},{9,8},{10,11... | collective-permute-start | bytes 393224 | tf_op jit(solution)/shard_map/ppermute | solution.py:160
  76.2 10.0 %collective-permute-start.24 = (bf16[32,2048]{1,0:T(8,128)(2,1)S(1)}, bf16[32,2048]{1,0:T(8,128)(2,1)S(1)}, u32[]{:S(2)}, u32[]{:S(2)}) collective-permute-start(bf16[32,2048]{1,0:T(8,128)(2,1)S(1)} %collective-permute-done.23.refs_0_.refs_4_), channel_id=1, source_target_pairs={{0,2},{1,3},{2,0},{3,1},{4,6},{5,7},{6,4},{7,5},{8,10},{9,11},{10,... | collective-permute-start | bytes 393224 | tf_op jit(solution)/shard_map/ppermute | solution.py:160
  76.3 1.4 %collective-permute-start.19 = (bf16[32,2048]{1,0:T(8,128)(2,1)S(1)}, bf16[32,2048]{1,0:T(8,128)(2,1)S(1)}, u32[]{:S(2)}, u32[]{:S(2)}) collective-permute-start(bf16[32,2048]{1,0:T(8,128)(2,1)S(1)} %collective-permute-done.17.refs_1_), channel_id=1, source_target_pairs={{0,1},{1,0},{2,3},{3,2},{4,5},{5,4},{6,7},{7,6},{8,9},{9,8},{10,11... | collective-permute-start | bytes 393224 | tf_op jit(solution)/shard_map/ppermute | solution.py:160
  82.6 12.1 %collective-permute-start.20 = (bf16[128,512]{1,0:T(8,128)(2,1)S(1)}, bf16[128,512]{1,0:T(8,128)(2,1)S(1)}, u32[]{:S(2)}, u32[]{:S(2)}) collective-permute-start(bf16[128,512]{1,0:T(8,128)(2,1)S(1)} %get-tuple-element.23), channel_id=1, source_target_pairs={{0,8},{8,0},{16,24},{24,16},{1,9},{9,1},{17,25},{25,17},{2,10},{10... | collective-permute-start | bytes 393224 | tf_op jit(solution)/shard_map/ppermute | solution.py:163
  83.6 13.2 %collective-permute-start.21 = (bf16[128,512]{1,0:T(8,128)(2,1)S(1)}, bf16[128,512]{1,0:T(8,128)(2,1)S(1)}, u32[]{:S(2)}, u32[]{:S(2)}) collective-permute-start(bf16[128,512]{1,0:T(8,128)(2,1)S(1)} %get-tuple-element.24), channel_id=1, source_target_pairs={{0,16},{8,24},{16,0},{24,8},{1,17},{9,25},{17,1},{25,9},{2,18},{10... | collective-permute-start | bytes 393224 | tf_op jit(solution)/shard_map/ppermute | solution.py:163
  84.1 12.6 %collective-permute-start.22 = (bf16[128,512]{1,0:T(8,128)(2,1)S(1)}, bf16[128,512]{1,0:T(8,128)(2,1)S(1)}, u32[]{:S(2)}, u32[]{:S(2)}) collective-permute-start(bf16[128,512]{1,0:T(8,128)(2,1)S(1)} %get-tuple-element.25), channel_id=1, source_target_pairs={{0,24},{8,16},{16,8},{24,0},{1,25},{9,17},{17,9},{25,1},{2,26},{10... | collective-permute-start | bytes 393224 | tf_op jit(solution)/shard_map/ppermute | solution.py:163
  86.2 1.4 %collective-permute-start.26 = (bf16[32,2048]{1,0:T(8,128)(2,1)S(1)}, bf16[32,2048]{1,0:T(8,128)(2,1)S(1)}, u32[]{:S(2)}, u32[]{:S(2)}) collective-permute-start(bf16[32,2048]{1,0:T(8,128)(2,1)S(1)} %collective-permute-done.24.refs_1_.refs_5_), channel_id=1, source_target_pairs={{0,1},{1,0},{2,3},{3,2},{4,5},{5,4},{6,7},{7,6},{8,9},{9,8},{10,11... | collective-permute-start | bytes 393224 | tf_op jit(solution)/shard_map/ppermute | solution.py:160
  92.6 13.6 %collective-permute-start.27 = (bf16[128,512]{1,0:T(8,128)(2,1)S(1)}, bf16[128,512]{1,0:T(8,128)(2,1)S(1)}, u32[]{:S(2)}, u32[]{:S(2)}) collective-permute-start(bf16[128,512]{1,0:T(8,128)(2,1)S(1)} %get-tuple-element.27), channel_id=1, source_target_pairs={{0,8},{8,0},{16,24},{24,16},{1,9},{9,1},{17,25},{25,17},{2,10},{10... | collective-permute-start | bytes 393224 | tf_op jit(solution)/shard_map/ppermute | solution.py:163
  93.5 12.6 %collective-permute-start.28 = (bf16[128,512]{1,0:T(8,128)(2,1)S(1)}, bf16[128,512]{1,0:T(8,128)(2,1)S(1)}, u32[]{:S(2)}, u32[]{:S(2)}) collective-permute-start(bf16[128,512]{1,0:T(8,128)(2,1)S(1)} %get-tuple-element.28), channel_id=1, source_target_pairs={{0,16},{8,24},{16,0},{24,8},{1,17},{9,25},{17,1},{25,9},{2,18},{10... | collective-permute-start | bytes 393224 | tf_op jit(solution)/shard_map/ppermute | solution.py:163
  94.7 11.4 %collective-permute-start.29 = (bf16[128,512]{1,0:T(8,128)(2,1)S(1)}, bf16[128,512]{1,0:T(8,128)(2,1)S(1)}, u32[]{:S(2)}, u32[]{:S(2)}) collective-permute-start(bf16[128,512]{1,0:T(8,128)(2,1)S(1)} %get-tuple-element.29), channel_id=1, source_target_pairs={{0,24},{8,16},{16,8},{24,0},{1,25},{9,17},{17,9},{25,1},{2,26},{10... | collective-permute-start | bytes 393224 | tf_op jit(solution)/shard_map/ppermute | solution.py:163
  96.8 10.1 %copy-start.5 = (bf16[256,2048]{1,0:T(8,128)(2,1)S(1)}, bf16[256,2048]{1,0:T(8,128)(2,1)}, u32[]{:S(2)}) copy-start(bf16[256,2048]{1,0:T(8,128)(2,1)} %copy-done.4) | copy-start | bytes 3145732

commit v2 on v0

v2 whole, which is shorter than its diff:
```python
import functools
import math

import jax
import jax.numpy as jnp
from jax import lax
from jax.experimental import pallas as pl
from jax.experimental.pallas import tpu as pltpu
from jax.sharding import PartitionSpec as P

BF16 = jnp.bfloat16
F32 = jnp.float32
VMEM_LIMIT = 16 * 1024 * 1024
MICROSECOND = 1_150_000_000


def whole(count):
    return [pl.BlockSpec(memory_space=pltpu.VMEM)] * count


def call(kernel, out_shape, in_specs, out_specs, scratch, flops, moved, limit=VMEM_LIMIT):
    return pl.pallas_call(
        kernel,
        out_shape=out_shape,
        in_specs=in_specs,
        out_specs=out_specs,
        scratch_shapes=scratch,
        compiler_params=pltpu.CompilerParams(vmem_limit_bytes=limit),
        cost_estimate=pl.CostEstimate(flops=flops, bytes_accessed=moved, transcendentals=0),
    )


def table_kernel(relative, rows_ref, order, table):
    rank = lax.axis_index("tok")
    total_rows = table.shape[0]
    height = total_rows // len(relative)
    lane = lax.broadcasted_iota(jnp.int32, (1, total_rows), 1)
    held_rows = lane % height
    for index, offset in enumerate(relative):
        held_rows = held_rows + jnp.where(lane // height == index, (rank ^ offset) * height, 0)
    wanted = jnp.broadcast_to(rows_ref[...], (total_rows, total_rows)).T
    table[...] = jnp.where(wanted == held_rows, 1.0, 0.0)
    for index, offset in enumerate(relative):
        start = pl.multiple_of((rank ^ offset) * height, height)
        order[pl.ds(index * height, height), :] = table[pl.ds(start, height), :].astype(BF16)


def norm_kernel(weights, squares):
    layers, features, width = weights.shape
    target = lax.axis_index("layer")
    for source in range(layers):
        total = jnp.zeros((features, 128), F32)
        for part in range(width // 128):
            value = weights[source, :, pl.ds(part * 128, 128)].astype(F32)
            total = total + value * value
        column = jnp.sum(total, axis=1, keepdims=True)
        row = jnp.broadcast_to(column, (features, 128)).T[:1]
        squares[pl.ds(source, 1), :] = jnp.where(source <= target, row, 0.0)


def gather_rows(pieces, rows):
    height = pieces[0].shape[0]
    for index, piece in enumerate(pieces):
        rows[pl.ds(index * height, height), :] = piece[...]


def gather_parts(parts, rows):
    start = 0
    for part in parts:
        rows[pl.ds(start, part.shape[0]), :] = part[...]
        start += part.shape[0]


def encode_kernel(count, *refs):
    pieces, (weight, bias, out, rows) = refs[:count], refs[count:]
    gather_rows(pieces, rows)
    value = jnp.dot(rows[...], weight[...], preferred_element_type=F32) + bias[...]
    out[...] = jnp.maximum(value, 0.0).astype(BF16)


def encode_last_kernel(count, *refs):
    pieces, (weight, bias, squares, out, rows, extra) = refs[:count], refs[count:]
    gather_rows(pieces, rows)
    value = jnp.dot(rows[...], weight[...], preferred_element_type=F32) + bias[...]
    out[pl.ds(0, rows.shape[0]), :] = jnp.maximum(value, 0.0).astype(BF16)
    extra[...] = jnp.zeros(extra.shape, F32)
    rest = squares[...]
    layers = rest.shape[0]
    for part in range(3):
        term = rest.astype(BF16).astype(F32)
        extra[pl.ds(part * layers, layers), :] = term
        rest = rest - term
    out[pl.ds(rows.shape[0], extra.shape[0]), :] = extra[...].astype(BF16)


def sort_kernel(layers, order, *refs):
    acts, out = refs[:layers], refs[layers]
    target = lax.axis_index("layer")
    first, features = acts[0].shape
    for offset in range(layers):
        place = pl.ds(pl.multiple_of((target ^ offset) * features, features), features)
        out[:, place] = jnp.dot(order[:, :first], acts[offset][...], preferred_element_type=F32)


def decode_kernel(layers, last, columns, order_ref, first_sorted, *refs):
    acts, weights = refs[:layers], refs[layers]
    acts_out, keep, send, norms = refs[layers + 1 :]
    target = lax.axis_index("layer")
    features, width = weights.shape[1:]
    total_rows = order_ref.shape[0]
    first = total_rows - last
    for offset in range(layers):
        source = target ^ offset
        place = pl.ds(pl.multiple_of(source * features, features), features)
        value = jnp.dot(
            order_ref[:, pl.ds(first, last)],
            acts[offset][pl.ds(0, last), :],
            preferred_element_type=F32,
        )
        used = jnp.where(source <= target, 1.0, 0.0)
        acts_out[:, place] = ((first_sorted[:, place] + value) * used).astype(BF16)
    near, far = first // 2, last // 2
    for part in range(width // columns):
        lanes = pl.ds(part * columns, columns)
        block = weights[:, :, lanes].reshape(layers * features, columns)
        value = jnp.dot(acts_out[...], block, preferred_element_type=F32).astype(BF16)
        keep[pl.ds(0, near), lanes] = value[:near]
        send[pl.ds(0, near), lanes] = value[near:first]
        keep[pl.ds(near, far), lanes] = value[first : first + far]
        send[pl.ds(near, far), lanes] = value[first + far :]
    total = jnp.zeros((layers, features), F32)
    for offset in range(layers):
        value = acts[offset][pl.ds(last, acts[0].shape[0] - last), :].astype(F32)
        for part in range(3):
            total = total + value[part * layers : (part + 1) * layers]
    norms[...] = jnp.sqrt(total + 1e-06)


def order_kernel(count, *refs):
    pieces, (order, out, rows) = refs[:count], refs[count:]
    gather_rows(pieces, rows)
    out[...] = lax.dot_general(
        rows[...], order[...], (((0,), (1,)), ((), ())), preferred_element_type=F32
    ).astype(BF16)


def grad_kernel(layers, count, *refs):
    pieces, weights = refs[:count], refs[count]
    outs, rows = refs[count + 1 : count + 1 + layers], refs[count + 1 + layers]
    target = lax.axis_index("layer")
    gather_rows(pieces, rows)
    for offset in range(layers):
        source = target ^ offset
        value = lax.dot_general(
            rows[...], weights[source], (((1,), (1,)), ((), ())), preferred_element_type=F32
        )
        outs[offset][...] = jnp.where(source <= target, value, 0.0).astype(outs[offset].dtype)


def decoder_grad_kernel(loss_scale, acts, norms, main_rows, last_rows, weights, *refs):
    out, bias_out, rows, slots, sems = refs
    layers, features, width = weights.shape
    depth, tall = slots.shape[:2]
    steps = features // tall
    pending = [None] * depth
    gather_parts((main_rows, last_rows), rows)
    bias_out[...] = jnp.sum(rows[...].astype(F32), axis=0, keepdims=True)
    for source in range(layers):
        used = source <= lax.axis_index("layer")
        for step in range(steps):
            slot = (source * steps + step) % depth
            if pending[slot] is not None:
                pending[slot].wait()
            block = acts[:, pl.ds(source * features + step * tall, tall)]
            sums = jnp.sum(block.astype(F32), axis=0, keepdims=True)
            norm = norms[pl.ds(source, 1), pl.ds(step * tall, tall)]
            factor_row = jnp.where(used, sums * loss_scale / norm, 0.0)
            factor = jnp.broadcast_to(factor_row, (128, tall)).T
            product = lax.dot_general(
                block, rows[...], (((0,), (0,)), ((), ())), preferred_element_type=F32
            )
            for part in range(width // 128):
                cut = slice(part * 128, part * 128 + 128)
                value = weights[source, pl.ds(step * tall, tall), cut].astype(F32)
                slots[slot, :, cut] = (product[:, cut] + factor * value).astype(BF16)
            copy = pltpu.make_async_copy(
                slots.at[slot], out.at[source, pl.ds(step * tall, tall)], sems.at[slot]
            )
            copy.start()
            pending[slot] = copy
    for copy in pending:
        if copy is not None:
            copy.wait()


def encoder_grad_kernel(layers, loss_scale, tall, ordered, acts, norms, *refs):
    main_parts, last_parts = refs[:layers], refs[layers : 2 * layers]
    out, sums_out, low, slots, sems = refs[2 * layers :]
    target = lax.axis_index("layer")
    features = main_parts[0].shape[1]
    place = pl.ds(pl.multiple_of(target * features, features), features)
    shift = norms[pl.ds(target, 1), :] * loss_scale
    sums = jnp.zeros((1, features), F32)
    start = 0
    for parts in (main_parts, last_parts):
        total = parts[0][...]
        rows = pl.ds(start, total.shape[0])
        start += total.shape[0]
        for part in parts[1:]:
            total = total + part[...].astype(F32)
        grad = jnp.where(acts[rows, place] > 0, total + shift, 0.0)
        sums = sums + jnp.sum(grad, axis=0, keepdims=True)
        low[rows, :] = grad.astype(BF16)
    sums_out[...] = sums
    width = ordered.shape[0]
    copies = []
    for step in range(width // tall):
        rows = pl.ds(step * tall, tall)
        slots[rows, :] = jnp.dot(
            ordered[rows, :], low[...], preferred_element_type=F32
        ).astype(BF16)
        copy = pltpu.make_async_copy(slots.at[rows], out.at[rows], sems.at[step])
        copy.start()
        copies.append(copy)
    for copy in copies:
        copy.wait()


def on_device(
    layer_inputs,
    layer_targets,
    row_order,
    encoder_weight,
    encoder_bias,
    decoder_weight,
    decoder_bias,
):
    layers = lax.axis_size("layer")
    ranks = lax.axis_size("tok")
    lines = ranks // 2
    row_total = row_order.shape[0]
    height = row_total // ranks
    loss_scale = 1.0 / math.sqrt(row_total)
    weights = decoder_weight[0]
    features, width = weights.shape[1:]
    last = 2 * height
    first = row_total - last
    groups = (range(lines - 1), range(lines - 1, lines))
    hbm = pl.BlockSpec(memory_space=pltpu.HBM)
    struct = jax.ShapeDtypeStruct
    block_flops = 2 * row_total * features * width

    def swap_tok(value, step):
        return lax.ppermute(value, "tok", [(i, i ^ step) for i in range(ranks)])

    def swap_layer(value, step):
        return lax.ppermute(value, "layer", [(i, i ^ step) for i in range(layers)])

    def gather_lines(own, before=()):
        lane = {0: own}
        for line in sorted(range(1, lines), key=lambda j: (bin(j).count("1"), j)):
            low = line & -line
            lane[line] = swap_tok(lane[line ^ low], 2 * low)
        here, *_ = lax.optimization_barrier((own, *before)) if before else (own,)
        main = [lane[j] for j in groups[0]]
        main += [swap_tok(lane[j] if j else here, 1) for j in groups[0]]
        return main, [lane[lines - 1]]

    def other_core(pieces, after):
        *pieces, _ = lax.optimization_barrier((*pieces, after))
        return pieces + [swap_tok(piece, 1) for piece in pieces]

    relative = []
    for group in groups:
        for core in range(2):
            relative += [2 * j + core for j in group]
    order = call(
        functools.partial(table_kernel, tuple(relative)),
        struct((row_total, row_total), BF16),
        whole(1),
        whole(1)[0],
        [pltpu.VMEM((row_total, row_total), F32)],
        6 * MICROSECOND,
        4 * row_total * row_total,
    )(row_order[None])

    squares = call(
        norm_kernel,
        struct((layers, features), F32),
        whole(1),
        whole(1)[0],
        [],
        4 * layers * features * width,
        2 * layers * features * width,
    )(weights)
    main_inputs, last_inputs = gather_lines(layer_inputs[0], (order, squares))
    encode_operands = (encoder_weight[0], encoder_bias)
    main_own = call(
        functools.partial(encode_kernel, len(main_inputs)),
        struct((first, features), BF16),
        whole(len(main_inputs) + 2),
        whole(1)[0],
        [pltpu.VMEM((first, width), BF16)],
        2 * first * width * features,
        2 * width * features,
    )(*main_inputs, *encode_operands)
    main_acts = [main_own] + [swap_layer(main_own, step) for step in range(1, layers)]
    last_inputs = other_core(last_inputs, main_own)
    extra = -(-3 * layers // 16) * 16
    last_own = call(
        functools.partial(encode_last_kernel, len(last_inputs)),
        struct((last + extra, features), BF16),
        whole(len(last_inputs) + 3),
        whole(1)[0],
        [pltpu.VMEM((last, width), BF16), pltpu.VMEM((extra, features), F32)],
        2 * last * width * features,
        2 * width * features,
    )(*last_inputs, *encode_operands, squares)
    last_acts = [last_own] + [swap_layer(last_own, step) for step in range(1, layers)]
    first_sorted = call(
        functools.partial(sort_kernel, layers),
        struct((row_total, layers * features), F32),
        whole(layers + 1),
        whole(1)[0],
        [],
        2 * row_total * first * layers * features,
        2 * first * layers * features,
    )(order, *main_acts)

    columns = min(512, width)
    acts_all, keep, send, norms = call(
        functools.partial(decode_kernel, layers, last, columns),
        (
            struct((row_total, layers * features), BF16),
            struct((row_total // 2, width), BF16),
            struct((row_total // 2, width), BF16),
            struct((layers, features), F32),
        ),
        whole(3 + layers),
        tuple(whole(4)),
        [],
        layers * block_flops,
        2 * layers * features * width,
    )(order, first_sorted, *last_acts, weights)

    pair = keep.astype(F32) + swap_tok(send, 1).astype(F32)
    parts = [pair[i * height : (i + 1) * height] for i in range(lines)]
    last_leaf = None
    for line in reversed(range(1, lines)):
        low = line & -line
        block = parts[line].astype(BF16)
        if low == 1 and last_leaf is not None:
            block, last_leaf = lax.optimization_barrier((block, last_leaf))
        arrived = swap_tok(block, 2 * low)
        if low == 1:
            last_leaf = arrived
        parts[line ^ low] = parts[line ^ low] + arrived.astype(F32)
    resid_full = (
        parts[0] + decoder_bias[0] - layer_targets[0].astype(F32)
    ) * loss_scale

    _, *late = lax.optimization_barrier((send, *main_inputs, *last_inputs))
    ordered = call(
        functools.partial(order_kernel, len(late)),
        struct((width, row_total), BF16),
        whole(len(late) + 1),
        whole(1)[0],
        [pltpu.VMEM((row_total, width), BF16)],
        2 * row_total * row_total * width,
        4 * row_total * width,
    )(*late, order)
    resid_low, ordered = lax.optimization_barrier((resid_full.astype(BF16), ordered))
    main_resid, last_resid = gather_lines(resid_low)

    def grad_acts(pieces):
        count = len(pieces) * height
        *parts, rows = call(
            functools.partial(grad_kernel, layers, len(pieces)),
            (
                *[struct((count, features), BF16 if step else F32) for step in range(layers)],
                struct((count, width), BF16),
            ),
            whole(len(pieces) + 1),
            tuple(whole(layers + 1)),
            [],
            2 * count * layers * features * width,
            2 * layers * features * width,
        )(*pieces, weights)
        sums = [swap_layer(parts[step], step) if step else parts[0] for step in range(layers)]
        return parts[0], sums, rows

    main_grad, main_sums, main_rows = grad_acts(main_resid)
    last_resid = other_core(last_resid, main_grad)
    _, last_sums, last_rows = grad_acts(last_resid)

    tall = math.gcd(256, features)
    decoder_grad, bias_grad = call(
        functools.partial(decoder_grad_kernel, loss_scale),
        (struct((layers, features, width), BF16), struct((1, width), F32)),
        whole(5),
        (hbm, whole(1)[0]),
        [
            pltpu.VMEM((row_total, width), BF16),
            pltpu.VMEM((4, tall, width), BF16),
            pltpu.SemaphoreType.DMA((4,)),
        ],
        layers * block_flops,
        4 * layers * features * width,
    )(acts_all, norms, main_rows, last_rows, weights)

    tall = min(512, width)
    encoder_grad, feature_grad = call(
        functools.partial(encoder_grad_kernel, layers, loss_scale, tall),
        (struct((width, features), BF16), struct((1, features), F32)),
        whole(3 + 2 * layers),
        (hbm, whole(1)[0]),
        [
            pltpu.VMEM((row_total, features), BF16),
            pltpu.VMEM((width, features), BF16),
            pltpu.SemaphoreType.DMA((width // tall,)),
        ],
        block_flops,
        2 * features * width,
    )(ordered, acts_all, norms, *main_sums, *last_sums)
    return (encoder_grad[None], feature_grad, decoder_grad[None], bias_grad)


def solution(mesh):
    placed = (
        P("layer", "tok", None),
        P("layer", "tok", None),
        P(),
        P("layer", None, "tok"),
        P("layer", "tok"),
        P("layer", None, "tok", None),
        P("layer", None),
    )
    return jax.shard_map(
        on_device,
        mesh=mesh,
        in_specs=placed,
        out_specs=(
            P("layer", None, "tok"),
            P("layer", "tok"),
            P("layer", None, "tok", None),
            P("layer", None),
        ),
        check_vma=False,
    )
```

time: 250 us -> 81.9 us (0.33)
  the two profiles are of different devices: /device:TPU:7 before, /device:TPU:0 now
where the time goes in v2:
time: 81.9 us; the launch traced here: 81.7 us
  starting transfers between devices  30.1 us (37%)
  waiting for transfers between devices  26.1 us (32%)
  Pallas kernels  20.3 us (25%)
  local copies, waits for them, and re-layouts  3.98 us (5%)
  between operations  0.98 us (1%)
    ppermute x18, waiting for transfers between devices, swap_tok(): return lax.ppermute(value, 'tok', [(i, i ^ step) for i in range(ranks)])  21.5 us
    ppermute x12, starting transfers between devices, swap_layer(): return lax.ppermute(value, 'layer', [(i, i ^ step) for i in range(layers)])  17.3 us
    ppermute x18, starting transfers between devices, swap_tok(): return lax.ppermute(value, 'tok', [(i, i ^ step) for i in range(ranks)])  12.8 us
    pallas_call x2, Pallas kernels, grad_acts(): call(functools.partial(grad_kernel, layers, len(pieces)), (*[struct((coun...  5.55 us
    pallas_call x1, Pallas kernels, on_device(): call(functools.partial(decoder_grad_kernel, loss_scale), (struct((layers,...  5.41 us
    ppermute x12, waiting for transfers between devices, swap_layer(): return lax.ppermute(value, 'layer', [(i, i ^ step) for i in range(layers)])  4.59 us
    unnamed x14, local copies, waits for them, and re-layouts  3.96 us
    pallas_call x1, Pallas kernels, on_device(): call(functools.partial(decode_kernel, layers, last, columns), (struct((ro...  2.84 us
  transfers between devices with their start and end apart: 30, of which 16 were waited for; matrix products, arithmetic and copies ran while one was open for 0% of the time, Pallas kernels for 18%

profile of v2, /device:TPU:0, one launch (start us, length us, event | category | flops | bytes accessed | tf_op | source)
XLA Modules:
  0.0 81.7 jit_solution(14982122215698902150)
XLA Ops:
  0.6 4.1 %collective-permute-start.1 = (bf16[32,2048]{1,0:T(8,128)(2,1)}, bf16[32,2048]{1,0:T(8,128)(2,1)S(1)}, u32[]{:S(2)}, u32[]{:S(2)}) collective-permute-start(bf16[32,2048]{1,0:T(8,128)(2,1)} %bitcast.17), channel_id=1, source_target_pairs={{0,4},{1,5},{2,6},{3,7},{4,0},{5,1},{6,2},{7,3},{8,12},{9,13},{10,... | collective-permute-start | bytes 393224 | tf_op jit(solution)/shard_map/ppermute | solution.py:254
  4.7 1.6 %collective-permute-start = (bf16[32,2048]{1,0:T(8,128)(2,1)}, bf16[32,2048]{1,0:T(8,128)(2,1)S(1)}, u32[]{:S(2)}, u32[]{:S(2)}) collective-permute-start(bf16[32,2048]{1,0:T(8,128)(2,1)} %bitcast.18), channel_id=1, source_target_pairs={{0,2},{1,3},{2,0},{3,1},{4,6},{5,7},{6,4},{7,5},{8,10},{9,11},{10,... | collective-permute-start | bytes 393224 | tf_op jit(solution)/shard_map/ppermute | solution.py:254
  6.3 0.7 copy-done.4
  7.0 0.1 shard_map.102.order.order_ref.refs_8_
  7.1 3.3 %copy-done = bf16[1,4,512,2048]{3,2,1,0:T(8,128)(2,1)S(1)} copy-done((bf16[1,4,512,2048]{3,2,1,0:T(8,128)(2,1)S(1)}, bf16[1,4,512,2048]{3,2,1,0:T(8,128)(2,1)}, u32[]{:S(2)}) %copy-start) | copy-done | bytes 8388632
  10.4 1.9 %shard_map.103.refs_4_ = f32[4,512]{1,0:T(4,128)S(1)} custom-call(bf16[4,512,2048]{2,1,0:T(8,128)(2,1)S(1)} %bitcast.10), custom_call_target="tpu_custom_call" | custom-call | flops 16777216 | bytes 8388608 | tf_op jit(solution)/shard_map/pallas_call | solution.py:287
  12.3 0.1 collective-permute-start.2
  12.4 0.0 collective-permute-done.1.refs_2_
  12.4 0.5 collective-permute-start.4
  12.9 0.0 collective-permute-done.refs_1_
  12.9 0.1 collective-permute-start.3
  12.9 0.4 collective-permute-start.8
  13.4 0.3 collective-permute-done.2.refs_3_
  13.7 0.2 collective-permute-done.4.refs_5_
  13.9 0.3 collective-permute-done.3.refs_4_
  14.2 0.6 shard_map.104.refs_0_
  14.8 2.5 %collective-permute-start.7 = (bf16[192,512]{1,0:T(8,128)(2,1)S(1)}, bf16[192,512]{1,0:T(8,128)(2,1)S(1)}, u32[]{:S(2)}, u32[]{:S(2)}) collective-permute-start(bf16[192,512]{1,0:T(8,128)(2,1)S(1)} %shard_map.104.refs_0_), channel_id=1, source_target_pairs={{0,24},{8,16},{16,8},{24,0},{1,25},{9,17},{17,9},{25,1},{2,26},{10... | collective-permute-start | bytes 589832 | tf_op jit(solution)/shard_map/ppermute | solution.py:257
  17.3 1.5 %collective-permute-done.8.refs_0_.refs_6_ = bf16[32,2048]{1,0:T(8,128)(2,1)S(1)} collective-permute-done((bf16[32,2048]{1,0:T(8,128)(2,1)S(1)}, bf16[32,2048]{1,0:T(8,128)(2,1)S(1)}, u32[]{:S(2)}, u32[]{:S(2)}) %collective-permute-start.8) | collective-permute-done | bytes 131104 | tf_op jit(solution)/shard_map/ppermute | solution.py:254
  18.8 1.5 %collective-permute-start.6 = (bf16[192,512]{1,0:T(8,128)(2,1)S(1)}, bf16[192,512]{1,0:T(8,128)(2,1)S(1)}, u32[]{:S(2)}, u32[]{:S(2)}) collective-permute-start(bf16[192,512]{1,0:T(8,128)(2,1)S(1)} %shard_map.104.refs_0_), channel_id=1, source_target_pairs={{0,16},{8,24},{16,0},{24,8},{1,17},{9,25},{17,1},{25,9},{2,18},{10... | collective-permute-start | bytes 589832 | tf_op jit(solution)/shard_map/ppermute | solution.py:257
  20.3 1.5 %collective-permute-start.5 = (bf16[192,512]{1,0:T(8,128)(2,1)S(1)}, bf16[192,512]{1,0:T(8,128)(2,1)S(1)}, u32[]{:S(2)}, u32[]{:S(2)}) collective-permute-start(bf16[192,512]{1,0:T(8,128)(2,1)S(1)} %shard_map.104.refs_0_), channel_id=1, source_target_pairs={{0,8},{8,0},{16,24},{24,16},{1,9},{9,1},{17,25},{25,17},{2,10},{10... | collective-permute-start | bytes 589832 | tf_op jit(solution)/shard_map/ppermute | solution.py:257
  21.8 0.5 shard_map.106.refs_0_
  22.3 0.8 %collective-permute-start.12 = (bf16[80,512]{1,0:T(8,128)(2,1)S(1)}, bf16[80,512]{1,0:T(8,128)(2,1)S(1)}, u32[]{:S(2)}, u32[]{:S(2)}) collective-permute-start(bf16[80,512]{1,0:T(8,128)(2,1)S(1)} %shard_map.106.refs_0_), channel_id=1, source_target_pairs={{0,24},{8,16},{16,8},{24,0},{1,25},{9,17},{17,9},{25,1},{2,26},{10... | collective-permute-start | bytes 245768 | tf_op jit(solution)/shard_map/ppermute | solution.py:257
  23.1 1.2 %collective-permute-start.11 = (bf16[80,512]{1,0:T(8,128)(2,1)S(1)}, bf16[80,512]{1,0:T(8,128)(2,1)S(1)}, u32[]{:S(2)}, u32[]{:S(2)}) collective-permute-start(bf16[80,512]{1,0:T(8,128)(2,1)S(1)} %shard_map.106.refs_0_), channel_id=1, source_target_pairs={{0,16},{8,24},{16,0},{24,8},{1,17},{9,25},{17,1},{25,9},{2,18},{10... | collective-permute-start | bytes 245768 | tf_op jit(solution)/shard_map/ppermute | solution.py:257
  24.4 1.5 %collective-permute-start.10 = (bf16[80,512]{1,0:T(8,128)(2,1)S(1)}, bf16[80,512]{1,0:T(8,128)(2,1)S(1)}, u32[]{:S(2)}, u32[]{:S(2)}) collective-permute-start(bf16[80,512]{1,0:T(8,128)(2,1)S(1)} %shard_map.106.refs_0_), channel_id=1, source_target_pairs={{0,8},{8,0},{16,24},{24,16},{1,9},{9,1},{17,25},{25,17},{2,10},{10... | collective-permute-start | bytes 245768 | tf_op jit(solution)/shard_map/ppermute | solution.py:257
  25.9 1.6 %collective-permute-done.6.refs_2_ = bf16[192,512]{1,0:T(8,128)(2,1)S(1)} collective-permute-done((bf16[192,512]{1,0:T(8,128)(2,1)S(1)}, bf16[192,512]{1,0:T(8,128)(2,1)S(1)}, u32[]{:S(2)}, u32[]{:S(2)}) %collective-permute-start.6) | collective-permute-done | bytes 196640 | tf_op jit(solution)/shard_map/ppermute | solution.py:257
  27.5 0.6 collective-permute-done.5.refs_1_
  28.0 0.4 shard_map.105.first_sorted
  28.5 1.3 %collective-permute-done.12.refs_3_ = bf16[80,512]{1,0:T(8,128)(2,1)S(1)} collective-permute-done((bf16[80,512]{1,0:T(8,128)(2,1)S(1)}, bf16[80,512]{1,0:T(8,128)(2,1)S(1)}, u32[]{:S(2)}, u32[]{:S(2)}) %collective-permute-start.12) | collective-permute-done | bytes 81952 | tf_op jit(solution)/shard_map/ppermute | solution.py:257
  29.7 0.8 collective-permute-done.11.refs_2_
  30.5 0.4 collective-permute-done.10.refs_1_
  30.9 2.8 %shard_map.107 = (bf16[256,2048]{1,0:T(8,128)(2,1)S(1)}, bf16[128,2048]{1,0:T(8,128)(2,1)S(1)}, bf16[128,2048]{1,0:T(8,128)(2,1)S(1)}, f32[4,512]{1,0:T(4,128)S(1)}) custom-call(bf16[256,256]{1,0:T(8,128)(2,1)S(1)} %shard_map.102.order.order_ref.refs_8_, f32[256,2048]{1,0:T(8,128)S(1)} %shard_map.105.first_sorted, bf16[80,512]{1,0:T(8,128)(2,1)S(1)} %shard_map.106.refs_0_, ...), custom_call_target="tpu_custom_call" | custom-call | flops 2147483648 | bytes 8388608 | tf_op jit(solution)/shard_map/pallas_call | solution.py:331
  33.7 0.1 collective-permute-start.13
  33.8 1.9 %collective-permute-done.13 = bf16[128,2048]{1,0:T(8,128)(2,1)S(1)} collective-permute-done((bf16[128,2048]{1,0:T(8,128)(2,1)S(1)}, bf16[128,2048]{1,0:T(8,128)(2,1)S(1)}, u32[]{:S(2)}, u32[]{:S(2)}) %collective-permute-start.13) | collective-permute-done | bytes 524320 | tf_op jit(solution)/shard_map/ppermute | solution.py:254
  35.7 0.1 fusion.6
  35.8 0.0 copy-start.5
  35.8 0.0 copy-start.6
  35.9 0.5 collective-permute-start.14
  36.4 5.1 %collective-permute-done.14 = bf16[32,2048]{1,0:T(8,128)(2,1)S(1)} collective-permute-done((bf16[32,2048]{1,0:T(8,128)(2,1)S(1)}, bf16[32,2048]{1,0:T(8,128)(2,1)S(1)}, u32[]{:S(2)}, u32[]{:S(2)}) %collective-permute-start.14) | collective-permute-done | bytes 131104 | tf_op jit(solution)/shard_map/ppermute | solution.py:254
  41.5 1.0 %collective-permute-start.15 = (bf16[32,2048]{1,0:T(8,128)(2,1)S(1)}, bf16[32,2048]{1,0:T(8,128)(2,1)S(1)}, u32[]{:S(2)}, u32[]{:S(2)}) collective-permute-start(bf16[32,2048]{1,0:T(8,128)(2,1)S(1)} %fusion), channel_id=1, source_target_pairs={{0,4},{1,5},{2,6},{3,7},{4,0},{5,1},{6,2},{7,3},{8,12},{9,13},{10,... | collective-permute-start | bytes 393224 | tf_op jit(solution)/shard_map/ppermute | solution.py:254
  42.5 1.6 %collective-permute-start.16 = (bf16[32,2048]{1,0:T(8,128)(2,1)S(1)}, bf16[32,2048]{1,0:T(8,128)(2,1)S(1)}, u32[]{:S(2)}, u32[]{:S(2)}) collective-permute-start(bf16[32,2048]{1,0:T(8,128)(2,1)S(1)} %get-tuple-element.40), channel_id=1, source_target_pairs={{0,2},{1,3},{2,0},{3,1},{4,6},{5,7},{6,4},{7,5},{8,10},{9,11},{10,... | collective-permute-start | bytes 393224 | tf_op jit(solution)/shard_map/ppermute | solution.py:254
  44.1 0.5 shard_map.108.ordered
  44.6 5.3 %collective-permute-done.15 = bf16[32,2048]{1,0:T(8,128)(2,1)S(1)} collective-permute-done((bf16[32,2048]{1,0:T(8,128)(2,1)S(1)}, bf16[32,2048]{1,0:T(8,128)(2,1)S(1)}, u32[]{:S(2)}, u32[]{:S(2)}) %collective-permute-start.15) | collective-permute-done | bytes 131104 | tf_op jit(solution)/shard_map/ppermute | solution.py:254
  49.9 0.1 fusion.5.refs_0_
  50.0 0.6 collective-permute-start.18
  50.6 2.0 %collective-permute-start.17 = (bf16[32,2048]{1,0:T(8,128)(2,1)S(1)}, bf16[32,2048]{1,0:T(8,128)(2,1)S(1)}, u32[]{:S(2)}, u32[]{:S(2)}) collective-permute-start(bf16[32,2048]{1,0:T(8,128)(2,1)S(1)} %fusion.5.refs_0_), channel_id=1, source_target_pairs={{0,2},{1,3},{2,0},{3,1},{4,6},{5,7},{6,4},{7,5},{8,10},{9,11},{10,... | collective-permute-start | bytes 393224 | tf_op jit(solution)/shard_map/ppermute | solution.py:254
  52.6 5.6 %collective-permute-done.18.refs_2_ = bf16[32,2048]{1,0:T(8,128)(2,1)S(1)} collective-permute-done((bf16[32,2048]{1,0:T(8,128)(2,1)S(1)}, bf16[32,2048]{1,0:T(8,128)(2,1)S(1)}, u32[]{:S(2)}, u32[]{:S(2)}) %collective-permute-start.18) | collective-permute-done | bytes 131104 | tf_op jit(solution)/shard_map/ppermute | solution.py:254
  58.2 0.0 collective-permute-start.21
  58.2 0.2 collective-permute-done.17.refs_1_
  58.4 0.3 collective-permute-start.20
  58.7 0.0 collective-permute-start.25
  58.7 0.0 collective-permute-done.19.refs_3_
  58.7 0.8 %collective-permute-done.21.refs_5_ = bf16[32,2048]{1,0:T(8,128)(2,1)S(1)} collective-permute-done((bf16[32,2048]{1,0:T(8,128)(2,1)S(1)}, bf16[32,2048]{1,0:T(8,128)(2,1)S(1)}, u32[]{:S(2)}, u32[]{:S(2)}) %collective-permute-start.21) | collective-permute-done | bytes 131104 | tf_op jit(solution)/shard_map/ppermute | solution.py:254
  59.6 0.2 collective-permute-done.20.refs_4_
  59.8 2.9 %shard_map.109 = (f32[192,512]{1,0:T(8,128)S(1)}, bf16[192,512]{1,0:T(8,128)(2,1)S(1)}, bf16[192,512]{1,0:T(8,128)(2,1)S(1)}, bf16[192,512]{1,0:T(8,128)(2,1)S(1)}, bf16[192,2048]{1,0:T(8,128)(2,1)S(1)}) custom-call(bf16[32,2048]{1,0:T(8,128)(2,1)S(1)} %fusion.5.refs_0_, bf16[32,2048]{1,0:T(8,128)(2,1)S(1)} %collective-permute-done.17.refs_1_, ...), custom_call_target="tpu_custom_call" | custom-call | flops 1610612736 | bytes 8388608 | tf_op jit(solution)/shard_map/pallas_call | solution.py:377
  62.7 1.6 %collective-permute-start.22 = (bf16[192,512]{1,0:T(8,128)(2,1)S(1)}, bf16[192,512]{1,0:T(8,128)(2,1)S(1)}, u32[]{:S(2)}, u32[]{:S(2)}) collective-permute-start(bf16[192,512]{1,0:T(8,128)(2,1)S(1)} %get-tuple-element.54), channel_id=1, source_target_pairs={{0,8},{8,0},{16,24},{24,16},{1,9},{9,1},{17,25},{25,17},{2,10},{10... | collective-permute-start | bytes 589832 | tf_op jit(solution)/shard_map/ppermute | solution.py:257
  64.3 0.0 collective-permute-done.25.refs_0_
  64.4 1.5 %collective-permute-start.23 = (bf16[192,512]{1,0:T(8,128)(2,1)S(1)}, bf16[192,512]{1,0:T(8,128)(2,1)S(1)}, u32[]{:S(2)}, u32[]{:S(2)}) collective-permute-start(bf16[192,512]{1,0:T(8,128)(2,1)S(1)} %get-tuple-element.55), channel_id=1, source_target_pairs={{0,16},{8,24},{16,0},{24,8},{1,17},{9,25},{17,1},{25,9},{2,18},{10... | collective-permute-start | bytes 589832 | tf_op jit(solution)/shard_map/ppermute | solution.py:257
  65.9 1.5 %collective-permute-start.24 = (bf16[192,512]{1,0:T(8,128)(2,1)S(1)}, bf16[192,512]{1,0:T(8,128)(2,1)S(1)}, u32[]{:S(2)}, u32[]{:S(2)}) collective-permute-start(bf16[192,512]{1,0:T(8,128)(2,1)S(1)} %get-tuple-element.56), channel_id=1, source_target_pairs={{0,24},{8,16},{16,8},{24,0},{1,25},{9,17},{17,9},{25,1},{2,26},{10... | collective-permute-start | bytes 589832 | tf_op jit(solution)/shard_map/ppermute | solution.py:257
  67.4 2.7 %shard_map.110 = (f32[64,512]{1,0:T(8,128)S(1)}, bf16[64,512]{1,0:T(8,128)(2,1)S(1)}, bf16[64,512]{1,0:T(8,128)(2,1)S(1)}, bf16[64,512]{1,0:T(8,128)(2,1)S(1)}, bf16[64,2048]{1,0:T(8,128)(2,1)S(1)}) custom-call(bf16[32,2048]{1,0:T(8,128)(2,1)S(1)} %collective-permute-done.25.refs_0_, bf16[32,2048]{1,0:T(8,128)(2,1)S(1)} %collective-permute-done.26.refs_1_, ...), custom_call_target="tpu_custom_call" | custom-call | flops 536870912 | bytes 8388608 | tf_op jit(solution)/shard_map/pallas_call | solution.py:377
  70.0 0.5 collective-permute-start.27
  70.6 1.5 %collective-permute-start.28 = (bf16[64,512]{1,0:T(8,128)(2,1)S(1)}, bf16[64,512]{1,0:T(8,128)(2,1)S(1)}, u32[]{:S(2)}, u32[]{:S(2)}) collective-permute-start(bf16[64,512]{1,0:T(8,128)(2,1)S(1)} %get-tuple-element.60), channel_id=1, source_target_pairs={{0,16},{8,24},{16,0},{24,8},{1,17},{9,25},{17,1},{25,9},{2,18},{10... | collective-permute-start | bytes 196616 | tf_op jit(solution)/shard_map/ppermute | solution.py:257
  72.1 1.5 %collective-permute-start.29 = (bf16[64,512]{1,0:T(8,128)(2,1)S(1)}, bf16[64,512]{1,0:T(8,128)(2,1)S(1)}, u32[]{:S(2)}, u32[]{:S(2)}) collective-permute-start(bf16[64,512]{1,0:T(8,128)(2,1)S(1)} %get-tuple-element.61), channel_id=1, source_target_pairs={{0,24},{8,16},{16,8},{24,0},{1,25},{9,17},{17,9},{25,1},{2,26},{10... | collective-permute-start | bytes 196616 | tf_op jit(solution)/shard_map/ppermute | solution.py:257
  73.6 5.4 %shard_map.112 = (bf16[4,512,2048]{2,1,0:T(8,128)(2,1)}, f32[1,2048]{1,0:T(1,128)}) custom-call(bf16[256,2048]{1,0:T(8,128)(2,1)S(1)} %get-tuple-element.50.acts, f32[4,512]{1,0:T(4,128)S(1)} %get-tuple-element.51.norms, bf16[192,2048]{1,0:T(8,128)(2,1)S(1)} %get-tuple-element.64.main_rows, bf16[64,2048]{1,0:T(8,128)(2,1)S(1)} %get-tuple-element.65.last_rows, ...), custom_call_target="tpu_custom_call" | custom-call | flops 2147483648 | bytes 16777216 | tf_op jit(solution)/shard_map/pallas_call | solution.py:397
  79.1 2.5 %shard_map.111 = (bf16[2048,512]{1,0:T(8,128)(2,1)}, f32[1,512]{1,0:T(1,128)}) custom-call(bf16[2048,256]{1,0:T(8,128)(2,1)S(1)} %shard_map.108.ordered, bf16[256,2048]{1,0:T(8,128)(2,1)S(1)} %get-tuple-element.50.acts, f32[4,512]{1,0:T(4,128)S(1)} %get-tuple-element.51.norms, f32[192,512]{1,0:T(8,128)S(1)} %get-tuple-element.53.refs_0_, ...), custom_call_target="tpu_custom_call" | custom-call | flops 536870912 | bytes 2097152 | tf_op jit(solution)/shard_map/pallas_call | solution.py:412
  (25 shorter events, 0.1 us)
Async XLA Ops:
  0.6 11.7 %collective-permute-start.1 = (bf16[32,2048]{1,0:T(8,128)(2,1)}, bf16[32,2048]{1,0:T(8,128)(2,1)S(1)}, u32[]{:S(2)}, u32[]{:S(2)}) collective-permute-start(bf16[32,2048]{1,0:T(8,128)(2,1)} %bitcast.17), channel_id=1, source_target_pairs={{0,4},{1,5},{2,6},{3,7},{4,0},{5,1},{6,2},{7,3},{8,12},{9,13},{10,... | collective-permute-start | bytes 393224 | tf_op jit(solution)/shard_map/ppermute | solution.py:254
  4.7 8.1 %collective-permute-start = (bf16[32,2048]{1,0:T(8,128)(2,1)}, bf16[32,2048]{1,0:T(8,128)(2,1)S(1)}, u32[]{:S(2)}, u32[]{:S(2)}) collective-permute-start(bf16[32,2048]{1,0:T(8,128)(2,1)} %bitcast.18), channel_id=1, source_target_pairs={{0,2},{1,3},{2,0},{3,1},{4,6},{5,7},{6,4},{7,5},{8,10},{9,11},{10,... | collective-permute-start | bytes 393224 | tf_op jit(solution)/shard_map/ppermute | solution.py:254
  6.3 0.7 copy-start.4
  7.0 3.4 %copy-start = (bf16[1,4,512,2048]{3,2,1,0:T(8,128)(2,1)S(1)}, bf16[1,4,512,2048]{3,2,1,0:T(8,128)(2,1)}, u32[]{:S(2)}) copy-start(bf16[1,4,512,2048]{3,2,1,0:T(8,128)(2,1)} %param.12) | copy-start | bytes 25165828
  10.4 1.9 %copy-start.2 = (bf16[1,32,2048]{2,1,0:T(8,128)(2,1)S(1)}, bf16[1,32,2048]{2,1,0:T(8,128)(2,1)}, u32[]{:S(2)}) copy-start(bf16[1,32,2048]{2,1,0:T(8,128)(2,1)} %param.7) | copy-start | bytes 393220
  10.4 3.8 %copy-start.1 = (bf16[1,2048,512]{2,1,0:T(8,128)(2,1)S(1)}, bf16[1,2048,512]{2,1,0:T(8,128)(2,1)}, u32[]{:S(2)}) copy-start(bf16[1,2048,512]{2,1,0:T(8,128)(2,1)} %param.10) | copy-start | bytes 6291460
  10.4 3.8 %copy-start.3 = (f32[1,512]{1,0:T(1,128)S(1)}, f32[1,512]{1,0:T(1,128)}, u32[]{:S(2)}) copy-start(f32[1,512]{1,0:T(1,128)} %refs_3_.1) | copy-start | bytes 6148
  12.3 1.4 %collective-permute-start.2 = (bf16[32,2048]{1,0:T(8,128)(2,1)S(1)}, bf16[32,2048]{1,0:T(8,128)(2,1)S(1)}, u32[]{:S(2)}, u32[]{:S(2)}) collective-permute-start(bf16[32,2048]{1,0:T(8,128)(2,1)S(1)} %bitcast.19), channel_id=1, source_target_pairs={{0,1},{1,0},{2,3},{3,2},{4,5},{5,4},{6,7},{7,6},{8,9},{9,8},{10,11... | collective-permute-start | bytes 393224 | tf_op jit(solution)/shard_map/ppermute | solution.py:254
  12.4 1.5 %collective-permute-start.4 = (bf16[32,2048]{1,0:T(8,128)(2,1)S(1)}, bf16[32,2048]{1,0:T(8,128)(2,1)S(1)}, u32[]{:S(2)}, u32[]{:S(2)}) collective-permute-start(bf16[32,2048]{1,0:T(8,128)(2,1)S(1)} %collective-permute-done.1.refs_2_), channel_id=1, source_target_pairs={{0,1},{1,0},{2,3},{3,2},{4,5},{5,4},{6,7},{7,6},{8,9},{9,8},{10,11... | collective-permute-start | bytes 393224 | tf_op jit(solution)/shard_map/ppermute | solution.py:254
  12.9 1.3 %collective-permute-start.3 = (bf16[32,2048]{1,0:T(8,128)(2,1)S(1)}, bf16[32,2048]{1,0:T(8,128)(2,1)S(1)}, u32[]{:S(2)}, u32[]{:S(2)}) collective-permute-start(bf16[32,2048]{1,0:T(8,128)(2,1)S(1)} %collective-permute-done.refs_1_), channel_id=1, source_target_pairs={{0,1},{1,0},{2,3},{3,2},{4,5},{5,4},{6,7},{7,6},{8,9},{9,8},{10,11... | collective-permute-start | bytes 393224 | tf_op jit(solution)/shard_map/ppermute | solution.py:254
  12.9 5.8 %collective-permute-start.8 = (bf16[32,2048]{1,0:T(8,128)(2,1)S(1)}, bf16[32,2048]{1,0:T(8,128)(2,1)S(1)}, u32[]{:S(2)}, u32[]{:S(2)}) collective-permute-start(bf16[32,2048]{1,0:T(8,128)(2,1)S(1)} %collective-permute-done.1.refs_2_), channel_id=1, source_target_pairs={{0,2},{1,3},{2,0},{3,1},{4,6},{5,7},{6,4},{7,5},{8,10},{9,11},{10,... | collective-permute-start | bytes 393224 | tf_op jit(solution)/shard_map/ppermute | solution.py:254
  14.8 9.5 %collective-permute-start.7 = (bf16[192,512]{1,0:T(8,128)(2,1)S(1)}, bf16[192,512]{1,0:T(8,128)(2,1)S(1)}, u32[]{:S(2)}, u32[]{:S(2)}) collective-permute-start(bf16[192,512]{1,0:T(8,128)(2,1)S(1)} %shard_map.104.refs_0_), channel_id=1, source_target_pairs={{0,24},{8,16},{16,8},{24,0},{1,25},{9,17},{17,9},{25,1},{2,26},{10... | collective-permute-start | bytes 589832 | tf_op jit(solution)/shard_map/ppermute | solution.py:257
  18.8 3.0 %collective-permute-start.9 = (bf16[32,2048]{1,0:T(8,128)(2,1)S(1)}, bf16[32,2048]{1,0:T(8,128)(2,1)S(1)}, u32[]{:S(2)}, u32[]{:S(2)}) collective-permute-start(bf16[32,2048]{1,0:T(8,128)(2,1)S(1)} %collective-permute-done.8.refs_0_.refs_6_), channel_id=1, source_target_pairs={{0,1},{1,0},{2,3},{3,2},{4,5},{5,4},{6,7},{7,6},{8,9},{9,8},{10,11... | collective-permute-start | bytes 393224 | tf_op jit(solution)/shard_map/ppermute | solution.py:254
  18.8 8.7 %collective-permute-start.6 = (bf16[192,512]{1,0:T(8,128)(2,1)S(1)}, bf16[192,512]{1,0:T(8,128)(2,1)S(1)}, u32[]{:S(2)}, u32[]{:S(2)}) collective-permute-start(bf16[192,512]{1,0:T(8,128)(2,1)S(1)} %shard_map.104.refs_0_), channel_id=1, source_target_pairs={{0,16},{8,24},{16,0},{24,8},{1,17},{9,25},{17,1},{25,9},{2,18},{10... | collective-permute-start | bytes 589832 | tf_op jit(solution)/shard_map/ppermute | solution.py:257
  20.3 7.7 %collective-permute-start.5 = (bf16[192,512]{1,0:T(8,128)(2,1)S(1)}, bf16[192,512]{1,0:T(8,128)(2,1)S(1)}, u32[]{:S(2)}, u32[]{:S(2)}) collective-permute-start(bf16[192,512]{1,0:T(8,128)(2,1)S(1)} %shard_map.104.refs_0_), channel_id=1, source_target_pairs={{0,8},{8,0},{16,24},{24,16},{1,9},{9,1},{17,25},{25,17},{2,10},{10... | collective-permute-start | bytes 589832 | tf_op jit(solution)/shard_map/ppermute | solution.py:257
  22.3 7.4 %collective-permute-start.12 = (bf16[80,512]{1,0:T(8,128)(2,1)S(1)}, bf16[80,512]{1,0:T(8,128)(2,1)S(1)}, u32[]{:S(2)}, u32[]{:S(2)}) collective-permute-start(bf16[80,512]{1,0:T(8,128)(2,1)S(1)} %shard_map.106.refs_0_), channel_id=1, source_target_pairs={{0,24},{8,16},{16,8},{24,0},{1,25},{9,17},{17,9},{25,1},{2,26},{10... | collective-permute-start | bytes 245768 | tf_op jit(solution)/shard_map/ppermute | solution.py:257
  23.1 7.4 %collective-permute-start.11 = (bf16[80,512]{1,0:T(8,128)(2,1)S(1)}, bf16[80,512]{1,0:T(8,128)(2,1)S(1)}, u32[]{:S(2)}, u32[]{:S(2)}) collective-permute-start(bf16[80,512]{1,0:T(8,128)(2,1)S(1)} %shard_map.106.refs_0_), channel_id=1, source_target_pairs={{0,16},{8,24},{16,0},{24,8},{1,17},{9,25},{17,1},{25,9},{2,18},{10... | collective-permute-start | bytes 245768 | tf_op jit(solution)/shard_map/ppermute | solution.py:257
  24.4 6.5 %collective-permute-start.10 = (bf16[80,512]{1,0:T(8,128)(2,1)S(1)}, bf16[80,512]{1,0:T(8,128)(2,1)S(1)}, u32[]{:S(2)}, u32[]{:S(2)}) collective-permute-start(bf16[80,512]{1,0:T(8,128)(2,1)S(1)} %shard_map.106.refs_0_), channel_id=1, source_target_pairs={{0,8},{8,0},{16,24},{24,16},{1,9},{9,1},{17,25},{25,17},{2,10},{10... | collective-permute-start | bytes 245768 | tf_op jit(solution)/shard_map/ppermute | solution.py:257
  33.7 2.0 %collective-permute-start.13 = (bf16[128,2048]{1,0:T(8,128)(2,1)S(1)}, bf16[128,2048]{1,0:T(8,128)(2,1)S(1)}, u32[]{:S(2)}, u32[]{:S(2)}) collective-permute-start(bf16[128,2048]{1,0:T(8,128)(2,1)S(1)} %get-tuple-element.39), channel_id=1, source_target_pairs={{0,1},{1,0},{2,3},{3,2},{4,5},{5,4},{6,7},{7,6},{8,9},{9,8},{10,11... | collective-permute-start | bytes 1572872 | tf_op jit(solution)/shard_map/ppermute | solution.py:254
  35.8 14.1 %copy-start.5 = (bf16[1,32,2048]{2,1,0:T(8,128)(2,1)S(1)}, bf16[1,32,2048]{2,1,0:T(8,128)(2,1)}, u32[]{:S(2)}) copy-start(bf16[1,32,2048]{2,1,0:T(8,128)(2,1)} %param.8) | copy-start | bytes 393220
  35.8 14.1 %copy-start.6 = (f32[1,2048]{1,0:T(1,128)S(1)}, f32[1,2048]{1,0:T(1,128)}, u32[]{:S(2)}) copy-start(f32[1,2048]{1,0:T(1,128)} %param.13) | copy-start | bytes 24580
  35.9 5.6 %collective-permute-start.14 = (bf16[32,2048]{1,0:T(8,128)(2,1)S(1)}, bf16[32,2048]{1,0:T(8,128)(2,1)S(1)}, u32[]{:S(2)}, u32[]{:S(2)}) collective-permute-start(bf16[32,2048]{1,0:T(8,128)(2,1)S(1)} %get-tuple-element.70), channel_id=1, source_target_pairs={{0,2},{1,3},{2,0},{3,1},{4,6},{5,7},{6,4},{7,5},{8,10},{9,11},{10,... | collective-permute-start | bytes 393224 | tf_op jit(solution)/shard_map/ppermute | solution.py:254
  41.5 8.4 %collective-permute-start.15 = (bf16[32,2048]{1,0:T(8,128)(2,1)S(1)}, bf16[32,2048]{1,0:T(8,128)(2,1)S(1)}, u32[]{:S(2)}, u32[]{:S(2)}) collective-permute-start(bf16[32,2048]{1,0:T(8,128)(2,1)S(1)} %fusion), channel_id=1, source_target_pairs={{0,4},{1,5},{2,6},{3,7},{4,0},{5,1},{6,2},{7,3},{8,12},{9,13},{10,... | collective-permute-start | bytes 393224 | tf_op jit(solution)/shard_map/ppermute | solution.py:254
  42.5 7.4 %collective-permute-start.16 = (bf16[32,2048]{1,0:T(8,128)(2,1)S(1)}, bf16[32,2048]{1,0:T(8,128)(2,1)S(1)}, u32[]{:S(2)}, u32[]{:S(2)}) collective-permute-start(bf16[32,2048]{1,0:T(8,128)(2,1)S(1)} %get-tuple-element.40), channel_id=1, source_target_pairs={{0,2},{1,3},{2,0},{3,1},{4,6},{5,7},{6,4},{7,5},{8,10},{9,11},{10,... | collective-permute-start | bytes 393224 | tf_op jit(solution)/shard_map/ppermute | solution.py:254
  50.0 8.2 %collective-permute-start.18 = (bf16[32,2048]{1,0:T(8,128)(2,1)S(1)}, bf16[32,2048]{1,0:T(8,128)(2,1)S(1)}, u32[]{:S(2)}, u32[]{:S(2)}) collective-permute-start(bf16[32,2048]{1,0:T(8,128)(2,1)S(1)} %fusion.5.refs_0_), channel_id=1, source_target_pairs={{0,4},{1,5},{2,6},{3,7},{4,0},{5,1},{6,2},{7,3},{8,12},{9,13},{10,... | collective-permute-start | bytes 393224 | tf_op jit(solution)/shard_map/ppermute | solution.py:254
  50.6 7.8 %collective-permute-start.17 = (bf16[32,2048]{1,0:T(8,128)(2,1)S(1)}, bf16[32,2048]{1,0:T(8,128)(2,1)S(1)}, u32[]{:S(2)}, u32[]{:S(2)}) collective-permute-start(bf16[32,2048]{1,0:T(8,128)(2,1)S(1)} %fusion.5.refs_0_), channel_id=1, source_target_pairs={{0,2},{1,3},{2,0},{3,1},{4,6},{5,7},{6,4},{7,5},{8,10},{9,11},{10,... | collective-permute-start | bytes 393224 | tf_op jit(solution)/shard_map/ppermute | solution.py:254
  52.6 6.2 %collective-permute-start.19 = (bf16[32,2048]{1,0:T(8,128)(2,1)S(1)}, bf16[32,2048]{1,0:T(8,128)(2,1)S(1)}, u32[]{:S(2)}, u32[]{:S(2)}) collective-permute-start(bf16[32,2048]{1,0:T(8,128)(2,1)S(1)} %fusion.5.refs_0_), channel_id=1, source_target_pairs={{0,1},{1,0},{2,3},{3,2},{4,5},{5,4},{6,7},{7,6},{8,9},{9,8},{10,11... | collective-permute-start | bytes 393224 | tf_op jit(solution)/shard_map/ppermute | solution.py:254
  58.2 1.3 %collective-permute-start.21 = (bf16[32,2048]{1,0:T(8,128)(2,1)S(1)}, bf16[32,2048]{1,0:T(8,128)(2,1)S(1)}, u32[]{:S(2)}, u32[]{:S(2)}) collective-permute-start(bf16[32,2048]{1,0:T(8,128)(2,1)S(1)} %collective-permute-done.18.refs_2_), channel_id=1, source_target_pairs={{0,1},{1,0},{2,3},{3,2},{4,5},{5,4},{6,7},{7,6},{8,9},{9,8},{10,11... | collective-permute-start | bytes 393224 | tf_op jit(solution)/shard_map/ppermute | solution.py:254
  58.4 1.3 %collective-permute-start.20 = (bf16[32,2048]{1,0:T(8,128)(2,1)S(1)}, bf16[32,2048]{1,0:T(8,128)(2,1)S(1)}, u32[]{:S(2)}, u32[]{:S(2)}) collective-permute-start(bf16[32,2048]{1,0:T(8,128)(2,1)S(1)} %collective-permute-done.17.refs_1_), channel_id=1, source_target_pairs={{0,1},{1,0},{2,3},{3,2},{4,5},{5,4},{6,7},{7,6},{8,9},{9,8},{10,11... | collective-permute-start | bytes 393224 | tf_op jit(solution)/shard_map/ppermute | solution.py:254
  58.7 5.6 %collective-permute-start.25 = (bf16[32,2048]{1,0:T(8,128)(2,1)S(1)}, bf16[32,2048]{1,0:T(8,128)(2,1)S(1)}, u32[]{:S(2)}, u32[]{:S(2)}) collective-permute-start(bf16[32,2048]{1,0:T(8,128)(2,1)S(1)} %collective-permute-done.18.refs_2_), channel_id=1, source_target_pairs={{0,2},{1,3},{2,0},{3,1},{4,6},{5,7},{6,4},{7,5},{8,10},{9,11},{10,... | collective-permute-start | bytes 393224 | tf_op jit(solution)/shard_map/ppermute | solution.py:254
  62.7 9.4 %collective-permute-start.22 = (bf16[192,512]{1,0:T(8,128)(2,1)S(1)}, bf16[192,512]{1,0:T(8,128)(2,1)S(1)}, u32[]{:S(2)}, u32[]{:S(2)}) collective-permute-start(bf16[192,512]{1,0:T(8,128)(2,1)S(1)} %get-tuple-element.54), channel_id=1, source_target_pairs={{0,8},{8,0},{16,24},{24,16},{1,9},{9,1},{17,25},{25,17},{2,10},{10... | collective-permute-start | bytes 589832 | tf_op jit(solution)/shard_map/ppermute | solution.py:257
  64.3 3.0 %collective-permute-start.26 = (bf16[32,2048]{1,0:T(8,128)(2,1)S(1)}, bf16[32,2048]{1,0:T(8,128)(2,1)S(1)}, u32[]{:S(2)}, u32[]{:S(2)}) collective-permute-start(bf16[32,2048]{1,0:T(8,128)(2,1)S(1)} %collective-permute-done.25.refs_0_), channel_id=1, source_target_pairs={{0,1},{1,0},{2,3},{3,2},{4,5},{5,4},{6,7},{7,6},{8,9},{9,8},{10,11... | collective-permute-start | bytes 393224 | tf_op jit(solution)/shard_map/ppermute | solution.py:254
  64.4 14.7 %collective-permute-start.23 = (bf16[192,512]{1,0:T(8,128)(2,1)S(1)}, bf16[192,512]{1,0:T(8,128)(2,1)S(1)}, u32[]{:S(2)}, u32[]{:S(2)}) collective-permute-start(bf16[192,512]{1,0:T(8,128)(2,1)S(1)} %get-tuple-element.55), channel_id=1, source_target_pairs={{0,16},{8,24},{16,0},{24,8},{1,17},{9,25},{17,1},{25,9},{2,18},{10... | collective-permute-start | bytes 589832 | tf_op jit(solution)/shard_map/ppermute | solution.py:257
  65.9 13.2 %collective-permute-start.24 = (bf16[192,512]{1,0:T(8,128)(2,1)S(1)}, bf16[192,512]{1,0:T(8,128)(2,1)S(1)}, u32[]{:S(2)}, u32[]{:S(2)}) collective-permute-start(bf16[192,512]{1,0:T(8,128)(2,1)S(1)} %get-tuple-element.56), channel_id=1, source_target_pairs={{0,24},{8,16},{16,8},{24,0},{1,25},{9,17},{17,9},{25,1},{2,26},{10... | collective-permute-start | bytes 589832 | tf_op jit(solution)/shard_map/ppermute | solution.py:257
  70.0 9.0 %collective-permute-start.27 = (bf16[64,512]{1,0:T(8,128)(2,1)S(1)}, bf16[64,512]{1,0:T(8,128)(2,1)S(1)}, u32[]{:S(2)}, u32[]{:S(2)}) collective-permute-start(bf16[64,512]{1,0:T(8,128)(2,1)S(1)} %get-tuple-element.59), channel_id=1, source_target_pairs={{0,8},{8,0},{16,24},{24,16},{1,9},{9,1},{17,25},{25,17},{2,10},{10... | collective-permute-start | bytes 196616 | tf_op jit(solution)/shard_map/ppermute | solution.py:257
  70.6 8.5 %collective-permute-start.28 = (bf16[64,512]{1,0:T(8,128)(2,1)S(1)}, bf16[64,512]{1,0:T(8,128)(2,1)S(1)}, u32[]{:S(2)}, u32[]{:S(2)}) collective-permute-start(bf16[64,512]{1,0:T(8,128)(2,1)S(1)} %get-tuple-element.60), channel_id=1, source_target_pairs={{0,16},{8,24},{16,0},{24,8},{1,17},{9,25},{17,1},{25,9},{2,18},{10... | collective-permute-start | bytes 196616 | tf_op jit(solution)/shard_map/ppermute | solution.py:257
  72.1 7.0 %collective-permute-start.29 = (bf16[64,512]{1,0:T(8,128)(2,1)S(1)}, bf16[64,512]{1,0:T(8,128)(2,1)S(1)}, u32[]{:S(2)}, u32[]{:S(2)}) collective-permute-start(bf16[64,512]{1,0:T(8,128)(2,1)S(1)} %get-tuple-element.61), channel_id=1, source_target_pairs={{0,24},{8,16},{16,8},{24,0},{1,25},{9,17},{17,9},{25,1},{2,26},{10... | collective-permute-start | bytes 196616 | tf_op jit(solution)/shard_map/ppermute | solution.py:257

commit v3 on v2

--- a/solution.py
+++ b/solution.py
@@ -45,7 +45,7 @@
         order[pl.ds(index * height, height), :] = table[pl.ds(start, height), :].astype(BF16)
 
 
-def norm_kernel(weights, squares):
+def norm_kernel(weights, after, squares):
     layers, features, width = weights.shape
     target = lax.axis_index("layer")
     for source in range(layers):
@@ -72,7 +72,7 @@
 
 
 def encode_kernel(count, *refs):
-    pieces, (weight, bias, out, rows) = refs[:count], refs[count:]
+    pieces, (weight, bias, out, rows) = refs[:count][::-1], refs[count:]
     gather_rows(pieces, rows)
     value = jnp.dot(rows[...], weight[...], preferred_element_type=F32) + bias[...]
     out[...] = jnp.maximum(value, 0.0).astype(BF16)
@@ -94,7 +94,7 @@
 
 
 def sort_kernel(layers, order, *refs):
-    acts, out = refs[:layers], refs[layers]
+    acts, out = refs[:layers][::-1], refs[layers]
     target = lax.axis_index("layer")
     first, features = acts[0].shape
     for offset in range(layers):
@@ -103,8 +103,8 @@
 
 
 def decode_kernel(layers, last, columns, order_ref, first_sorted, *refs):
-    acts, weights = refs[:layers], refs[layers]
-    acts_out, keep, send, norms = refs[layers + 1 :]
+    acts, weights = refs[:layers][::-1], refs[layers]
+    acts_out, keep, send, far_keep, far_send, norms = refs[layers + 1 :]
     target = lax.axis_index("layer")
     features, width = weights.shape[1:]
     total_rows = order_ref.shape[0]
@@ -124,10 +124,10 @@
         lanes = pl.ds(part * columns, columns)
         block = weights[:, :, lanes].reshape(layers * features, columns)
         value = jnp.dot(acts_out[...], block, preferred_element_type=F32).astype(BF16)
-        keep[pl.ds(0, near), lanes] = value[:near]
-        send[pl.ds(0, near), lanes] = value[near:first]
-        keep[pl.ds(near, far), lanes] = value[first : first + far]
-        send[pl.ds(near, far), lanes] = value[first + far :]
+        keep[:, lanes] = value[:near]
+        send[:, lanes] = value[near:first]
+        far_keep[:, lanes] = value[first : first + far]
+        far_send[:, lanes] = value[first + far :]
     total = jnp.zeros((layers, features), F32)
     for offset in range(layers):
         value = acts[offset][pl.ds(last, acts[0].shape[0] - last), :].astype(F32)
@@ -137,23 +137,23 @@
 
 
 def order_kernel(count, *refs):
-    pieces, (order, out, rows) = refs[:count], refs[count:]
+    pieces, (order, weights, out, turned, rows) = refs[:count], refs[count:]
     gather_rows(pieces, rows)
     out[...] = lax.dot_general(
         rows[...], order[...], (((0,), (1,)), ((), ())), preferred_element_type=F32
     ).astype(BF16)
+    for source in range(weights.shape[0]):
+        turned[source] = weights[source].T
 
 
 def grad_kernel(layers, count, *refs):
-    pieces, weights = refs[:count], refs[count]
+    pieces, turned = refs[:count][::-1], refs[count]
     outs, rows = refs[count + 1 : count + 1 + layers], refs[count + 1 + layers]
     target = lax.axis_index("layer")
     gather_rows(pieces, rows)
     for offset in range(layers):
         source = target ^ offset
-        value = lax.dot_general(
-            rows[...], weights[source], (((1,), (1,)), ((), ())), preferred_element_type=F32
-        )
+        value = jnp.dot(rows[...], turned[source], preferred_element_type=F32)
         outs[offset][...] = jnp.where(source <= target, value, 0.0).astype(outs[offset].dtype)
 
 
@@ -194,7 +194,7 @@
 
 
 def encoder_grad_kernel(layers, loss_scale, tall, ordered, acts, norms, *refs):
-    main_parts, last_parts = refs[:layers], refs[layers : 2 * layers]
+    main_parts, last_parts = refs[:layers][::-1], refs[layers : 2 * layers][::-1]
     out, sums_out, low, slots, sems = refs[2 * layers :]
     target = lax.axis_index("layer")
     features = main_parts[0].shape[1]
@@ -256,9 +256,15 @@
     def swap_layer(value, step):
         return lax.ppermute(value, "layer", [(i, i ^ step) for i in range(layers)])
 
+    def exchange(parts):
+        arrived = list(parts)
+        for step in reversed(range(1, layers)):
+            arrived[step] = swap_layer(parts[step], step)
+        return arrived
+
     def gather_lines(own, before=()):
         lane = {0: own}
-        for line in sorted(range(1, lines), key=lambda j: (bin(j).count("1"), j)):
+        for line in sorted(range(1, lines), key=lambda j: (bin(j).count("1"), -j)):
             low = line & -line
             lane[line] = swap_tok(lane[line ^ low], 2 * low)
         here, *_ = lax.optimization_barrier((own, *before)) if before else (own,)
@@ -284,16 +290,7 @@
         4 * row_total * row_total,
     )(row_order[None])
 
-    squares = call(
-        norm_kernel,
-        struct((layers, features), F32),
-        whole(1),
-        whole(1)[0],
-        [],
-        4 * layers * features * width,
-        2 * layers * features * width,
-    )(weights)
-    main_inputs, last_inputs = gather_lines(layer_inputs[0], (order, squares))
+    main_inputs, last_inputs = gather_lines(layer_inputs[0], (order,))
     encode_operands = (encoder_weight[0], encoder_bias)
     main_own = call(
         functools.partial(encode_kernel, len(main_inputs)),
@@ -303,8 +300,17 @@
         [pltpu.VMEM((first, width), BF16)],
         2 * first * width * features,
         2 * width * features,
-    )(*main_inputs, *encode_operands)
-    main_acts = [main_own] + [swap_layer(main_own, step) for step in range(1, layers)]
+    )(*main_inputs[::-1], *encode_operands)
+    main_acts = exchange([main_own] * layers)
+    squares = call(
+        norm_kernel,
+        struct((layers, features), F32),
+        whole(2),
+        whole(1)[0],
+        [],
+        4 * layers * features * width,
+        2 * layers * features * width,
+    )(weights, main_own)
     last_inputs = other_core(last_inputs, main_own)
     extra = -(-3 * layers // 16) * 16
     last_own = call(
@@ -316,7 +322,7 @@
         2 * last * width * features,
         2 * width * features,
     )(*last_inputs, *encode_operands, squares)
-    last_acts = [last_own] + [swap_layer(last_own, step) for step in range(1, layers)]
+    last_acts = exchange([last_own] * layers)
     first_sorted = call(
         functools.partial(sort_kernel, layers),
         struct((row_total, layers * features), F32),
@@ -325,26 +331,27 @@
         [],
         2 * row_total * first * layers * features,
         2 * first * layers * features,
-    )(order, *main_acts)
+    )(order, *main_acts[::-1])
 
     columns = min(512, width)
-    acts_all, keep, send, norms = call(
+    acts_all, keep, send, far_keep, far_send, norms = call(
         functools.partial(decode_kernel, layers, last, columns),
         (
             struct((row_total, layers * features), BF16),
-            struct((row_total // 2, width), BF16),
-            struct((row_total // 2, width), BF16),
+            *[struct((first // 2, width), BF16)] * 2,
+            *[struct((last // 2, width), BF16)] * 2,
             struct((layers, features), F32),
         ),
         whole(3 + layers),
-        tuple(whole(4)),
+        tuple(whole(6)),
         [],
         layers * block_flops,
         2 * layers * features * width,
-    )(order, first_sorted, *last_acts, weights)
-
-    pair = keep.astype(F32) + swap_tok(send, 1).astype(F32)
-    parts = [pair[i * height : (i + 1) * height] for i in range(lines)]
+    )(order, first_sorted, *last_acts[::-1], weights)
+
+    far = far_keep.astype(F32) + swap_tok(far_send, 1).astype(F32)
+    near = keep.astype(F32) + swap_tok(send, 1).astype(F32)
+    parts = [near[i * height : (i + 1) * height] for i in range(lines - 1)] + [far]
     last_leaf = None
     for line in reversed(range(1, lines)):
         low = line & -line
@@ -360,16 +367,18 @@
     ) * loss_scale
 
     _, *late = lax.optimization_barrier((send, *main_inputs, *last_inputs))
-    ordered = call(
+    ordered, turned = call(
         functools.partial(order_kernel, len(late)),
-        struct((width, row_total), BF16),
-        whole(len(late) + 1),
-        whole(1)[0],
+        (struct((width, row_total), BF16), struct((layers, width, features), BF16)),
+        whole(len(late) + 2),
+        tuple(whole(2)),
         [pltpu.VMEM((row_total, width), BF16)],
         2 * row_total * row_total * width,
-        4 * row_total * width,
-    )(*late, order)
-    resid_low, ordered = lax.optimization_barrier((resid_full.astype(BF16), ordered))
+        4 * layers * features * width,
+    )(*late, order, weights)
+    resid_low, ordered, turned = lax.optimization_barrier(
+        (resid_full.astype(BF16), ordered, turned)
+    )
     main_resid, last_resid = gather_lines(resid_low)
 
     def grad_acts(pieces):
@@ -385,9 +394,8 @@
             [],
             2 * count * layers * features * width,
             2 * layers * features * width,
-        )(*pieces, weights)
-        sums = [swap_layer(parts[step], step) if step else parts[0] for step in range(layers)]
-        return parts[0], sums, rows
+        )(*pieces[::-1], turned)
+        return parts[0], exchange(parts), rows
 
     main_grad, main_sums, main_rows = grad_acts(main_resid)
     last_resid = other_core(last_resid, main_grad)
@@ -421,7 +429,7 @@
         ],
         block_flops,
         2 * features * width,
-    )(ordered, acts_all, norms, *main_sums, *last_sums)
+    )(ordered, acts_all, norms, *main_sums[::-1], *last_sums[::-1])
     return (encoder_grad[None], feature_grad, decoder_grad[None], bias_grad)
 
 

time: 81.9 us -> 78.9 us (0.963)
  waiting for transfers between devices: 26.1 us -> 20.7 us
  starting transfers between devices: 30.1 us -> 35.2 us
  local copies, waits for them, and re-layouts: 3.98 us -> 1.83 us
    ppermute x18 -> x19, starting transfers between devices: 12.8 us -> 16.8 us  [swap_tok(): return lax.ppermute(value, 'tok', [(i, i ^ step) for i in range(ranks)])]
    ppermute x18 -> x19, waiting for transfers between devices: 21.5 us -> 18.1 us  [swap_tok(): return lax.ppermute(value, 'tok', [(i, i ^ step) for i in range(ranks)])]
    pallas_call x2, Pallas kernels: 5.55 us -> 3.37 us  [grad_acts(): call(functools.partial(grad_kernel, layers, len(pieces)), (*[struct((coun...]
    unnamed x14 -> x16, local copies, waits for them, and re-layouts: 3.96 us -> 1.81 us
    pallas_call x2, Pallas kernels: 2.41 us -> 4.4 us  [the longest x1 2.49 us: on_device(): call(functools.partial(order_kernel, len(late)), (struct((width, row_tota...]
    ppermute x12, waiting for transfers between devices: 4.59 us -> 2.67 us  [swap_layer(): return lax.ppermute(value, 'layer', [(i, i ^ step) for i in range(layers)])]
    ppermute x12, starting transfers between devices: 17.3 us -> 18.4 us  [swap_layer(): return lax.ppermute(value, 'layer', [(i, i ^ step) for i in range(layers)])]
  transfers between devices with their start and end apart: 30 -> 31, of which waited for: 16 -> 16; matrix products, arithmetic and copies ran while one was open for 0% -> 0% of each run, Pallas kernels for 18% -> 18%
where the time goes in v3:
time: 78.9 us; the launch traced here: 78.7 us
  starting transfers between devices  35.2 us (45%)
  waiting for transfers between devices  20.7 us (26%)
  Pallas kernels  19.8 us (25%)
  local copies, waits for them, and re-layouts  1.83 us (2%)
  between operations  1 us (1%)
    ppermute x12, starting transfers between devices, swap_layer(): return lax.ppermute(value, 'layer', [(i, i ^ step) for i in range(layers)])  18.4 us
    ppermute x19, waiting for transfers between devices, swap_tok(): return lax.ppermute(value, 'tok', [(i, i ^ step) for i in range(ranks)])  18.1 us
    ppermute x19, starting transfers between devices, swap_tok(): return lax.ppermute(value, 'tok', [(i, i ^ step) for i in range(ranks)])  16.8 us
    pallas_call x1, Pallas kernels, on_device(): call(functools.partial(decoder_grad_kernel, loss_scale), (struct((layers,...  5.14 us
    pallas_call x2, Pallas kernels, grad_acts(): call(functools.partial(grad_kernel, layers, len(pieces)), (*[struct((coun...  3.37 us
    pallas_call x1, Pallas kernels, on_device(): call(functools.partial(decode_kernel, layers, last, columns), (struct((ro...  2.77 us
    ppermute x12, waiting for transfers between devices, swap_layer(): return lax.ppermute(value, 'layer', [(i, i ^ step) for i in range(layers)])  2.67 us
    pallas_call x1, Pallas kernels, on_device(): call(functools.partial(order_kernel, len(late)), (struct((width, row_tota...  2.49 us
  transfers between devices with their start and end apart: 31, of which 16 were waited for; matrix products, arithmetic and copies ran while one was open for 0% of the time, Pallas kernels for 18%

profile of v3, /device:TPU:0, one launch (start us, length us, event | category | flops | bytes accessed | tf_op | source)
XLA Modules:
  0.0 78.7 jit_solution(18154409502605842272)
XLA Ops:
  0.6 4.1 %collective-permute-start = (bf16[32,2048]{1,0:T(8,128)(2,1)}, bf16[32,2048]{1,0:T(8,128)(2,1)S(1)}, u32[]{:S(2)}, u32[]{:S(2)}) collective-permute-start(bf16[32,2048]{1,0:T(8,128)(2,1)} %bitcast.18), channel_id=1, source_target_pairs={{0,4},{1,5},{2,6},{3,7},{4,0},{5,1},{6,2},{7,3},{8,12},{9,13},{10,... | collective-permute-start | bytes 393224 | tf_op jit(solution)/shard_map/ppermute | solution.py:254
  4.7 1.6 %collective-permute-start.2 = (bf16[32,2048]{1,0:T(8,128)(2,1)}, bf16[32,2048]{1,0:T(8,128)(2,1)S(1)}, u32[]{:S(2)}, u32[]{:S(2)}) collective-permute-start(bf16[32,2048]{1,0:T(8,128)(2,1)} %bitcast.19), channel_id=1, source_target_pairs={{0,2},{1,3},{2,0},{3,1},{4,6},{5,7},{6,4},{7,5},{8,10},{9,11},{10,... | collective-permute-start | bytes 393224 | tf_op jit(solution)/shard_map/ppermute | solution.py:254
  6.3 0.8 %copy-done.3 = s32[256]{0:T(256)S(1)} copy-done((s32[256]{0:T(256)S(1)}, s32[256]{0:T(256)}, u32[]{:S(2)}) %copy-start.3) | copy-done | bytes 1048
  7.2 0.1 shard_map.102.order.order_ref.refs_8_
  7.3 1.0 %copy-done.1 = bf16[1,32,2048]{2,1,0:T(8,128)(2,1)S(1)} copy-done((bf16[1,32,2048]{2,1,0:T(8,128)(2,1)S(1)}, bf16[1,32,2048]{2,1,0:T(8,128)(2,1)}, u32[]{:S(2)}) %copy-start.1) | copy-done | bytes 131096
  8.2 0.0 collective-permute-start.4
  8.2 3.1 %collective-permute-done.refs_3_.refs_2_ = bf16[32,2048]{1,0:T(8,128)(2,1)S(1)} collective-permute-done((bf16[32,2048]{1,0:T(8,128)(2,1)}, bf16[32,2048]{1,0:T(8,128)(2,1)S(1)}, u32[]{:S(2)}, u32[]{:S(2)}) %collective-permute-start) | collective-permute-done | bytes 131104 | tf_op jit(solution)/shard_map/ppermute | solution.py:254
  11.4 0.2 collective-permute-done.2.refs_4_.refs_1_
  11.6 0.3 collective-permute-start.3
  11.9 1.1 %collective-permute-start.8 = (bf16[32,2048]{1,0:T(8,128)(2,1)S(1)}, bf16[32,2048]{1,0:T(8,128)(2,1)S(1)}, u32[]{:S(2)}, u32[]{:S(2)}) collective-permute-start(bf16[32,2048]{1,0:T(8,128)(2,1)S(1)} %collective-permute-done.refs_3_.refs_2_), channel_id=1, source_target_pairs={{0,2},{1,3},{2,0},{3,1},{4,6},{5,7},{6,4},{7,5},{8,10},{9,11},{10,... | collective-permute-start | bytes 393224 | tf_op jit(solution)/shard_map/ppermute | solution.py:254
  13.0 0.0 collective-permute-done.4.refs_2_.refs_3_
  13.0 0.0 collective-permute-done.1.refs_0_.refs_5_
  13.0 0.6 shard_map.103.refs_3_.after
  13.6 2.5 %collective-permute-start.5 = (bf16[192,512]{1,0:T(8,128)(2,1)S(1)}, bf16[192,512]{1,0:T(8,128)(2,1)S(1)}, u32[]{:S(2)}, u32[]{:S(2)}) collective-permute-start(bf16[192,512]{1,0:T(8,128)(2,1)S(1)} %shard_map.103.refs_3_.after), channel_id=1, source_target_pairs={{0,24},{8,16},{16,8},{24,0},{1,25},{9,17},{17,9},{25,1},{2,26},{10... | collective-permute-start | bytes 589832 | tf_op jit(solution)/shard_map/ppermute | solution.py:257
  16.1 1.3 %collective-permute-done.8.refs_0_.refs_6_ = bf16[32,2048]{1,0:T(8,128)(2,1)S(1)} collective-permute-done((bf16[32,2048]{1,0:T(8,128)(2,1)S(1)}, bf16[32,2048]{1,0:T(8,128)(2,1)S(1)}, u32[]{:S(2)}, u32[]{:S(2)}) %collective-permute-start.8) | collective-permute-done | bytes 131104 | tf_op jit(solution)/shard_map/ppermute | solution.py:254
  17.5 1.6 %collective-permute-start.6 = (bf16[192,512]{1,0:T(8,128)(2,1)S(1)}, bf16[192,512]{1,0:T(8,128)(2,1)S(1)}, u32[]{:S(2)}, u32[]{:S(2)}) collective-permute-start(bf16[192,512]{1,0:T(8,128)(2,1)S(1)} %shard_map.103.refs_3_.after), channel_id=1, source_target_pairs={{0,16},{8,24},{16,0},{24,8},{1,17},{9,25},{17,1},{25,9},{2,18},{10... | collective-permute-start | bytes 589832 | tf_op jit(solution)/shard_map/ppermute | solution.py:257
  19.0 1.5 %collective-permute-start.7 = (bf16[192,512]{1,0:T(8,128)(2,1)S(1)}, bf16[192,512]{1,0:T(8,128)(2,1)S(1)}, u32[]{:S(2)}, u32[]{:S(2)}) collective-permute-start(bf16[192,512]{1,0:T(8,128)(2,1)S(1)} %shard_map.103.refs_3_.after), channel_id=1, source_target_pairs={{0,8},{8,0},{16,24},{24,16},{1,9},{9,1},{17,25},{25,17},{2,10},{10... | collective-permute-start | bytes 589832 | tf_op jit(solution)/shard_map/ppermute | solution.py:257
  20.5 1.9 %shard_map.105.refs_4_ = f32[4,512]{1,0:T(4,128)S(1)} custom-call(bf16[4,512,2048]{2,1,0:T(8,128)(2,1)S(1)} %bitcast.12, bf16[192,512]{1,0:T(8,128)(2,1)S(1)} %shard_map.103.refs_3_.after), custom_call_target="tpu_custom_call" | custom-call | flops 16777216 | bytes 8388608 | tf_op jit(solution)/shard_map/pallas_call | solution.py:305
  22.5 0.0 collective-permute-done.9.refs_1_.refs_7_
  22.5 0.5 shard_map.106.refs_3_
  23.0 0.5 collective-permute-start.10
  23.5 1.6 %collective-permute-start.11 = (bf16[80,512]{1,0:T(8,128)(2,1)S(1)}, bf16[80,512]{1,0:T(8,128)(2,1)S(1)}, u32[]{:S(2)}, u32[]{:S(2)}) collective-permute-start(bf16[80,512]{1,0:T(8,128)(2,1)S(1)} %shard_map.106.refs_3_), channel_id=1, source_target_pairs={{0,16},{8,24},{16,0},{24,8},{1,17},{9,25},{17,1},{25,9},{2,18},{10... | collective-permute-start | bytes 245768 | tf_op jit(solution)/shard_map/ppermute | solution.py:257
  25.0 1.5 %collective-permute-start.12 = (bf16[80,512]{1,0:T(8,128)(2,1)S(1)}, bf16[80,512]{1,0:T(8,128)(2,1)S(1)}, u32[]{:S(2)}, u32[]{:S(2)}) collective-permute-start(bf16[80,512]{1,0:T(8,128)(2,1)S(1)} %shard_map.106.refs_3_), channel_id=1, source_target_pairs={{0,8},{8,0},{16,24},{24,16},{1,9},{9,1},{17,25},{25,17},{2,10},{10... | collective-permute-start | bytes 245768 | tf_op jit(solution)/shard_map/ppermute | solution.py:257
  26.5 0.0 collective-permute-done.6.refs_1_
  26.5 0.1 collective-permute-done.7.refs_2_
  26.6 0.4 shard_map.104.first_sorted
  27.0 2.1 %collective-permute-done.10.refs_0_ = bf16[80,512]{1,0:T(8,128)(2,1)S(1)} collective-permute-done((bf16[80,512]{1,0:T(8,128)(2,1)S(1)}, bf16[80,512]{1,0:T(8,128)(2,1)S(1)}, u32[]{:S(2)}, u32[]{:S(2)}) %collective-permute-start.10) | collective-permute-done | bytes 81952 | tf_op jit(solution)/shard_map/ppermute | solution.py:257
  29.1 0.2 collective-permute-done.11.refs_1_
  29.4 0.2 collective-permute-done.12.refs_2_
  29.6 2.8 %shard_map.107 = (bf16[256,2048]{1,0:T(8,128)(2,1)S(1)}, bf16[96,2048]{1,0:T(8,128)(2,1)S(1)}, bf16[96,2048]{1,0:T(8,128)(2,1)S(1)}, bf16[32,2048]{1,0:T(8,128)(...) custom-call(bf16[256,256]{1,0:T(8,128)(2,1)S(1)} %shard_map.102.order.order_ref.refs_8_, ...), custom_call_target="tpu_custom_call" | custom-call | flops 2147483648 | bytes 8388608 | tf_op jit(solution)/shard_map/pallas_call | solution.py:337
  32.4 0.0 copy-start.4
  32.4 0.0 copy-start.5
  32.4 0.1 collective-permute-start.14
  32.5 0.5 collective-permute-start.13
  33.0 0.8 %collective-permute-done.14 = bf16[32,2048]{1,0:T(8,128)(2,1)S(1)} collective-permute-done((bf16[32,2048]{1,0:T(8,128)(2,1)S(1)}, bf16[32,2048]{1,0:T(8,128)(2,1)S(1)}, u32[]{:S(2)}, u32[]{:S(2)}) %collective-permute-start.14) | collective-permute-done | bytes 131104 | tf_op jit(solution)/shard_map/ppermute | solution.py:254
  33.8 1.5 %collective-permute-start.15 = (bf16[32,2048]{1,0:T(8,128)(2,1)S(1)}, bf16[32,2048]{1,0:T(8,128)(2,1)S(1)}, u32[]{:S(2)}, u32[]{:S(2)}) collective-permute-start(bf16[32,2048]{1,0:T(8,128)(2,1)S(1)} %add_convert_fusion), channel_id=1, source_target_pairs={{0,2},{1,3},{2,0},{3,1},{4,6},{5,7},{6,4},{7,5},{8,10},{9,11},{10,... | collective-permute-start | bytes 393224 | tf_op jit(solution)/shard_map/ppermute | solution.py:254
  35.3 0.0 collective-permute-done.13
  35.3 0.1 convert_add_fusion
  35.4 4.0 %collective-permute-done.15 = bf16[32,2048]{1,0:T(8,128)(2,1)S(1)} collective-permute-done((bf16[32,2048]{1,0:T(8,128)(2,1)S(1)}, bf16[32,2048]{1,0:T(8,128)(2,1)S(1)}, u32[]{:S(2)}, u32[]{:S(2)}) %collective-permute-start.15) | collective-permute-done | bytes 131104 | tf_op jit(solution)/shard_map/ppermute | solution.py:254
  39.5 1.4 %collective-permute-start.17 = (bf16[32,2048]{1,0:T(8,128)(2,1)S(1)}, bf16[32,2048]{1,0:T(8,128)(2,1)S(1)}, u32[]{:S(2)}, u32[]{:S(2)}) collective-permute-start(bf16[32,2048]{1,0:T(8,128)(2,1)S(1)} %slice.31), channel_id=1, source_target_pairs={{0,2},{1,3},{2,0},{3,1},{4,6},{5,7},{6,4},{7,5},{8,10},{9,11},{10,... | collective-permute-start | bytes 393224 | tf_op jit(solution)/shard_map/ppermute | solution.py:254
  40.9 2.5 %collective-permute-start.16 = (bf16[32,2048]{1,0:T(8,128)(2,1)S(1)}, bf16[32,2048]{1,0:T(8,128)(2,1)S(1)}, u32[]{:S(2)}, u32[]{:S(2)}) collective-permute-start(bf16[32,2048]{1,0:T(8,128)(2,1)S(1)} %fusion), channel_id=1, source_target_pairs={{0,4},{1,5},{2,6},{3,7},{4,0},{5,1},{6,2},{7,3},{8,12},{9,13},{10,... | collective-permute-start | bytes 393224 | tf_op jit(solution)/shard_map/ppermute | solution.py:254
  43.4 2.5 %shard_map.108 = (bf16[2048,256]{1,0:T(8,128)(2,1)S(1)}, bf16[4,2048,512]{2,1,0:T(8,128)(2,1)S(1)}) custom-call(bf16[32,2048]{1,0:T(8,128)(2,1)S(1)} %bitcast.22, bf16[32,2048]{1,0:T(8,128)(2,1)S(1)} %collective-permute-done.2.refs_4_.refs_1_, bf16[32,2048]{1,0:T(8,128)(2,1)S(1)} %collective-permute-done.refs_3_.refs_2_, ...), custom_call_target="tpu_custom_call" | custom-call | flops 268435456 | bytes 16777216 | tf_op jit(solution)/shard_map/pallas_call | solution.py:370
  45.9 0.1 collective-permute-done.17
  46.0 3.1 %collective-permute-done.16 = bf16[32,2048]{1,0:T(8,128)(2,1)S(1)} collective-permute-done((bf16[32,2048]{1,0:T(8,128)(2,1)S(1)}, bf16[32,2048]{1,0:T(8,128)(2,1)S(1)}, u32[]{:S(2)}, u32[]{:S(2)}) %collective-permute-start.16) | collective-permute-done | bytes 131104 | tf_op jit(solution)/shard_map/ppermute | solution.py:254
  49.1 0.1 fusion.5.refs_5_
  49.2 0.5 collective-permute-start.18
  49.7 2.6 %collective-permute-start.20 = (bf16[32,2048]{1,0:T(8,128)(2,1)S(1)}, bf16[32,2048]{1,0:T(8,128)(2,1)S(1)}, u32[]{:S(2)}, u32[]{:S(2)}) collective-permute-start(bf16[32,2048]{1,0:T(8,128)(2,1)S(1)} %fusion.5.refs_5_), channel_id=1, source_target_pairs={{0,2},{1,3},{2,0},{3,1},{4,6},{5,7},{6,4},{7,5},{8,10},{9,11},{10,... | collective-permute-start | bytes 393224 | tf_op jit(solution)/shard_map/ppermute | solution.py:254
  52.3 3.9 %collective-permute-done.18.refs_3_ = bf16[32,2048]{1,0:T(8,128)(2,1)S(1)} collective-permute-done((bf16[32,2048]{1,0:T(8,128)(2,1)S(1)}, bf16[32,2048]{1,0:T(8,128)(2,1)S(1)}, u32[]{:S(2)}, u32[]{:S(2)}) %collective-permute-start.18) | collective-permute-done | bytes 131104 | tf_op jit(solution)/shard_map/ppermute | solution.py:254
  56.2 0.4 collective-permute-done.20.refs_4_
  56.7 0.1 collective-permute-start.21
  56.7 0.6 collective-permute-start.26
  57.3 0.3 collective-permute-done.19.refs_0_
  57.6 0.4 collective-permute-done.21.refs_1_
  58.0 1.8 %shard_map.109 = (f32[192,512]{1,0:T(8,128)S(1)}, bf16[192,512]{1,0:T(8,128)(2,1)S(1)}, bf16[192,512]{1,0:T(8,128)(2,1)S(1)}, bf16[192,512]{1,0:T(8,128)(2,1)S(1)}, bf16[192,2048]{1,0:T(8,128)(2,1)S(1)}) custom-call(bf16[32,2048]{1,0:T(8,128)(2,1)S(1)} %collective-permute-done.19.refs_0_, bf16[32,2048]{1,0:T(8,128)(2,1)S(1)} %collective-permute-done.21.refs_1_, ...), custom_call_target="tpu_custom_call" | custom-call | flops 1610612736 | bytes 8388608 | tf_op jit(solution)/shard_map/pallas_call | solution.py:386
  59.8 2.5 %collective-permute-start.23 = (bf16[192,512]{1,0:T(8,128)(2,1)S(1)}, bf16[192,512]{1,0:T(8,128)(2,1)S(1)}, u32[]{:S(2)}, u32[]{:S(2)}) collective-permute-start(bf16[192,512]{1,0:T(8,128)(2,1)S(1)} %get-tuple-element.63), channel_id=1, source_target_pairs={{0,24},{8,16},{16,8},{24,0},{1,25},{9,17},{17,9},{25,1},{2,26},{10... | collective-permute-start | bytes 589832 | tf_op jit(solution)/shard_map/ppermute | solution.py:257
  62.4 0.2 collective-permute-done.26.refs_1_
  62.6 1.5 %collective-permute-start.24 = (bf16[192,512]{1,0:T(8,128)(2,1)S(1)}, bf16[192,512]{1,0:T(8,128)(2,1)S(1)}, u32[]{:S(2)}, u32[]{:S(2)}) collective-permute-start(bf16[192,512]{1,0:T(8,128)(2,1)S(1)} %get-tuple-element.64), channel_id=1, source_target_pairs={{0,16},{8,24},{16,0},{24,8},{1,17},{9,25},{17,1},{25,9},{2,18},{10... | collective-permute-start | bytes 589832 | tf_op jit(solution)/shard_map/ppermute | solution.py:257
  64.1 1.5 %collective-permute-start.25 = (bf16[192,512]{1,0:T(8,128)(2,1)S(1)}, bf16[192,512]{1,0:T(8,128)(2,1)S(1)}, u32[]{:S(2)}, u32[]{:S(2)}) collective-permute-start(bf16[192,512]{1,0:T(8,128)(2,1)S(1)} %get-tuple-element.65), channel_id=1, source_target_pairs={{0,8},{8,0},{16,24},{24,16},{1,9},{9,1},{17,25},{25,17},{2,10},{10... | collective-permute-start | bytes 589832 | tf_op jit(solution)/shard_map/ppermute | solution.py:257
  65.6 1.6 %shard_map.110 = (f32[64,512]{1,0:T(8,128)S(1)}, bf16[64,512]{1,0:T(8,128)(2,1)S(1)}, bf16[64,512]{1,0:T(8,128)(2,1)S(1)}, bf16[64,512]{1,0:T(8,128)(2,1)S(1)}, bf16[64,2048]{1,0:T(8,128)(2,1)S(1)}) custom-call(bf16[32,2048]{1,0:T(8,128)(2,1)S(1)} %collective-permute-done.27.refs_0_, bf16[32,2048]{1,0:T(8,128)(2,1)S(1)} %collective-permute-done.26.refs_1_, ...), custom_call_target="tpu_custom_call" | custom-call | flops 536870912 | bytes 8388608 | tf_op jit(solution)/shard_map/pallas_call | solution.py:386
  67.2 1.0 %collective-permute-start.28 = (bf16[64,512]{1,0:T(8,128)(2,1)S(1)}, bf16[64,512]{1,0:T(8,128)(2,1)S(1)}, u32[]{:S(2)}, u32[]{:S(2)}) collective-permute-start(bf16[64,512]{1,0:T(8,128)(2,1)S(1)} %get-tuple-element.68), channel_id=1, source_target_pairs={{0,24},{8,16},{16,8},{24,0},{1,25},{9,17},{17,9},{25,1},{2,26},{10... | collective-permute-start | bytes 196616 | tf_op jit(solution)/shard_map/ppermute | solution.py:257
  68.2 1.2 %collective-permute-start.29 = (bf16[64,512]{1,0:T(8,128)(2,1)S(1)}, bf16[64,512]{1,0:T(8,128)(2,1)S(1)}, u32[]{:S(2)}, u32[]{:S(2)}) collective-permute-start(bf16[64,512]{1,0:T(8,128)(2,1)S(1)} %get-tuple-element.69), channel_id=1, source_target_pairs={{0,16},{8,24},{16,0},{24,8},{1,17},{9,25},{17,1},{25,9},{2,18},{10... | collective-permute-start | bytes 196616 | tf_op jit(solution)/shard_map/ppermute | solution.py:257
  69.4 1.5 %collective-permute-start.30 = (bf16[64,512]{1,0:T(8,128)(2,1)S(1)}, bf16[64,512]{1,0:T(8,128)(2,1)S(1)}, u32[]{:S(2)}, u32[]{:S(2)}) collective-permute-start(bf16[64,512]{1,0:T(8,128)(2,1)S(1)} %get-tuple-element.70), channel_id=1, source_target_pairs={{0,8},{8,0},{16,24},{24,16},{1,9},{9,1},{17,25},{25,17},{2,10},{10... | collective-permute-start | bytes 196616 | tf_op jit(solution)/shard_map/ppermute | solution.py:257
  70.9 5.1 %shard_map.112 = (bf16[4,512,2048]{2,1,0:T(8,128)(2,1)}, f32[1,2048]{1,0:T(1,128)}) custom-call(bf16[256,2048]{1,0:T(8,128)(2,1)S(1)} %get-tuple-element.59.acts, f32[4,512]{1,0:T(4,128)S(1)} %get-tuple-element.60.norms, bf16[192,2048]{1,0:T(8,128)(2,1)S(1)} %get-tuple-element.74.main_rows, bf16[64,2048]{1,0:T(8,128)(2,1)S(1)} %get-tuple-element.75.last_rows, ...), custom_call_target="tpu_custom_call" | custom-call | flops 2147483648 | bytes 16777216 | tf_op jit(solution)/shard_map/pallas_call | solution.py:405
  76.1 2.4 %shard_map.111 = (bf16[2048,512]{1,0:T(8,128)(2,1)}, f32[1,512]{1,0:T(1,128)}) custom-call(bf16[2048,256]{1,0:T(8,128)(2,1)S(1)} %get-tuple-element.58.ordered, bf16[256,2048]{1,0:T(8,128)(2,1)S(1)} %get-tuple-element.59.acts, f32[4,512]{1,0:T(4,128)S(1)} %get-tuple-element.60.norms, bf16[192,512]{1,0:T(8,128)(2,1)S(1)} %collective-permute-done.23.refs_0_, ...), custom_call_target="tpu_custom_call" | custom-call | flops 536870912 | bytes 2097152 | tf_op jit(solution)/shard_map/pallas_call | solution.py:420
  (31 shorter events, 0.1 us)
Async XLA Ops:
  0.6 10.7 %collective-permute-start = (bf16[32,2048]{1,0:T(8,128)(2,1)}, bf16[32,2048]{1,0:T(8,128)(2,1)S(1)}, u32[]{:S(2)}, u32[]{:S(2)}) collective-permute-start(bf16[32,2048]{1,0:T(8,128)(2,1)} %bitcast.18), channel_id=1, source_target_pairs={{0,4},{1,5},{2,6},{3,7},{4,0},{5,1},{6,2},{7,3},{8,12},{9,13},{10,... | collective-permute-start | bytes 393224 | tf_op jit(solution)/shard_map/ppermute | solution.py:254
  4.7 6.8 %collective-permute-start.2 = (bf16[32,2048]{1,0:T(8,128)(2,1)}, bf16[32,2048]{1,0:T(8,128)(2,1)S(1)}, u32[]{:S(2)}, u32[]{:S(2)}) collective-permute-start(bf16[32,2048]{1,0:T(8,128)(2,1)} %bitcast.19), channel_id=1, source_target_pairs={{0,2},{1,3},{2,0},{3,1},{4,6},{5,7},{6,4},{7,5},{8,10},{9,11},{10,... | collective-permute-start | bytes 393224 | tf_op jit(solution)/shard_map/ppermute | solution.py:254
  6.3 14.2 %slice-start = ((s8[8388608]{0:T(1024)(128)(4,1)}), s8[4194304]{0:T(1024)(128)(4,1)S(1)}, s32[]{:S(2)}) async-start(s8[8388608]{0:T(1024)(128)(4,1)} %bitcast.10), calls=%async_computation | async-start | bytes 8388608
  6.3 0.8 %copy-start.3 = (s32[256]{0:T(256)S(1)}, s32[256]{0:T(256)}, u32[]{:S(2)}) copy-start(s32[256]{0:T(256)} %param.9) | copy-start | bytes 3076
  7.1 1.1 %copy-start.1 = (bf16[1,32,2048]{2,1,0:T(8,128)(2,1)S(1)}, bf16[1,32,2048]{2,1,0:T(8,128)(2,1)}, u32[]{:S(2)}) copy-start(bf16[1,32,2048]{2,1,0:T(8,128)(2,1)} %param.7) | copy-start | bytes 393220
  7.1 5.9 %copy-start = (bf16[1,2048,512]{2,1,0:T(8,128)(2,1)S(1)}, bf16[1,2048,512]{2,1,0:T(8,128)(2,1)}, u32[]{:S(2)}) copy-start(bf16[1,2048,512]{2,1,0:T(8,128)(2,1)} %param.10) | copy-start | bytes 6291460
  7.1 5.9 %copy-start.2 = (f32[1,512]{1,0:T(1,128)S(1)}, f32[1,512]{1,0:T(1,128)}, u32[]{:S(2)}) copy-start(f32[1,512]{1,0:T(1,128)} %refs_3_.1) | copy-start | bytes 6148
  7.1 13.4 %slice-start.1 = ((s8[8388608]{0:T(1024)(128)(4,1)}), s8[4194304]{0:T(1024)(128)(4,1)S(1)}, s32[]{:S(2)}) async-start(s8[8388608]{0:T(1024)(128)(4,1)} %bitcast.10), calls=%async_computation.1 | async-start | bytes 8388608
  8.2 4.8 %collective-permute-start.4 = (bf16[32,2048]{1,0:T(8,128)(2,1)S(1)}, bf16[32,2048]{1,0:T(8,128)(2,1)S(1)}, u32[]{:S(2)}, u32[]{:S(2)}) collective-permute-start(bf16[32,2048]{1,0:T(8,128)(2,1)S(1)} %bitcast.20), channel_id=1, source_target_pairs={{0,1},{1,0},{2,3},{3,2},{4,5},{5,4},{6,7},{7,6},{8,9},{9,8},{10,11... | collective-permute-start | bytes 393224 | tf_op jit(solution)/shard_map/ppermute | solution.py:254
  11.4 1.6 %collective-permute-start.1 = (bf16[32,2048]{1,0:T(8,128)(2,1)S(1)}, bf16[32,2048]{1,0:T(8,128)(2,1)S(1)}, u32[]{:S(2)}, u32[]{:S(2)}) collective-permute-start(bf16[32,2048]{1,0:T(8,128)(2,1)S(1)} %collective-permute-done.refs_3_.refs_2_), channel_id=1, source_target_pairs={{0,1},{1,0},{2,3},{3,2},{4,5},{5,4},{6,7},{7,6},{8,9},{9,8},{10,11... | collective-permute-start | bytes 393224 | tf_op jit(solution)/shard_map/ppermute | solution.py:254
  11.6 1.4 %collective-permute-start.3 = (bf16[32,2048]{1,0:T(8,128)(2,1)S(1)}, bf16[32,2048]{1,0:T(8,128)(2,1)S(1)}, u32[]{:S(2)}, u32[]{:S(2)}) collective-permute-start(bf16[32,2048]{1,0:T(8,128)(2,1)S(1)} %collective-permute-done.2.refs_4_.refs_1_), channel_id=1, source_target_pairs={{0,1},{1,0},{2,3},{3,2},{4,5},{5,4},{6,7},{7,6},{8,9},{9,8},{10,11... | collective-permute-start | bytes 393224 | tf_op jit(solution)/shard_map/ppermute | solution.py:254
  11.9 5.6 %collective-permute-start.8 = (bf16[32,2048]{1,0:T(8,128)(2,1)S(1)}, bf16[32,2048]{1,0:T(8,128)(2,1)S(1)}, u32[]{:S(2)}, u32[]{:S(2)}) collective-permute-start(bf16[32,2048]{1,0:T(8,128)(2,1)S(1)} %collective-permute-done.refs_3_.refs_2_), channel_id=1, source_target_pairs={{0,2},{1,3},{2,0},{3,1},{4,6},{5,7},{6,4},{7,5},{8,10},{9,11},{10,... | collective-permute-start | bytes 393224 | tf_op jit(solution)/shard_map/ppermute | solution.py:254
  13.6 11.4 %collective-permute-start.5 = (bf16[192,512]{1,0:T(8,128)(2,1)S(1)}, bf16[192,512]{1,0:T(8,128)(2,1)S(1)}, u32[]{:S(2)}, u32[]{:S(2)}) collective-permute-start(bf16[192,512]{1,0:T(8,128)(2,1)S(1)} %shard_map.103.refs_3_.after), channel_id=1, source_target_pairs={{0,24},{8,16},{16,8},{24,0},{1,25},{9,17},{17,9},{25,1},{2,26},{10... | collective-permute-start | bytes 589832 | tf_op jit(solution)/shard_map/ppermute | solution.py:257
  17.5 5.0 %collective-permute-start.9 = (bf16[32,2048]{1,0:T(8,128)(2,1)S(1)}, bf16[32,2048]{1,0:T(8,128)(2,1)S(1)}, u32[]{:S(2)}, u32[]{:S(2)}) collective-permute-start(bf16[32,2048]{1,0:T(8,128)(2,1)S(1)} %collective-permute-done.8.refs_0_.refs_6_), channel_id=1, source_target_pairs={{0,1},{1,0},{2,3},{3,2},{4,5},{5,4},{6,7},{7,6},{8,9},{9,8},{10,11... | collective-permute-start | bytes 393224 | tf_op jit(solution)/shard_map/ppermute | solution.py:254
  17.5 9.0 %collective-permute-start.6 = (bf16[192,512]{1,0:T(8,128)(2,1)S(1)}, bf16[192,512]{1,0:T(8,128)(2,1)S(1)}, u32[]{:S(2)}, u32[]{:S(2)}) collective-permute-start(bf16[192,512]{1,0:T(8,128)(2,1)S(1)} %shard_map.103.refs_3_.after), channel_id=1, source_target_pairs={{0,16},{8,24},{16,0},{24,8},{1,17},{9,25},{17,1},{25,9},{2,18},{10... | collective-permute-start | bytes 589832 | tf_op jit(solution)/shard_map/ppermute | solution.py:257
  19.0 7.5 %collective-permute-start.7 = (bf16[192,512]{1,0:T(8,128)(2,1)S(1)}, bf16[192,512]{1,0:T(8,128)(2,1)S(1)}, u32[]{:S(2)}, u32[]{:S(2)}) collective-permute-start(bf16[192,512]{1,0:T(8,128)(2,1)S(1)} %shard_map.103.refs_3_.after), channel_id=1, source_target_pairs={{0,8},{8,0},{16,24},{24,16},{1,9},{9,1},{17,25},{25,17},{2,10},{10... | collective-permute-start | bytes 589832 | tf_op jit(solution)/shard_map/ppermute | solution.py:257
  23.0 6.2 %collective-permute-start.10 = (bf16[80,512]{1,0:T(8,128)(2,1)S(1)}, bf16[80,512]{1,0:T(8,128)(2,1)S(1)}, u32[]{:S(2)}, u32[]{:S(2)}) collective-permute-start(bf16[80,512]{1,0:T(8,128)(2,1)S(1)} %shard_map.106.refs_3_), channel_id=1, source_target_pairs={{0,24},{8,16},{16,8},{24,0},{1,25},{9,17},{17,9},{25,1},{2,26},{10... | collective-permute-start | bytes 245768 | tf_op jit(solution)/shard_map/ppermute | solution.py:257
  23.5 5.9 %collective-permute-start.11 = (bf16[80,512]{1,0:T(8,128)(2,1)S(1)}, bf16[80,512]{1,0:T(8,128)(2,1)S(1)}, u32[]{:S(2)}, u32[]{:S(2)}) collective-permute-start(bf16[80,512]{1,0:T(8,128)(2,1)S(1)} %shard_map.106.refs_3_), channel_id=1, source_target_pairs={{0,16},{8,24},{16,0},{24,8},{1,17},{9,25},{17,1},{25,9},{2,18},{10... | collective-permute-start | bytes 245768 | tf_op jit(solution)/shard_map/ppermute | solution.py:257
  25.0 4.6 %collective-permute-start.12 = (bf16[80,512]{1,0:T(8,128)(2,1)S(1)}, bf16[80,512]{1,0:T(8,128)(2,1)S(1)}, u32[]{:S(2)}, u32[]{:S(2)}) collective-permute-start(bf16[80,512]{1,0:T(8,128)(2,1)S(1)} %shard_map.106.refs_3_), channel_id=1, source_target_pairs={{0,8},{8,0},{16,24},{24,16},{1,9},{9,1},{17,25},{25,17},{2,10},{10... | collective-permute-start | bytes 245768 | tf_op jit(solution)/shard_map/ppermute | solution.py:257
  32.4 16.7 %copy-start.4 = (bf16[1,32,2048]{2,1,0:T(8,128)(2,1)S(1)}, bf16[1,32,2048]{2,1,0:T(8,128)(2,1)}, u32[]{:S(2)}) copy-start(bf16[1,32,2048]{2,1,0:T(8,128)(2,1)} %param.8) | copy-start | bytes 393220
  32.4 16.7 %copy-start.5 = (f32[1,2048]{1,0:T(1,128)S(1)}, f32[1,2048]{1,0:T(1,128)}, u32[]{:S(2)}) copy-start(f32[1,2048]{1,0:T(1,128)} %param.13) | copy-start | bytes 24580
  32.4 1.4 %collective-permute-start.14 = (bf16[32,2048]{1,0:T(8,128)(2,1)S(1)}, bf16[32,2048]{1,0:T(8,128)(2,1)S(1)}, u32[]{:S(2)}, u32[]{:S(2)}) collective-permute-start(bf16[32,2048]{1,0:T(8,128)(2,1)S(1)} %get-tuple-element.46), channel_id=1, source_target_pairs={{0,1},{1,0},{2,3},{3,2},{4,5},{5,4},{6,7},{7,6},{8,9},{9,8},{10,11... | collective-permute-start | bytes 393224 | tf_op jit(solution)/shard_map/ppermute | solution.py:254
  32.5 2.8 %collective-permute-start.13 = (bf16[96,2048]{1,0:T(8,128)(2,1)S(1)}, bf16[96,2048]{1,0:T(8,128)(2,1)S(1)}, u32[]{:S(2)}, u32[]{:S(2)}) collective-permute-start(bf16[96,2048]{1,0:T(8,128)(2,1)S(1)} %get-tuple-element.44), channel_id=1, source_target_pairs={{0,1},{1,0},{2,3},{3,2},{4,5},{5,4},{6,7},{7,6},{8,9},{9,8},{10,11... | collective-permute-start | bytes 1179656 | tf_op jit(solution)/shard_map/ppermute | solution.py:254
  33.8 5.6 %collective-permute-start.15 = (bf16[32,2048]{1,0:T(8,128)(2,1)S(1)}, bf16[32,2048]{1,0:T(8,128)(2,1)S(1)}, u32[]{:S(2)}, u32[]{:S(2)}) collective-permute-start(bf16[32,2048]{1,0:T(8,128)(2,1)S(1)} %add_convert_fusion), channel_id=1, source_target_pairs={{0,2},{1,3},{2,0},{3,1},{4,6},{5,7},{6,4},{7,5},{8,10},{9,11},{10,... | collective-permute-start | bytes 393224 | tf_op jit(solution)/shard_map/ppermute | solution.py:254
  39.5 6.5 %collective-permute-start.17 = (bf16[32,2048]{1,0:T(8,128)(2,1)S(1)}, bf16[32,2048]{1,0:T(8,128)(2,1)S(1)}, u32[]{:S(2)}, u32[]{:S(2)}) collective-permute-start(bf16[32,2048]{1,0:T(8,128)(2,1)S(1)} %slice.31), channel_id=1, source_target_pairs={{0,2},{1,3},{2,0},{3,1},{4,6},{5,7},{6,4},{7,5},{8,10},{9,11},{10,... | collective-permute-start | bytes 393224 | tf_op jit(solution)/shard_map/ppermute | solution.py:254
  40.9 8.2 %collective-permute-start.16 = (bf16[32,2048]{1,0:T(8,128)(2,1)S(1)}, bf16[32,2048]{1,0:T(8,128)(2,1)S(1)}, u32[]{:S(2)}, u32[]{:S(2)}) collective-permute-start(bf16[32,2048]{1,0:T(8,128)(2,1)S(1)} %fusion), channel_id=1, source_target_pairs={{0,4},{1,5},{2,6},{3,7},{4,0},{5,1},{6,2},{7,3},{8,12},{9,13},{10,... | collective-permute-start | bytes 393224 | tf_op jit(solution)/shard_map/ppermute | solution.py:254
  49.2 7.0 %collective-permute-start.18 = (bf16[32,2048]{1,0:T(8,128)(2,1)S(1)}, bf16[32,2048]{1,0:T(8,128)(2,1)S(1)}, u32[]{:S(2)}, u32[]{:S(2)}) collective-permute-start(bf16[32,2048]{1,0:T(8,128)(2,1)S(1)} %fusion.5.refs_5_), channel_id=1, source_target_pairs={{0,4},{1,5},{2,6},{3,7},{4,0},{5,1},{6,2},{7,3},{8,12},{9,13},{10,... | collective-permute-start | bytes 393224 | tf_op jit(solution)/shard_map/ppermute | solution.py:254
  49.7 7.0 %collective-permute-start.20 = (bf16[32,2048]{1,0:T(8,128)(2,1)S(1)}, bf16[32,2048]{1,0:T(8,128)(2,1)S(1)}, u32[]{:S(2)}, u32[]{:S(2)}) collective-permute-start(bf16[32,2048]{1,0:T(8,128)(2,1)S(1)} %fusion.5.refs_5_), channel_id=1, source_target_pairs={{0,2},{1,3},{2,0},{3,1},{4,6},{5,7},{6,4},{7,5},{8,10},{9,11},{10,... | collective-permute-start | bytes 393224 | tf_op jit(solution)/shard_map/ppermute | solution.py:254
  52.3 5.0 %collective-permute-start.22 = (bf16[32,2048]{1,0:T(8,128)(2,1)S(1)}, bf16[32,2048]{1,0:T(8,128)(2,1)S(1)}, u32[]{:S(2)}, u32[]{:S(2)}) collective-permute-start(bf16[32,2048]{1,0:T(8,128)(2,1)S(1)} %fusion.5.refs_5_), channel_id=1, source_target_pairs={{0,1},{1,0},{2,3},{3,2},{4,5},{5,4},{6,7},{7,6},{8,9},{9,8},{10,11... | collective-permute-start | bytes 393224 | tf_op jit(solution)/shard_map/ppermute | solution.py:254
  56.2 1.3 %collective-permute-start.19 = (bf16[32,2048]{1,0:T(8,128)(2,1)S(1)}, bf16[32,2048]{1,0:T(8,128)(2,1)S(1)}, u32[]{:S(2)}, u32[]{:S(2)}) collective-permute-start(bf16[32,2048]{1,0:T(8,128)(2,1)S(1)} %collective-permute-done.18.refs_3_), channel_id=1, source_target_pairs={{0,1},{1,0},{2,3},{3,2},{4,5},{5,4},{6,7},{7,6},{8,9},{9,8},{10,11... | collective-permute-start | bytes 393224 | tf_op jit(solution)/shard_map/ppermute | solution.py:254
  56.7 1.3 %collective-permute-start.21 = (bf16[32,2048]{1,0:T(8,128)(2,1)S(1)}, bf16[32,2048]{1,0:T(8,128)(2,1)S(1)}, u32[]{:S(2)}, u32[]{:S(2)}) collective-permute-start(bf16[32,2048]{1,0:T(8,128)(2,1)S(1)} %collective-permute-done.20.refs_4_), channel_id=1, source_target_pairs={{0,1},{1,0},{2,3},{3,2},{4,5},{5,4},{6,7},{7,6},{8,9},{9,8},{10,11... | collective-permute-start | bytes 393224 | tf_op jit(solution)/shard_map/ppermute | solution.py:254
  56.7 5.8 %collective-permute-start.26 = (bf16[32,2048]{1,0:T(8,128)(2,1)S(1)}, bf16[32,2048]{1,0:T(8,128)(2,1)S(1)}, u32[]{:S(2)}, u32[]{:S(2)}) collective-permute-start(bf16[32,2048]{1,0:T(8,128)(2,1)S(1)} %collective-permute-done.18.refs_3_), channel_id=1, source_target_pairs={{0,2},{1,3},{2,0},{3,1},{4,6},{5,7},{6,4},{7,5},{8,10},{9,11},{10,... | collective-permute-start | bytes 393224 | tf_op jit(solution)/shard_map/ppermute | solution.py:254
  59.8 9.6 %collective-permute-start.23 = (bf16[192,512]{1,0:T(8,128)(2,1)S(1)}, bf16[192,512]{1,0:T(8,128)(2,1)S(1)}, u32[]{:S(2)}, u32[]{:S(2)}) collective-permute-start(bf16[192,512]{1,0:T(8,128)(2,1)S(1)} %get-tuple-element.63), channel_id=1, source_target_pairs={{0,24},{8,16},{16,8},{24,0},{1,25},{9,17},{17,9},{25,1},{2,26},{10... | collective-permute-start | bytes 589832 | tf_op jit(solution)/shard_map/ppermute | solution.py:257
  62.6 3.0 %collective-permute-start.27 = (bf16[32,2048]{1,0:T(8,128)(2,1)S(1)}, bf16[32,2048]{1,0:T(8,128)(2,1)S(1)}, u32[]{:S(2)}, u32[]{:S(2)}) collective-permute-start(bf16[32,2048]{1,0:T(8,128)(2,1)S(1)} %collective-permute-done.26.refs_1_), channel_id=1, source_target_pairs={{0,1},{1,0},{2,3},{3,2},{4,5},{5,4},{6,7},{7,6},{8,9},{9,8},{10,11... | collective-permute-start | bytes 393224 | tf_op jit(solution)/shard_map/ppermute | solution.py:254
  62.6 13.5 %collective-permute-start.24 = (bf16[192,512]{1,0:T(8,128)(2,1)S(1)}, bf16[192,512]{1,0:T(8,128)(2,1)S(1)}, u32[]{:S(2)}, u32[]{:S(2)}) collective-permute-start(bf16[192,512]{1,0:T(8,128)(2,1)S(1)} %get-tuple-element.64), channel_id=1, source_target_pairs={{0,16},{8,24},{16,0},{24,8},{1,17},{9,25},{17,1},{25,9},{2,18},{10... | collective-permute-start | bytes 589832 | tf_op jit(solution)/shard_map/ppermute | solution.py:257
  64.1 12.0 %collective-permute-start.25 = (bf16[192,512]{1,0:T(8,128)(2,1)S(1)}, bf16[192,512]{1,0:T(8,128)(2,1)S(1)}, u32[]{:S(2)}, u32[]{:S(2)}) collective-permute-start(bf16[192,512]{1,0:T(8,128)(2,1)S(1)} %get-tuple-element.65), channel_id=1, source_target_pairs={{0,8},{8,0},{16,24},{24,16},{1,9},{9,1},{17,25},{25,17},{2,10},{10... | collective-permute-start | bytes 589832 | tf_op jit(solution)/shard_map/ppermute | solution.py:257
  67.2 8.9 %collective-permute-start.28 = (bf16[64,512]{1,0:T(8,128)(2,1)S(1)}, bf16[64,512]{1,0:T(8,128)(2,1)S(1)}, u32[]{:S(2)}, u32[]{:S(2)}) collective-permute-start(bf16[64,512]{1,0:T(8,128)(2,1)S(1)} %get-tuple-element.68), channel_id=1, source_target_pairs={{0,24},{8,16},{16,8},{24,0},{1,25},{9,17},{17,9},{25,1},{2,26},{10... | collective-permute-start | bytes 196616 | tf_op jit(solution)/shard_map/ppermute | solution.py:257
  68.2 7.9 %collective-permute-start.29 = (bf16[64,512]{1,0:T(8,128)(2,1)S(1)}, bf16[64,512]{1,0:T(8,128)(2,1)S(1)}, u32[]{:S(2)}, u32[]{:S(2)}) collective-permute-start(bf16[64,512]{1,0:T(8,128)(2,1)S(1)} %get-tuple-element.69), channel_id=1, source_target_pairs={{0,16},{8,24},{16,0},{24,8},{1,17},{9,25},{17,1},{25,9},{2,18},{10... | collective-permute-start | bytes 196616 | tf_op jit(solution)/shard_map/ppermute | solution.py:257
  69.4 6.7 %collective-permute-start.30 = (bf16[64,512]{1,0:T(8,128)(2,1)S(1)}, bf16[64,512]{1,0:T(8,128)(2,1)S(1)}, u32[]{:S(2)}, u32[]{:S(2)}) collective-permute-start(bf16[64,512]{1,0:T(8,128)(2,1)S(1)} %get-tuple-element.70), channel_id=1, source_target_pairs={{0,8},{8,0},{16,24},{24,16},{1,9},{9,1},{17,25},{25,17},{2,10},{10... | collective-permute-start | bytes 196616 | tf_op jit(solution)/shard_map/ppermute | solution.py:257

commit v4 on v3

--- a/solution.py
+++ b/solution.py
@@ -311,7 +311,7 @@
         4 * layers * features * width,
         2 * layers * features * width,
     )(weights, main_own)
-    last_inputs = other_core(last_inputs, main_own)
+    last_inputs = other_core(last_inputs, squares)
     extra = -(-3 * layers // 16) * 16
     last_own = call(
         functools.partial(encode_last_kernel, len(last_inputs)),
@@ -352,15 +352,13 @@
     far = far_keep.astype(F32) + swap_tok(far_send, 1).astype(F32)
     near = keep.astype(F32) + swap_tok(send, 1).astype(F32)
     parts = [near[i * height : (i + 1) * height] for i in range(lines - 1)] + [far]
-    last_leaf = None
+    blocks = {}
     for line in reversed(range(1, lines)):
         low = line & -line
-        block = parts[line].astype(BF16)
-        if low == 1 and last_leaf is not None:
-            block, last_leaf = lax.optimization_barrier((block, last_leaf))
-        arrived = swap_tok(block, 2 * low)
-        if low == 1:
-            last_leaf = arrived
+        blocks[line] = parts[line].astype(BF16)
+        if low == 1 and line + 1 in blocks:
+            blocks[line], _ = lax.optimization_barrier((blocks[line], blocks[line + 1]))
+        arrived = swap_tok(blocks[line], 2 * low)
         parts[line ^ low] = parts[line ^ low] + arrived.astype(F32)
     resid_full = (
         parts[0] + decoder_bias[0] - layer_targets[0].astype(F32)
@@ -402,6 +400,7 @@
     _, last_sums, last_rows = grad_acts(last_resid)
 
     tall = math.gcd(256, features)
+    slots = min(8, layers * features // tall)
     decoder_grad, bias_grad = call(
         functools.partial(decoder_grad_kernel, loss_scale),
         (struct((layers, features, width), BF16), struct((1, width), F32)),
@@ -409,8 +408,8 @@
         (hbm, whole(1)[0]),
         [
             pltpu.VMEM((row_total, width), BF16),
-            pltpu.VMEM((4, tall, width), BF16),
-            pltpu.SemaphoreType.DMA((4,)),
+            pltpu.VMEM((slots, tall, width), BF16),
+            pltpu.SemaphoreType.DMA((slots,)),
         ],
         layers * block_flops,
         4 * layers * features * width,

time: 78.9 us -> 78.3 us (level)
  starting transfers between devices: 35.2 us -> 34 us
  waiting for transfers between devices: 20.7 us -> 21.7 us
    ppermute x12, waiting for transfers between devices: 2.67 us -> 4.59 us  [swap_layer(): return lax.ppermute(value, 'layer', [(i, i ^ step) for i in range(layers)])]
    ppermute x12, starting transfers between devices: 18.4 us -> 17.2 us  [swap_layer(): return lax.ppermute(value, 'layer', [(i, i ^ step) for i in range(layers)])]
    ppermute x19, waiting for transfers between devices: 18.1 us -> 17.1 us  [swap_tok(): return lax.ppermute(value, 'tok', [(i, i ^ step) for i in range(ranks)])]
where the time goes in v4:
time: 78.3 us; the launch traced here: 78.2 us
  starting transfers between devices  34 us (43%)
  waiting for transfers between devices  21.7 us (28%)
  Pallas kernels  19.4 us (25%)
  local copies, waits for them, and re-layouts  1.83 us (2%)
  between operations  1.01 us (1%)
    ppermute x12, starting transfers between devices, swap_layer(): return lax.ppermute(value, 'layer', [(i, i ^ step) for i in range(layers)])  17.2 us
    ppermute x19, waiting for transfers between devices, swap_tok(): return lax.ppermute(value, 'tok', [(i, i ^ step) for i in range(ranks)])  17.1 us
    ppermute x19, starting transfers between devices, swap_tok(): return lax.ppermute(value, 'tok', [(i, i ^ step) for i in range(ranks)])  16.8 us
    pallas_call x1, Pallas kernels, on_device(): call(functools.partial(decoder_grad_kernel, loss_scale), (struct((layers,...  4.81 us
    ppermute x12, waiting for transfers between devices, swap_layer(): return lax.ppermute(value, 'layer', [(i, i ^ step) for i in range(layers)])  4.59 us
    pallas_call x2, Pallas kernels, grad_acts(): call(functools.partial(grad_kernel, layers, len(pieces)), (*[struct((coun...  3.37 us
    pallas_call x1, Pallas kernels, on_device(): call(functools.partial(decode_kernel, layers, last, columns), (struct((ro...  2.77 us
    pallas_call x1, Pallas kernels, on_device(): call(functools.partial(order_kernel, len(late)), (struct((width, row_tota...  2.49 us
  transfers between devices with their start and end apart: 31, of which 16 were waited for; matrix products, arithmetic and copies ran while one was open for 0% of the time, Pallas kernels for 18%

profile of v4, /device:TPU:0, one launch (start us, length us, event | category | flops | bytes accessed | tf_op | source)
XLA Modules:
  0.0 78.2 jit_solution(14684536033668961545)
XLA Ops:
  0.6 4.1 %collective-permute-start = (bf16[32,2048]{1,0:T(8,128)(2,1)}, bf16[32,2048]{1,0:T(8,128)(2,1)S(1)}, u32[]{:S(2)}, u32[]{:S(2)}) collective-permute-start(bf16[32,2048]{1,0:T(8,128)(2,1)} %bitcast.18), channel_id=1, source_target_pairs={{0,4},{1,5},{2,6},{3,7},{4,0},{5,1},{6,2},{7,3},{8,12},{9,13},{10,... | collective-permute-start | bytes 393224 | tf_op jit(solution)/shard_map/ppermute | solution.py:254
  4.7 1.6 %collective-permute-start.2 = (bf16[32,2048]{1,0:T(8,128)(2,1)}, bf16[32,2048]{1,0:T(8,128)(2,1)S(1)}, u32[]{:S(2)}, u32[]{:S(2)}) collective-permute-start(bf16[32,2048]{1,0:T(8,128)(2,1)} %bitcast.19), channel_id=1, source_target_pairs={{0,2},{1,3},{2,0},{3,1},{4,6},{5,7},{6,4},{7,5},{8,10},{9,11},{10,... | collective-permute-start | bytes 393224 | tf_op jit(solution)/shard_map/ppermute | solution.py:254
  6.3 0.8 %copy-done.3 = s32[256]{0:T(256)S(1)} copy-done((s32[256]{0:T(256)S(1)}, s32[256]{0:T(256)}, u32[]{:S(2)}) %copy-start.3) | copy-done | bytes 1048
  7.2 0.1 shard_map.102.order.order_ref.refs_8_
  7.3 1.0 %copy-done.1 = bf16[1,32,2048]{2,1,0:T(8,128)(2,1)S(1)} copy-done((bf16[1,32,2048]{2,1,0:T(8,128)(2,1)S(1)}, bf16[1,32,2048]{2,1,0:T(8,128)(2,1)}, u32[]{:S(2)}) %copy-start.1) | copy-done | bytes 131096
  8.2 3.1 %collective-permute-done.refs_3_.refs_2_ = bf16[32,2048]{1,0:T(8,128)(2,1)S(1)} collective-permute-done((bf16[32,2048]{1,0:T(8,128)(2,1)}, bf16[32,2048]{1,0:T(8,128)(2,1)S(1)}, u32[]{:S(2)}, u32[]{:S(2)}) %collective-permute-start) | collective-permute-done | bytes 131104 | tf_op jit(solution)/shard_map/ppermute | solution.py:254
  11.4 0.0 collective-permute-start.1
  11.4 0.2 collective-permute-done.2.refs_4_.refs_1_
  11.6 0.3 collective-permute-start.3
  11.9 1.1 %collective-permute-start.8 = (bf16[32,2048]{1,0:T(8,128)(2,1)S(1)}, bf16[32,2048]{1,0:T(8,128)(2,1)S(1)}, u32[]{:S(2)}, u32[]{:S(2)}) collective-permute-start(bf16[32,2048]{1,0:T(8,128)(2,1)S(1)} %collective-permute-done.refs_3_.refs_2_), channel_id=1, source_target_pairs={{0,2},{1,3},{2,0},{3,1},{4,6},{5,7},{6,4},{7,5},{8,10},{9,11},{10,... | collective-permute-start | bytes 393224 | tf_op jit(solution)/shard_map/ppermute | solution.py:254
  13.0 0.0 collective-permute-done.1.refs_0_.refs_5_
  13.0 0.0 collective-permute-done.3.refs_1_.refs_4_
  13.0 0.6 shard_map.103.refs_3_.after
  13.6 2.5 %collective-permute-start.5 = (bf16[192,512]{1,0:T(8,128)(2,1)S(1)}, bf16[192,512]{1,0:T(8,128)(2,1)S(1)}, u32[]{:S(2)}, u32[]{:S(2)}) collective-permute-start(bf16[192,512]{1,0:T(8,128)(2,1)S(1)} %shard_map.103.refs_3_.after), channel_id=1, source_target_pairs={{0,24},{8,16},{16,8},{24,0},{1,25},{9,17},{17,9},{25,1},{2,26},{10... | collective-permute-start | bytes 589832 | tf_op jit(solution)/shard_map/ppermute | solution.py:257
  16.1 1.9 %shard_map.105.refs_4_ = f32[4,512]{1,0:T(4,128)S(1)} custom-call(bf16[4,512,2048]{2,1,0:T(8,128)(2,1)S(1)} %bitcast.12, bf16[192,512]{1,0:T(8,128)(2,1)S(1)} %shard_map.103.refs_3_.after), custom_call_target="tpu_custom_call" | custom-call | flops 16777216 | bytes 8388608 | tf_op jit(solution)/shard_map/pallas_call | solution.py:305
  18.1 0.0 collective-permute-done.8.refs_0_.refs_6_
  18.1 0.1 collective-permute-start.9
  18.1 0.9 %collective-permute-start.6 = (bf16[192,512]{1,0:T(8,128)(2,1)S(1)}, bf16[192,512]{1,0:T(8,128)(2,1)S(1)}, u32[]{:S(2)}, u32[]{:S(2)}) collective-permute-start(bf16[192,512]{1,0:T(8,128)(2,1)S(1)} %shard_map.103.refs_3_.after), channel_id=1, source_target_pairs={{0,16},{8,24},{16,0},{24,8},{1,17},{9,25},{17,1},{25,9},{2,18},{10... | collective-permute-start | bytes 589832 | tf_op jit(solution)/shard_map/ppermute | solution.py:257
  19.0 1.5 %collective-permute-start.7 = (bf16[192,512]{1,0:T(8,128)(2,1)S(1)}, bf16[192,512]{1,0:T(8,128)(2,1)S(1)}, u32[]{:S(2)}, u32[]{:S(2)}) collective-permute-start(bf16[192,512]{1,0:T(8,128)(2,1)S(1)} %shard_map.103.refs_3_.after), channel_id=1, source_target_pairs={{0,8},{8,0},{16,24},{24,16},{1,9},{9,1},{17,25},{25,17},{2,10},{10... | collective-permute-start | bytes 589832 | tf_op jit(solution)/shard_map/ppermute | solution.py:257
  20.5 0.0 collective-permute-done.9.refs_1_.refs_7_
  20.5 0.5 shard_map.106.refs_3_
  21.0 1.2 %collective-permute-start.10 = (bf16[80,512]{1,0:T(8,128)(2,1)S(1)}, bf16[80,512]{1,0:T(8,128)(2,1)S(1)}, u32[]{:S(2)}, u32[]{:S(2)}) collective-permute-start(bf16[80,512]{1,0:T(8,128)(2,1)S(1)} %shard_map.106.refs_3_), channel_id=1, source_target_pairs={{0,24},{8,16},{16,8},{24,0},{1,25},{9,17},{17,9},{25,1},{2,26},{10... | collective-permute-start | bytes 245768 | tf_op jit(solution)/shard_map/ppermute | solution.py:257
  22.2 0.9 %collective-permute-start.11 = (bf16[80,512]{1,0:T(8,128)(2,1)S(1)}, bf16[80,512]{1,0:T(8,128)(2,1)S(1)}, u32[]{:S(2)}, u32[]{:S(2)}) collective-permute-start(bf16[80,512]{1,0:T(8,128)(2,1)S(1)} %shard_map.106.refs_3_), channel_id=1, source_target_pairs={{0,16},{8,24},{16,0},{24,8},{1,17},{9,25},{17,1},{25,9},{2,18},{10... | collective-permute-start | bytes 245768 | tf_op jit(solution)/shard_map/ppermute | solution.py:257
  23.1 1.5 %collective-permute-start.12 = (bf16[80,512]{1,0:T(8,128)(2,1)S(1)}, bf16[80,512]{1,0:T(8,128)(2,1)S(1)}, u32[]{:S(2)}, u32[]{:S(2)}) collective-permute-start(bf16[80,512]{1,0:T(8,128)(2,1)S(1)} %shard_map.106.refs_3_), channel_id=1, source_target_pairs={{0,8},{8,0},{16,24},{24,16},{1,9},{9,1},{17,25},{25,17},{2,10},{10... | collective-permute-start | bytes 245768 | tf_op jit(solution)/shard_map/ppermute | solution.py:257
  24.6 1.5 %collective-permute-done.6.refs_1_ = bf16[192,512]{1,0:T(8,128)(2,1)S(1)} collective-permute-done((bf16[192,512]{1,0:T(8,128)(2,1)S(1)}, bf16[192,512]{1,0:T(8,128)(2,1)S(1)}, u32[]{:S(2)}, u32[]{:S(2)}) %collective-permute-start.6) | collective-permute-done | bytes 196640 | tf_op jit(solution)/shard_map/ppermute | solution.py:257
  26.1 0.7 collective-permute-done.7.refs_2_
  26.8 0.4 shard_map.104.first_sorted
  27.2 2.0 %collective-permute-done.10.refs_0_ = bf16[80,512]{1,0:T(8,128)(2,1)S(1)} collective-permute-done((bf16[80,512]{1,0:T(8,128)(2,1)S(1)}, bf16[80,512]{1,0:T(8,128)(2,1)S(1)}, u32[]{:S(2)}, u32[]{:S(2)}) %collective-permute-start.10) | collective-permute-done | bytes 81952 | tf_op jit(solution)/shard_map/ppermute | solution.py:257
  29.2 0.2 collective-permute-done.11.refs_1_
  29.4 0.2 collective-permute-done.12.refs_2_
  29.6 2.8 %shard_map.107 = (bf16[256,2048]{1,0:T(8,128)(2,1)S(1)}, bf16[96,2048]{1,0:T(8,128)(2,1)S(1)}, bf16[96,2048]{1,0:T(8,128)(2,1)S(1)}, bf16[32,2048]{1,0:T(8,128)(...) custom-call(bf16[256,256]{1,0:T(8,128)(2,1)S(1)} %shard_map.102.order.order_ref.refs_8_, ...), custom_call_target="tpu_custom_call" | custom-call | flops 2147483648 | bytes 8388608 | tf_op jit(solution)/shard_map/pallas_call | solution.py:337
  32.4 0.0 copy-start.4
  32.4 0.0 copy-start.5
  32.4 0.1 collective-permute-start.14
  32.5 0.5 collective-permute-start.13
  33.0 0.8 %collective-permute-done.14 = bf16[32,2048]{1,0:T(8,128)(2,1)S(1)} collective-permute-done((bf16[32,2048]{1,0:T(8,128)(2,1)S(1)}, bf16[32,2048]{1,0:T(8,128)(2,1)S(1)}, u32[]{:S(2)}, u32[]{:S(2)}) %collective-permute-start.14) | collective-permute-done | bytes 131104 | tf_op jit(solution)/shard_map/ppermute | solution.py:254
  33.8 1.5 %collective-permute-start.15 = (bf16[32,2048]{1,0:T(8,128)(2,1)S(1)}, bf16[32,2048]{1,0:T(8,128)(2,1)S(1)}, u32[]{:S(2)}, u32[]{:S(2)}) collective-permute-start(bf16[32,2048]{1,0:T(8,128)(2,1)S(1)} %add_convert_fusion), channel_id=1, source_target_pairs={{0,2},{1,3},{2,0},{3,1},{4,6},{5,7},{6,4},{7,5},{8,10},{9,11},{10,... | collective-permute-start | bytes 393224 | tf_op jit(solution)/shard_map/ppermute | solution.py:254
  35.3 0.1 convert_add_fusion
  35.4 4.0 %collective-permute-done.15 = bf16[32,2048]{1,0:T(8,128)(2,1)S(1)} collective-permute-done((bf16[32,2048]{1,0:T(8,128)(2,1)S(1)}, bf16[32,2048]{1,0:T(8,128)(2,1)S(1)}, u32[]{:S(2)}, u32[]{:S(2)}) %collective-permute-start.15) | collective-permute-done | bytes 131104 | tf_op jit(solution)/shard_map/ppermute | solution.py:254
  39.5 1.5 %collective-permute-start.17 = (bf16[32,2048]{1,0:T(8,128)(2,1)S(1)}, bf16[32,2048]{1,0:T(8,128)(2,1)S(1)}, u32[]{:S(2)}, u32[]{:S(2)}) collective-permute-start(bf16[32,2048]{1,0:T(8,128)(2,1)S(1)} %slice.31), channel_id=1, source_target_pairs={{0,2},{1,3},{2,0},{3,1},{4,6},{5,7},{6,4},{7,5},{8,10},{9,11},{10,... | collective-permute-start | bytes 393224 | tf_op jit(solution)/shard_map/ppermute | solution.py:254
  40.9 2.4 %collective-permute-start.16 = (bf16[32,2048]{1,0:T(8,128)(2,1)S(1)}, bf16[32,2048]{1,0:T(8,128)(2,1)S(1)}, u32[]{:S(2)}, u32[]{:S(2)}) collective-permute-start(bf16[32,2048]{1,0:T(8,128)(2,1)S(1)} %fusion), channel_id=1, source_target_pairs={{0,4},{1,5},{2,6},{3,7},{4,0},{5,1},{6,2},{7,3},{8,12},{9,13},{10,... | collective-permute-start | bytes 393224 | tf_op jit(solution)/shard_map/ppermute | solution.py:254
  43.3 2.5 %shard_map.108 = (bf16[2048,256]{1,0:T(8,128)(2,1)S(1)}, bf16[4,2048,512]{2,1,0:T(8,128)(2,1)S(1)}) custom-call(bf16[32,2048]{1,0:T(8,128)(2,1)S(1)} %bitcast.22, bf16[32,2048]{1,0:T(8,128)(2,1)S(1)} %collective-permute-done.2.refs_4_.refs_1_, bf16[32,2048]{1,0:T(8,128)(2,1)S(1)} %collective-permute-done.refs_3_.refs_2_, ...), custom_call_target="tpu_custom_call" | custom-call | flops 268435456 | bytes 16777216 | tf_op jit(solution)/shard_map/pallas_call | solution.py:368
  45.8 0.6 collective-permute-done.17
  46.4 2.7 %collective-permute-done.16 = bf16[32,2048]{1,0:T(8,128)(2,1)S(1)} collective-permute-done((bf16[32,2048]{1,0:T(8,128)(2,1)S(1)}, bf16[32,2048]{1,0:T(8,128)(2,1)S(1)}, u32[]{:S(2)}, u32[]{:S(2)}) %collective-permute-start.16) | collective-permute-done | bytes 131104 | tf_op jit(solution)/shard_map/ppermute | solution.py:254
  49.2 0.1 fusion.5.refs_5_
  49.2 0.5 collective-permute-start.18
  49.8 2.6 %collective-permute-start.20 = (bf16[32,2048]{1,0:T(8,128)(2,1)S(1)}, bf16[32,2048]{1,0:T(8,128)(2,1)S(1)}, u32[]{:S(2)}, u32[]{:S(2)}) collective-permute-start(bf16[32,2048]{1,0:T(8,128)(2,1)S(1)} %fusion.5.refs_5_), channel_id=1, source_target_pairs={{0,2},{1,3},{2,0},{3,1},{4,6},{5,7},{6,4},{7,5},{8,10},{9,11},{10,... | collective-permute-start | bytes 393224 | tf_op jit(solution)/shard_map/ppermute | solution.py:254
  52.4 4.2 %collective-permute-done.18.refs_3_ = bf16[32,2048]{1,0:T(8,128)(2,1)S(1)} collective-permute-done((bf16[32,2048]{1,0:T(8,128)(2,1)S(1)}, bf16[32,2048]{1,0:T(8,128)(2,1)S(1)}, u32[]{:S(2)}, u32[]{:S(2)}) %collective-permute-start.18) | collective-permute-done | bytes 131104 | tf_op jit(solution)/shard_map/ppermute | solution.py:254
  56.5 0.2 collective-permute-done.20.refs_4_
  56.7 0.3 collective-permute-start.21
  57.0 0.3 collective-permute-start.26
  57.3 0.5 collective-permute-done.19.refs_0_
  57.9 0.2 collective-permute-done.21.refs_1_
  58.1 1.8 %shard_map.109 = (f32[192,512]{1,0:T(8,128)S(1)}, bf16[192,512]{1,0:T(8,128)(2,1)S(1)}, bf16[192,512]{1,0:T(8,128)(2,1)S(1)}, bf16[192,512]{1,0:T(8,128)(2,1)S(1)}, bf16[192,2048]{1,0:T(8,128)(2,1)S(1)}) custom-call(bf16[32,2048]{1,0:T(8,128)(2,1)S(1)} %collective-permute-done.19.refs_0_, bf16[32,2048]{1,0:T(8,128)(2,1)S(1)} %collective-permute-done.21.refs_1_, ...), custom_call_target="tpu_custom_call" | custom-call | flops 1610612736 | bytes 8388608 | tf_op jit(solution)/shard_map/pallas_call | solution.py:384
  59.9 2.2 %collective-permute-start.23 = (bf16[192,512]{1,0:T(8,128)(2,1)S(1)}, bf16[192,512]{1,0:T(8,128)(2,1)S(1)}, u32[]{:S(2)}, u32[]{:S(2)}) collective-permute-start(bf16[192,512]{1,0:T(8,128)(2,1)S(1)} %get-tuple-element.63), channel_id=1, source_target_pairs={{0,24},{8,16},{16,8},{24,0},{1,25},{9,17},{17,9},{25,1},{2,26},{10... | collective-permute-start | bytes 589832 | tf_op jit(solution)/shard_map/ppermute | solution.py:257
  62.1 0.5 collective-permute-done.26.refs_1_
  62.6 0.7 collective-permute-start.24
  63.3 2.0 %collective-permute-start.25 = (bf16[192,512]{1,0:T(8,128)(2,1)S(1)}, bf16[192,512]{1,0:T(8,128)(2,1)S(1)}, u32[]{:S(2)}, u32[]{:S(2)}) collective-permute-start(bf16[192,512]{1,0:T(8,128)(2,1)S(1)} %get-tuple-element.65), channel_id=1, source_target_pairs={{0,8},{8,0},{16,24},{24,16},{1,9},{9,1},{17,25},{25,17},{2,10},{10... | collective-permute-start | bytes 589832 | tf_op jit(solution)/shard_map/ppermute | solution.py:257
  65.4 1.6 %shard_map.110 = (f32[64,512]{1,0:T(8,128)S(1)}, bf16[64,512]{1,0:T(8,128)(2,1)S(1)}, bf16[64,512]{1,0:T(8,128)(2,1)S(1)}, bf16[64,512]{1,0:T(8,128)(2,1)S(1)}, bf16[64,2048]{1,0:T(8,128)(2,1)S(1)}) custom-call(bf16[32,2048]{1,0:T(8,128)(2,1)S(1)} %collective-permute-done.27.refs_0_, bf16[32,2048]{1,0:T(8,128)(2,1)S(1)} %collective-permute-done.26.refs_1_, ...), custom_call_target="tpu_custom_call" | custom-call | flops 536870912 | bytes 8388608 | tf_op jit(solution)/shard_map/pallas_call | solution.py:384
  66.9 1.0 %collective-permute-start.28 = (bf16[64,512]{1,0:T(8,128)(2,1)S(1)}, bf16[64,512]{1,0:T(8,128)(2,1)S(1)}, u32[]{:S(2)}, u32[]{:S(2)}) collective-permute-start(bf16[64,512]{1,0:T(8,128)(2,1)S(1)} %get-tuple-element.68), channel_id=1, source_target_pairs={{0,24},{8,16},{16,8},{24,0},{1,25},{9,17},{17,9},{25,1},{2,26},{10... | collective-permute-start | bytes 196616 | tf_op jit(solution)/shard_map/ppermute | solution.py:257
  68.0 0.7 collective-permute-start.29
  68.6 2.0 %collective-permute-start.30 = (bf16[64,512]{1,0:T(8,128)(2,1)S(1)}, bf16[64,512]{1,0:T(8,128)(2,1)S(1)}, u32[]{:S(2)}, u32[]{:S(2)}) collective-permute-start(bf16[64,512]{1,0:T(8,128)(2,1)S(1)} %get-tuple-element.70), channel_id=1, source_target_pairs={{0,8},{8,0},{16,24},{24,16},{1,9},{9,1},{17,25},{25,17},{2,10},{10... | collective-permute-start | bytes 196616 | tf_op jit(solution)/shard_map/ppermute | solution.py:257
  70.7 4.8 %shard_map.112 = (bf16[4,512,2048]{2,1,0:T(8,128)(2,1)}, f32[1,2048]{1,0:T(1,128)}) custom-call(bf16[256,2048]{1,0:T(8,128)(2,1)S(1)} %get-tuple-element.59.acts, f32[4,512]{1,0:T(4,128)S(1)} %get-tuple-element.60.norms, bf16[192,2048]{1,0:T(8,128)(2,1)S(1)} %get-tuple-element.74.main_rows, bf16[64,2048]{1,0:T(8,128)(2,1)S(1)} %get-tuple-element.75.last_rows, ...), custom_call_target="tpu_custom_call" | custom-call | flops 2147483648 | bytes 16777216 | tf_op jit(solution)/shard_map/pallas_call | solution.py:404
  75.5 2.4 %shard_map.111 = (bf16[2048,512]{1,0:T(8,128)(2,1)}, f32[1,512]{1,0:T(1,128)}) custom-call(bf16[2048,256]{1,0:T(8,128)(2,1)S(1)} %get-tuple-element.58.ordered, bf16[256,2048]{1,0:T(8,128)(2,1)S(1)} %get-tuple-element.59.acts, f32[4,512]{1,0:T(4,128)S(1)} %get-tuple-element.60.norms, bf16[192,512]{1,0:T(8,128)(2,1)S(1)} %collective-permute-done.23.refs_0_, ...), custom_call_target="tpu_custom_call" | custom-call | flops 536870912 | bytes 2097152 | tf_op jit(solution)/shard_map/pallas_call | solution.py:419
  (31 shorter events, 0.1 us)
Async XLA Ops:
  0.6 10.7 %collective-permute-start = (bf16[32,2048]{1,0:T(8,128)(2,1)}, bf16[32,2048]{1,0:T(8,128)(2,1)S(1)}, u32[]{:S(2)}, u32[]{:S(2)}) collective-permute-start(bf16[32,2048]{1,0:T(8,128)(2,1)} %bitcast.18), channel_id=1, source_target_pairs={{0,4},{1,5},{2,6},{3,7},{4,0},{5,1},{6,2},{7,3},{8,12},{9,13},{10,... | collective-permute-start | bytes 393224 | tf_op jit(solution)/shard_map/ppermute | solution.py:254
  4.7 6.8 %collective-permute-start.2 = (bf16[32,2048]{1,0:T(8,128)(2,1)}, bf16[32,2048]{1,0:T(8,128)(2,1)S(1)}, u32[]{:S(2)}, u32[]{:S(2)}) collective-permute-start(bf16[32,2048]{1,0:T(8,128)(2,1)} %bitcast.19), channel_id=1, source_target_pairs={{0,2},{1,3},{2,0},{3,1},{4,6},{5,7},{6,4},{7,5},{8,10},{9,11},{10,... | collective-permute-start | bytes 393224 | tf_op jit(solution)/shard_map/ppermute | solution.py:254
  6.3 9.8 %slice-start = ((s8[8388608]{0:T(1024)(128)(4,1)}), s8[4194304]{0:T(1024)(128)(4,1)S(1)}, s32[]{:S(2)}) async-start(s8[8388608]{0:T(1024)(128)(4,1)} %bitcast.10), calls=%async_computation | async-start | bytes 8388608
  6.3 0.8 %copy-start.3 = (s32[256]{0:T(256)S(1)}, s32[256]{0:T(256)}, u32[]{:S(2)}) copy-start(s32[256]{0:T(256)} %param.9) | copy-start | bytes 3076
  7.1 1.1 %copy-start.1 = (bf16[1,32,2048]{2,1,0:T(8,128)(2,1)S(1)}, bf16[1,32,2048]{2,1,0:T(8,128)(2,1)}, u32[]{:S(2)}) copy-start(bf16[1,32,2048]{2,1,0:T(8,128)(2,1)} %param.7) | copy-start | bytes 393220
  7.1 5.9 %copy-start = (bf16[1,2048,512]{2,1,0:T(8,128)(2,1)S(1)}, bf16[1,2048,512]{2,1,0:T(8,128)(2,1)}, u32[]{:S(2)}) copy-start(bf16[1,2048,512]{2,1,0:T(8,128)(2,1)} %param.10) | copy-start | bytes 6291460
  7.1 5.9 %copy-start.2 = (f32[1,512]{1,0:T(1,128)S(1)}, f32[1,512]{1,0:T(1,128)}, u32[]{:S(2)}) copy-start(f32[1,512]{1,0:T(1,128)} %refs_3_.1) | copy-start | bytes 6148
  7.1 9.0 %slice-start.1 = ((s8[8388608]{0:T(1024)(128)(4,1)}), s8[4194304]{0:T(1024)(128)(4,1)S(1)}, s32[]{:S(2)}) async-start(s8[8388608]{0:T(1024)(128)(4,1)} %bitcast.10), calls=%async_computation.1 | async-start | bytes 8388608
  8.2 4.8 %collective-permute-start.4 = (bf16[32,2048]{1,0:T(8,128)(2,1)S(1)}, bf16[32,2048]{1,0:T(8,128)(2,1)S(1)}, u32[]{:S(2)}, u32[]{:S(2)}) collective-permute-start(bf16[32,2048]{1,0:T(8,128)(2,1)S(1)} %bitcast.20), channel_id=1, source_target_pairs={{0,1},{1,0},{2,3},{3,2},{4,5},{5,4},{6,7},{7,6},{8,9},{9,8},{10,11... | collective-permute-start | bytes 393224 | tf_op jit(solution)/shard_map/ppermute | solution.py:254
  11.4 1.6 %collective-permute-start.1 = (bf16[32,2048]{1,0:T(8,128)(2,1)S(1)}, bf16[32,2048]{1,0:T(8,128)(2,1)S(1)}, u32[]{:S(2)}, u32[]{:S(2)}) collective-permute-start(bf16[32,2048]{1,0:T(8,128)(2,1)S(1)} %collective-permute-done.refs_3_.refs_2_), channel_id=1, source_target_pairs={{0,1},{1,0},{2,3},{3,2},{4,5},{5,4},{6,7},{7,6},{8,9},{9,8},{10,11... | collective-permute-start | bytes 393224 | tf_op jit(solution)/shard_map/ppermute | solution.py:254
  11.6 1.4 %collective-permute-start.3 = (bf16[32,2048]{1,0:T(8,128)(2,1)S(1)}, bf16[32,2048]{1,0:T(8,128)(2,1)S(1)}, u32[]{:S(2)}, u32[]{:S(2)}) collective-permute-start(bf16[32,2048]{1,0:T(8,128)(2,1)S(1)} %collective-permute-done.2.refs_4_.refs_1_), channel_id=1, source_target_pairs={{0,1},{1,0},{2,3},{3,2},{4,5},{5,4},{6,7},{7,6},{8,9},{9,8},{10,11... | collective-permute-start | bytes 393224 | tf_op jit(solution)/shard_map/ppermute | solution.py:254
  11.9 6.2 %collective-permute-start.8 = (bf16[32,2048]{1,0:T(8,128)(2,1)S(1)}, bf16[32,2048]{1,0:T(8,128)(2,1)S(1)}, u32[]{:S(2)}, u32[]{:S(2)}) collective-permute-start(bf16[32,2048]{1,0:T(8,128)(2,1)S(1)} %collective-permute-done.refs_3_.refs_2_), channel_id=1, source_target_pairs={{0,2},{1,3},{2,0},{3,1},{4,6},{5,7},{6,4},{7,5},{8,10},{9,11},{10,... | collective-permute-start | bytes 393224 | tf_op jit(solution)/shard_map/ppermute | solution.py:254
  13.6 9.5 %collective-permute-start.5 = (bf16[192,512]{1,0:T(8,128)(2,1)S(1)}, bf16[192,512]{1,0:T(8,128)(2,1)S(1)}, u32[]{:S(2)}, u32[]{:S(2)}) collective-permute-start(bf16[192,512]{1,0:T(8,128)(2,1)S(1)} %shard_map.103.refs_3_.after), channel_id=1, source_target_pairs={{0,24},{8,16},{16,8},{24,0},{1,25},{9,17},{17,9},{25,1},{2,26},{10... | collective-permute-start | bytes 589832 | tf_op jit(solution)/shard_map/ppermute | solution.py:257
  18.1 2.5 %collective-permute-start.9 = (bf16[32,2048]{1,0:T(8,128)(2,1)S(1)}, bf16[32,2048]{1,0:T(8,128)(2,1)S(1)}, u32[]{:S(2)}, u32[]{:S(2)}) collective-permute-start(bf16[32,2048]{1,0:T(8,128)(2,1)S(1)} %collective-permute-done.8.refs_0_.refs_6_), channel_id=1, source_target_pairs={{0,1},{1,0},{2,3},{3,2},{4,5},{5,4},{6,7},{7,6},{8,9},{9,8},{10,11... | collective-permute-start | bytes 393224 | tf_op jit(solution)/shard_map/ppermute | solution.py:254
  18.1 7.9 %collective-permute-start.6 = (bf16[192,512]{1,0:T(8,128)(2,1)S(1)}, bf16[192,512]{1,0:T(8,128)(2,1)S(1)}, u32[]{:S(2)}, u32[]{:S(2)}) collective-permute-start(bf16[192,512]{1,0:T(8,128)(2,1)S(1)} %shard_map.103.refs_3_.after), channel_id=1, source_target_pairs={{0,16},{8,24},{16,0},{24,8},{1,17},{9,25},{17,1},{25,9},{2,18},{10... | collective-permute-start | bytes 589832 | tf_op jit(solution)/shard_map/ppermute | solution.py:257
  19.0 7.7 %collective-permute-start.7 = (bf16[192,512]{1,0:T(8,128)(2,1)S(1)}, bf16[192,512]{1,0:T(8,128)(2,1)S(1)}, u32[]{:S(2)}, u32[]{:S(2)}) collective-permute-start(bf16[192,512]{1,0:T(8,128)(2,1)S(1)} %shard_map.103.refs_3_.after), channel_id=1, source_target_pairs={{0,8},{8,0},{16,24},{24,16},{1,9},{9,1},{17,25},{25,17},{2,10},{10... | collective-permute-start | bytes 589832 | tf_op jit(solution)/shard_map/ppermute | solution.py:257
  21.0 8.1 %collective-permute-start.10 = (bf16[80,512]{1,0:T(8,128)(2,1)S(1)}, bf16[80,512]{1,0:T(8,128)(2,1)S(1)}, u32[]{:S(2)}, u32[]{:S(2)}) collective-permute-start(bf16[80,512]{1,0:T(8,128)(2,1)S(1)} %shard_map.106.refs_3_), channel_id=1, source_target_pairs={{0,24},{8,16},{16,8},{24,0},{1,25},{9,17},{17,9},{25,1},{2,26},{10... | collective-permute-start | bytes 245768 | tf_op jit(solution)/shard_map/ppermute | solution.py:257
  22.2 7.1 %collective-permute-start.11 = (bf16[80,512]{1,0:T(8,128)(2,1)S(1)}, bf16[80,512]{1,0:T(8,128)(2,1)S(1)}, u32[]{:S(2)}, u32[]{:S(2)}) collective-permute-start(bf16[80,512]{1,0:T(8,128)(2,1)S(1)} %shard_map.106.refs_3_), channel_id=1, source_target_pairs={{0,16},{8,24},{16,0},{24,8},{1,17},{9,25},{17,1},{25,9},{2,18},{10... | collective-permute-start | bytes 245768 | tf_op jit(solution)/shard_map/ppermute | solution.py:257
  23.1 6.5 %collective-permute-start.12 = (bf16[80,512]{1,0:T(8,128)(2,1)S(1)}, bf16[80,512]{1,0:T(8,128)(2,1)S(1)}, u32[]{:S(2)}, u32[]{:S(2)}) collective-permute-start(bf16[80,512]{1,0:T(8,128)(2,1)S(1)} %shard_map.106.refs_3_), channel_id=1, source_target_pairs={{0,8},{8,0},{16,24},{24,16},{1,9},{9,1},{17,25},{25,17},{2,10},{10... | collective-permute-start | bytes 245768 | tf_op jit(solution)/shard_map/ppermute | solution.py:257
  32.4 16.8 %copy-start.4 = (bf16[1,32,2048]{2,1,0:T(8,128)(2,1)S(1)}, bf16[1,32,2048]{2,1,0:T(8,128)(2,1)}, u32[]{:S(2)}) copy-start(bf16[1,32,2048]{2,1,0:T(8,128)(2,1)} %param.8) | copy-start | bytes 393220
  32.4 16.8 %copy-start.5 = (f32[1,2048]{1,0:T(1,128)S(1)}, f32[1,2048]{1,0:T(1,128)}, u32[]{:S(2)}) copy-start(f32[1,2048]{1,0:T(1,128)} %param.13) | copy-start | bytes 24580
  32.4 1.4 %collective-permute-start.14 = (bf16[32,2048]{1,0:T(8,128)(2,1)S(1)}, bf16[32,2048]{1,0:T(8,128)(2,1)S(1)}, u32[]{:S(2)}, u32[]{:S(2)}) collective-permute-start(bf16[32,2048]{1,0:T(8,128)(2,1)S(1)} %get-tuple-element.46), channel_id=1, source_target_pairs={{0,1},{1,0},{2,3},{3,2},{4,5},{5,4},{6,7},{7,6},{8,9},{9,8},{10,11... | collective-permute-start | bytes 393224 | tf_op jit(solution)/shard_map/ppermute | solution.py:254
  32.5 2.8 %collective-permute-start.13 = (bf16[96,2048]{1,0:T(8,128)(2,1)S(1)}, bf16[96,2048]{1,0:T(8,128)(2,1)S(1)}, u32[]{:S(2)}, u32[]{:S(2)}) collective-permute-start(bf16[96,2048]{1,0:T(8,128)(2,1)S(1)} %get-tuple-element.44), channel_id=1, source_target_pairs={{0,1},{1,0},{2,3},{3,2},{4,5},{5,4},{6,7},{7,6},{8,9},{9,8},{10,11... | collective-permute-start | bytes 1179656 | tf_op jit(solution)/shard_map/ppermute | solution.py:254
  33.8 5.6 %collective-permute-start.15 = (bf16[32,2048]{1,0:T(8,128)(2,1)S(1)}, bf16[32,2048]{1,0:T(8,128)(2,1)S(1)}, u32[]{:S(2)}, u32[]{:S(2)}) collective-permute-start(bf16[32,2048]{1,0:T(8,128)(2,1)S(1)} %add_convert_fusion), channel_id=1, source_target_pairs={{0,2},{1,3},{2,0},{3,1},{4,6},{5,7},{6,4},{7,5},{8,10},{9,11},{10,... | collective-permute-start | bytes 393224 | tf_op jit(solution)/shard_map/ppermute | solution.py:254
  39.5 7.0 %collective-permute-start.17 = (bf16[32,2048]{1,0:T(8,128)(2,1)S(1)}, bf16[32,2048]{1,0:T(8,128)(2,1)S(1)}, u32[]{:S(2)}, u32[]{:S(2)}) collective-permute-start(bf16[32,2048]{1,0:T(8,128)(2,1)S(1)} %slice.31), channel_id=1, source_target_pairs={{0,2},{1,3},{2,0},{3,1},{4,6},{5,7},{6,4},{7,5},{8,10},{9,11},{10,... | collective-permute-start | bytes 393224 | tf_op jit(solution)/shard_map/ppermute | solution.py:254
  40.9 8.2 %collective-permute-start.16 = (bf16[32,2048]{1,0:T(8,128)(2,1)S(1)}, bf16[32,2048]{1,0:T(8,128)(2,1)S(1)}, u32[]{:S(2)}, u32[]{:S(2)}) collective-permute-start(bf16[32,2048]{1,0:T(8,128)(2,1)S(1)} %fusion), channel_id=1, source_target_pairs={{0,4},{1,5},{2,6},{3,7},{4,0},{5,1},{6,2},{7,3},{8,12},{9,13},{10,... | collective-permute-start | bytes 393224 | tf_op jit(solution)/shard_map/ppermute | solution.py:254
  49.2 7.3 %collective-permute-start.18 = (bf16[32,2048]{1,0:T(8,128)(2,1)S(1)}, bf16[32,2048]{1,0:T(8,128)(2,1)S(1)}, u32[]{:S(2)}, u32[]{:S(2)}) collective-permute-start(bf16[32,2048]{1,0:T(8,128)(2,1)S(1)} %fusion.5.refs_5_), channel_id=1, source_target_pairs={{0,4},{1,5},{2,6},{3,7},{4,0},{5,1},{6,2},{7,3},{8,12},{9,13},{10,... | collective-permute-start | bytes 393224 | tf_op jit(solution)/shard_map/ppermute | solution.py:254
  49.8 6.9 %collective-permute-start.20 = (bf16[32,2048]{1,0:T(8,128)(2,1)S(1)}, bf16[32,2048]{1,0:T(8,128)(2,1)S(1)}, u32[]{:S(2)}, u32[]{:S(2)}) collective-permute-start(bf16[32,2048]{1,0:T(8,128)(2,1)S(1)} %fusion.5.refs_5_), channel_id=1, source_target_pairs={{0,2},{1,3},{2,0},{3,1},{4,6},{5,7},{6,4},{7,5},{8,10},{9,11},{10,... | collective-permute-start | bytes 393224 | tf_op jit(solution)/shard_map/ppermute | solution.py:254
  52.4 5.0 %collective-permute-start.22 = (bf16[32,2048]{1,0:T(8,128)(2,1)S(1)}, bf16[32,2048]{1,0:T(8,128)(2,1)S(1)}, u32[]{:S(2)}, u32[]{:S(2)}) collective-permute-start(bf16[32,2048]{1,0:T(8,128)(2,1)S(1)} %fusion.5.refs_5_), channel_id=1, source_target_pairs={{0,1},{1,0},{2,3},{3,2},{4,5},{5,4},{6,7},{7,6},{8,9},{9,8},{10,11... | collective-permute-start | bytes 393224 | tf_op jit(solution)/shard_map/ppermute | solution.py:254
  56.5 1.3 %collective-permute-start.19 = (bf16[32,2048]{1,0:T(8,128)(2,1)S(1)}, bf16[32,2048]{1,0:T(8,128)(2,1)S(1)}, u32[]{:S(2)}, u32[]{:S(2)}) collective-permute-start(bf16[32,2048]{1,0:T(8,128)(2,1)S(1)} %collective-permute-done.18.refs_3_), channel_id=1, source_target_pairs={{0,1},{1,0},{2,3},{3,2},{4,5},{5,4},{6,7},{7,6},{8,9},{9,8},{10,11... | collective-permute-start | bytes 393224 | tf_op jit(solution)/shard_map/ppermute | solution.py:254
  56.7 1.4 %collective-permute-start.21 = (bf16[32,2048]{1,0:T(8,128)(2,1)S(1)}, bf16[32,2048]{1,0:T(8,128)(2,1)S(1)}, u32[]{:S(2)}, u32[]{:S(2)}) collective-permute-start(bf16[32,2048]{1,0:T(8,128)(2,1)S(1)} %collective-permute-done.20.refs_4_), channel_id=1, source_target_pairs={{0,1},{1,0},{2,3},{3,2},{4,5},{5,4},{6,7},{7,6},{8,9},{9,8},{10,11... | collective-permute-start | bytes 393224 | tf_op jit(solution)/shard_map/ppermute | solution.py:254
  57.0 5.6 %collective-permute-start.26 = (bf16[32,2048]{1,0:T(8,128)(2,1)S(1)}, bf16[32,2048]{1,0:T(8,128)(2,1)S(1)}, u32[]{:S(2)}, u32[]{:S(2)}) collective-permute-start(bf16[32,2048]{1,0:T(8,128)(2,1)S(1)} %collective-permute-done.18.refs_3_), channel_id=1, source_target_pairs={{0,2},{1,3},{2,0},{3,1},{4,6},{5,7},{6,4},{7,5},{8,10},{9,11},{10,... | collective-permute-start | bytes 393224 | tf_op jit(solution)/shard_map/ppermute | solution.py:254
  59.9 8.8 %collective-permute-start.23 = (bf16[192,512]{1,0:T(8,128)(2,1)S(1)}, bf16[192,512]{1,0:T(8,128)(2,1)S(1)}, u32[]{:S(2)}, u32[]{:S(2)}) collective-permute-start(bf16[192,512]{1,0:T(8,128)(2,1)S(1)} %get-tuple-element.63), channel_id=1, source_target_pairs={{0,24},{8,16},{16,8},{24,0},{1,25},{9,17},{17,9},{25,1},{2,26},{10... | collective-permute-start | bytes 589832 | tf_op jit(solution)/shard_map/ppermute | solution.py:257
  62.6 2.8 %collective-permute-start.27 = (bf16[32,2048]{1,0:T(8,128)(2,1)S(1)}, bf16[32,2048]{1,0:T(8,128)(2,1)S(1)}, u32[]{:S(2)}, u32[]{:S(2)}) collective-permute-start(bf16[32,2048]{1,0:T(8,128)(2,1)S(1)} %collective-permute-done.26.refs_1_), channel_id=1, source_target_pairs={{0,1},{1,0},{2,3},{3,2},{4,5},{5,4},{6,7},{7,6},{8,9},{9,8},{10,11... | collective-permute-start | bytes 393224 | tf_op jit(solution)/shard_map/ppermute | solution.py:254
  62.6 12.9 %collective-permute-start.24 = (bf16[192,512]{1,0:T(8,128)(2,1)S(1)}, bf16[192,512]{1,0:T(8,128)(2,1)S(1)}, u32[]{:S(2)}, u32[]{:S(2)}) collective-permute-start(bf16[192,512]{1,0:T(8,128)(2,1)S(1)} %get-tuple-element.64), channel_id=1, source_target_pairs={{0,16},{8,24},{16,0},{24,8},{1,17},{9,25},{17,1},{25,9},{2,18},{10... | collective-permute-start | bytes 589832 | tf_op jit(solution)/shard_map/ppermute | solution.py:257
  63.3 12.2 %collective-permute-start.25 = (bf16[192,512]{1,0:T(8,128)(2,1)S(1)}, bf16[192,512]{1,0:T(8,128)(2,1)S(1)}, u32[]{:S(2)}, u32[]{:S(2)}) collective-permute-start(bf16[192,512]{1,0:T(8,128)(2,1)S(1)} %get-tuple-element.65), channel_id=1, source_target_pairs={{0,8},{8,0},{16,24},{24,16},{1,9},{9,1},{17,25},{25,17},{2,10},{10... | collective-permute-start | bytes 589832 | tf_op jit(solution)/shard_map/ppermute | solution.py:257
  66.9 8.6 %collective-permute-start.28 = (bf16[64,512]{1,0:T(8,128)(2,1)S(1)}, bf16[64,512]{1,0:T(8,128)(2,1)S(1)}, u32[]{:S(2)}, u32[]{:S(2)}) collective-permute-start(bf16[64,512]{1,0:T(8,128)(2,1)S(1)} %get-tuple-element.68), channel_id=1, source_target_pairs={{0,24},{8,16},{16,8},{24,0},{1,25},{9,17},{17,9},{25,1},{2,26},{10... | collective-permute-start | bytes 196616 | tf_op jit(solution)/shard_map/ppermute | solution.py:257
  68.0 7.6 %collective-permute-start.29 = (bf16[64,512]{1,0:T(8,128)(2,1)S(1)}, bf16[64,512]{1,0:T(8,128)(2,1)S(1)}, u32[]{:S(2)}, u32[]{:S(2)}) collective-permute-start(bf16[64,512]{1,0:T(8,128)(2,1)S(1)} %get-tuple-element.69), channel_id=1, source_target_pairs={{0,16},{8,24},{16,0},{24,8},{1,17},{9,25},{17,1},{25,9},{2,18},{10... | collective-permute-start | bytes 196616 | tf_op jit(solution)/shard_map/ppermute | solution.py:257
  68.6 6.9 %collective-permute-start.30 = (bf16[64,512]{1,0:T(8,128)(2,1)S(1)}, bf16[64,512]{1,0:T(8,128)(2,1)S(1)}, u32[]{:S(2)}, u32[]{:S(2)}) collective-permute-start(bf16[64,512]{1,0:T(8,128)(2,1)S(1)} %get-tuple-element.70), channel_id=1, source_target_pairs={{0,8},{8,0},{16,24},{24,16},{1,9},{9,1},{17,25},{25,17},{2,10},{10... | collective-permute-start | bytes 196616 | tf_op jit(solution)/shard_map/ppermute | solution.py:257

commit v5 on v4

--- a/solution.py
+++ b/solution.py
@@ -164,7 +164,8 @@
     steps = features // tall
     pending = [None] * depth
     gather_parts((main_rows, last_rows), rows)
-    bias_out[...] = jnp.sum(rows[...].astype(F32), axis=0, keepdims=True)
+    ones = jnp.ones((16, rows.shape[0]), BF16)
+    bias_out[...] = jnp.dot(ones, rows[...], preferred_element_type=F32)[:1]
     for source in range(layers):
         used = source <= lax.axis_index("layer")
         for step in range(steps):
@@ -333,7 +334,7 @@
         2 * first * layers * features,
     )(order, *main_acts[::-1])
 
-    columns = min(512, width)
+    columns = width
     acts_all, keep, send, far_keep, far_send, norms = call(
         functools.partial(decode_kernel, layers, last, columns),
         (

time: 78.3 us -> 78 us (level)
  transfers between devices with their start and end apart: 31 -> 31, of which waited for: 16 -> 17; matrix products, arithmetic and copies ran while one was open for 0% -> 0% of each run, Pallas kernels for 18% -> 18%
where the time goes in v5:
time: 78 us; the launch traced here: 77.9 us
  starting transfers between devices  33.7 us (43%)
  waiting for transfers between devices  21.8 us (28%)
  Pallas kernels  19.3 us (25%)
  local copies, waits for them, and re-layouts  1.83 us (2%)
  between operations  1.01 us (1%)
    ppermute x19, waiting for transfers between devices, swap_tok(): return lax.ppermute(value, 'tok', [(i, i ^ step) for i in range(ranks)])  17.1 us
    ppermute x12, starting transfers between devices, swap_layer(): return lax.ppermute(value, 'layer', [(i, i ^ step) for i in range(layers)])  16.8 us
    ppermute x19, starting transfers between devices, swap_tok(): return lax.ppermute(value, 'tok', [(i, i ^ step) for i in range(ranks)])  16.8 us
    ppermute x12, waiting for transfers between devices, swap_layer(): return lax.ppermute(value, 'layer', [(i, i ^ step) for i in range(layers)])  4.73 us
    pallas_call x1, Pallas kernels, on_device(): call(functools.partial(decoder_grad_kernel, loss_scale), (struct((layers,...  4.69 us
    pallas_call x2, Pallas kernels, grad_acts(): call(functools.partial(grad_kernel, layers, len(pieces)), (*[struct((coun...  3.37 us
    pallas_call x1, Pallas kernels, on_device(): call(functools.partial(decode_kernel, layers, last, columns), (struct((ro...  2.77 us
    pallas_call x1, Pallas kernels, on_device(): call(functools.partial(order_kernel, len(late)), (struct((width, row_tota...  2.49 us
  transfers between devices with their start and end apart: 31, of which 17 were waited for; matrix products, arithmetic and copies ran while one was open for 0% of the time, Pallas kernels for 18%

profile of v5, /device:TPU:0, one launch (start us, length us, event | category | flops | bytes accessed | tf_op | source)
XLA Modules:
  0.0 77.9 jit_solution(12183494727184625971)
XLA Ops:
  0.6 4.1 %collective-permute-start = (bf16[32,2048]{1,0:T(8,128)(2,1)}, bf16[32,2048]{1,0:T(8,128)(2,1)S(1)}, u32[]{:S(2)}, u32[]{:S(2)}) collective-permute-start(bf16[32,2048]{1,0:T(8,128)(2,1)} %bitcast.18), channel_id=1, source_target_pairs={{0,4},{1,5},{2,6},{3,7},{4,0},{5,1},{6,2},{7,3},{8,12},{9,13},{10,... | collective-permute-start | bytes 393224 | tf_op jit(solution)/shard_map/ppermute | solution.py:255
  4.7 1.6 %collective-permute-start.2 = (bf16[32,2048]{1,0:T(8,128)(2,1)}, bf16[32,2048]{1,0:T(8,128)(2,1)S(1)}, u32[]{:S(2)}, u32[]{:S(2)}) collective-permute-start(bf16[32,2048]{1,0:T(8,128)(2,1)} %bitcast.19), channel_id=1, source_target_pairs={{0,2},{1,3},{2,0},{3,1},{4,6},{5,7},{6,4},{7,5},{8,10},{9,11},{10,... | collective-permute-start | bytes 393224 | tf_op jit(solution)/shard_map/ppermute | solution.py:255
  6.3 0.8 %copy-done.3 = s32[256]{0:T(256)S(1)} copy-done((s32[256]{0:T(256)S(1)}, s32[256]{0:T(256)}, u32[]{:S(2)}) %copy-start.3) | copy-done | bytes 1048
  7.2 0.1 shard_map.102.order.order_ref.refs_8_
  7.3 1.0 %copy-done.1 = bf16[1,32,2048]{2,1,0:T(8,128)(2,1)S(1)} copy-done((bf16[1,32,2048]{2,1,0:T(8,128)(2,1)S(1)}, bf16[1,32,2048]{2,1,0:T(8,128)(2,1)}, u32[]{:S(2)}) %copy-start.1) | copy-done | bytes 131096
  8.2 0.0 collective-permute-start.4
  8.2 3.1 %collective-permute-done.refs_3_.refs_2_ = bf16[32,2048]{1,0:T(8,128)(2,1)S(1)} collective-permute-done((bf16[32,2048]{1,0:T(8,128)(2,1)}, bf16[32,2048]{1,0:T(8,128)(2,1)S(1)}, u32[]{:S(2)}, u32[]{:S(2)}) %collective-permute-start) | collective-permute-done | bytes 131104 | tf_op jit(solution)/shard_map/ppermute | solution.py:255
  11.4 0.0 collective-permute-start.1
  11.4 0.2 collective-permute-done.2.refs_4_.refs_1_
  11.6 0.3 collective-permute-start.3
  11.9 1.1 %collective-permute-start.8 = (bf16[32,2048]{1,0:T(8,128)(2,1)S(1)}, bf16[32,2048]{1,0:T(8,128)(2,1)S(1)}, u32[]{:S(2)}, u32[]{:S(2)}) collective-permute-start(bf16[32,2048]{1,0:T(8,128)(2,1)S(1)} %collective-permute-done.refs_3_.refs_2_), channel_id=1, source_target_pairs={{0,2},{1,3},{2,0},{3,1},{4,6},{5,7},{6,4},{7,5},{8,10},{9,11},{10,... | collective-permute-start | bytes 393224 | tf_op jit(solution)/shard_map/ppermute | solution.py:255
  13.0 0.0 collective-permute-done.4.refs_2_.refs_3_
  13.0 0.0 collective-permute-done.1.refs_0_.refs_5_
  13.0 0.6 shard_map.103.refs_3_.after
  13.6 2.5 %collective-permute-start.5 = (bf16[192,512]{1,0:T(8,128)(2,1)S(1)}, bf16[192,512]{1,0:T(8,128)(2,1)S(1)}, u32[]{:S(2)}, u32[]{:S(2)}) collective-permute-start(bf16[192,512]{1,0:T(8,128)(2,1)S(1)} %shard_map.103.refs_3_.after), channel_id=1, source_target_pairs={{0,24},{8,16},{16,8},{24,0},{1,25},{9,17},{17,9},{25,1},{2,26},{10... | collective-permute-start | bytes 589832 | tf_op jit(solution)/shard_map/ppermute | solution.py:258
  16.1 1.9 %shard_map.105.refs_4_ = f32[4,512]{1,0:T(4,128)S(1)} custom-call(bf16[4,512,2048]{2,1,0:T(8,128)(2,1)S(1)} %bitcast.12, bf16[192,512]{1,0:T(8,128)(2,1)S(1)} %shard_map.103.refs_3_.after), custom_call_target="tpu_custom_call" | custom-call | flops 16777216 | bytes 8388608 | tf_op jit(solution)/shard_map/pallas_call | solution.py:306
  18.1 0.1 collective-permute-start.9
  18.1 0.9 %collective-permute-start.6 = (bf16[192,512]{1,0:T(8,128)(2,1)S(1)}, bf16[192,512]{1,0:T(8,128)(2,1)S(1)}, u32[]{:S(2)}, u32[]{:S(2)}) collective-permute-start(bf16[192,512]{1,0:T(8,128)(2,1)S(1)} %shard_map.103.refs_3_.after), channel_id=1, source_target_pairs={{0,16},{8,24},{16,0},{24,8},{1,17},{9,25},{17,1},{25,9},{2,18},{10... | collective-permute-start | bytes 589832 | tf_op jit(solution)/shard_map/ppermute | solution.py:258
  19.0 1.5 %collective-permute-start.7 = (bf16[192,512]{1,0:T(8,128)(2,1)S(1)}, bf16[192,512]{1,0:T(8,128)(2,1)S(1)}, u32[]{:S(2)}, u32[]{:S(2)}) collective-permute-start(bf16[192,512]{1,0:T(8,128)(2,1)S(1)} %shard_map.103.refs_3_.after), channel_id=1, source_target_pairs={{0,8},{8,0},{16,24},{24,16},{1,9},{9,1},{17,25},{25,17},{2,10},{10... | collective-permute-start | bytes 589832 | tf_op jit(solution)/shard_map/ppermute | solution.py:258
  20.5 0.5 shard_map.106.refs_3_
  21.0 1.2 %collective-permute-start.10 = (bf16[80,512]{1,0:T(8,128)(2,1)S(1)}, bf16[80,512]{1,0:T(8,128)(2,1)S(1)}, u32[]{:S(2)}, u32[]{:S(2)}) collective-permute-start(bf16[80,512]{1,0:T(8,128)(2,1)S(1)} %shard_map.106.refs_3_), channel_id=1, source_target_pairs={{0,24},{8,16},{16,8},{24,0},{1,25},{9,17},{17,9},{25,1},{2,26},{10... | collective-permute-start | bytes 245768 | tf_op jit(solution)/shard_map/ppermute | solution.py:258
  22.2 0.9 %collective-permute-start.11 = (bf16[80,512]{1,0:T(8,128)(2,1)S(1)}, bf16[80,512]{1,0:T(8,128)(2,1)S(1)}, u32[]{:S(2)}, u32[]{:S(2)}) collective-permute-start(bf16[80,512]{1,0:T(8,128)(2,1)S(1)} %shard_map.106.refs_3_), channel_id=1, source_target_pairs={{0,16},{8,24},{16,0},{24,8},{1,17},{9,25},{17,1},{25,9},{2,18},{10... | collective-permute-start | bytes 245768 | tf_op jit(solution)/shard_map/ppermute | solution.py:258
  23.1 1.5 %collective-permute-start.12 = (bf16[80,512]{1,0:T(8,128)(2,1)S(1)}, bf16[80,512]{1,0:T(8,128)(2,1)S(1)}, u32[]{:S(2)}, u32[]{:S(2)}) collective-permute-start(bf16[80,512]{1,0:T(8,128)(2,1)S(1)} %shard_map.106.refs_3_), channel_id=1, source_target_pairs={{0,8},{8,0},{16,24},{24,16},{1,9},{9,1},{17,25},{25,17},{2,10},{10... | collective-permute-start | bytes 245768 | tf_op jit(solution)/shard_map/ppermute | solution.py:258
  24.6 1.5 %collective-permute-done.6.refs_1_ = bf16[192,512]{1,0:T(8,128)(2,1)S(1)} collective-permute-done((bf16[192,512]{1,0:T(8,128)(2,1)S(1)}, bf16[192,512]{1,0:T(8,128)(2,1)S(1)}, u32[]{:S(2)}, u32[]{:S(2)}) %collective-permute-start.6) | collective-permute-done | bytes 196640 | tf_op jit(solution)/shard_map/ppermute | solution.py:258
  26.1 0.7 collective-permute-done.7.refs_2_
  26.8 0.4 shard_map.104.first_sorted
  27.2 2.0 %collective-permute-done.10.refs_0_ = bf16[80,512]{1,0:T(8,128)(2,1)S(1)} collective-permute-done((bf16[80,512]{1,0:T(8,128)(2,1)S(1)}, bf16[80,512]{1,0:T(8,128)(2,1)S(1)}, u32[]{:S(2)}, u32[]{:S(2)}) %collective-permute-start.10) | collective-permute-done | bytes 81952 | tf_op jit(solution)/shard_map/ppermute | solution.py:258
  29.2 0.2 collective-permute-done.11.refs_1_
  29.4 0.2 collective-permute-done.12.refs_2_
  29.6 2.8 %shard_map.107 = (bf16[256,2048]{1,0:T(8,128)(2,1)S(1)}, bf16[96,2048]{1,0:T(8,128)(2,1)S(1)}, bf16[96,2048]{1,0:T(8,128)(2,1)S(1)}, bf16[32,2048]{1,0:T(8,128)(...) custom-call(bf16[256,256]{1,0:T(8,128)(2,1)S(1)} %shard_map.102.order.order_ref.refs_8_, ...), custom_call_target="tpu_custom_call" | custom-call | flops 2147483648 | bytes 8388608 | tf_op jit(solution)/shard_map/pallas_call | solution.py:338
  32.4 0.0 copy-start.4
  32.4 0.0 copy-start.5
  32.4 0.1 collective-permute-start.14
  32.5 0.5 collective-permute-start.13
  33.0 0.8 %collective-permute-done.14 = bf16[32,2048]{1,0:T(8,128)(2,1)S(1)} collective-permute-done((bf16[32,2048]{1,0:T(8,128)(2,1)S(1)}, bf16[32,2048]{1,0:T(8,128)(2,1)S(1)}, u32[]{:S(2)}, u32[]{:S(2)}) %collective-permute-start.14) | collective-permute-done | bytes 131104 | tf_op jit(solution)/shard_map/ppermute | solution.py:255
  33.8 1.5 %collective-permute-start.15 = (bf16[32,2048]{1,0:T(8,128)(2,1)S(1)}, bf16[32,2048]{1,0:T(8,128)(2,1)S(1)}, u32[]{:S(2)}, u32[]{:S(2)}) collective-permute-start(bf16[32,2048]{1,0:T(8,128)(2,1)S(1)} %add_convert_fusion), channel_id=1, source_target_pairs={{0,2},{1,3},{2,0},{3,1},{4,6},{5,7},{6,4},{7,5},{8,10},{9,11},{10,... | collective-permute-start | bytes 393224 | tf_op jit(solution)/shard_map/ppermute | solution.py:255
  35.3 0.1 convert_add_fusion
  35.4 4.0 %collective-permute-done.15 = bf16[32,2048]{1,0:T(8,128)(2,1)S(1)} collective-permute-done((bf16[32,2048]{1,0:T(8,128)(2,1)S(1)}, bf16[32,2048]{1,0:T(8,128)(2,1)S(1)}, u32[]{:S(2)}, u32[]{:S(2)}) %collective-permute-start.15) | collective-permute-done | bytes 131104 | tf_op jit(solution)/shard_map/ppermute | solution.py:255
  39.5 1.5 %collective-permute-start.17 = (bf16[32,2048]{1,0:T(8,128)(2,1)S(1)}, bf16[32,2048]{1,0:T(8,128)(2,1)S(1)}, u32[]{:S(2)}, u32[]{:S(2)}) collective-permute-start(bf16[32,2048]{1,0:T(8,128)(2,1)S(1)} %slice.31), channel_id=1, source_target_pairs={{0,2},{1,3},{2,0},{3,1},{4,6},{5,7},{6,4},{7,5},{8,10},{9,11},{10,... | collective-permute-start | bytes 393224 | tf_op jit(solution)/shard_map/ppermute | solution.py:255
  40.9 2.4 %collective-permute-start.16 = (bf16[32,2048]{1,0:T(8,128)(2,1)S(1)}, bf16[32,2048]{1,0:T(8,128)(2,1)S(1)}, u32[]{:S(2)}, u32[]{:S(2)}) collective-permute-start(bf16[32,2048]{1,0:T(8,128)(2,1)S(1)} %fusion), channel_id=1, source_target_pairs={{0,4},{1,5},{2,6},{3,7},{4,0},{5,1},{6,2},{7,3},{8,12},{9,13},{10,... | collective-permute-start | bytes 393224 | tf_op jit(solution)/shard_map/ppermute | solution.py:255
  43.3 2.5 %shard_map.108 = (bf16[2048,256]{1,0:T(8,128)(2,1)S(1)}, bf16[4,2048,512]{2,1,0:T(8,128)(2,1)S(1)}) custom-call(bf16[32,2048]{1,0:T(8,128)(2,1)S(1)} %bitcast.22, bf16[32,2048]{1,0:T(8,128)(2,1)S(1)} %collective-permute-done.2.refs_4_.refs_1_, bf16[32,2048]{1,0:T(8,128)(2,1)S(1)} %collective-permute-done.refs_3_.refs_2_, ...), custom_call_target="tpu_custom_call" | custom-call | flops 268435456 | bytes 16777216 | tf_op jit(solution)/shard_map/pallas_call | solution.py:369
  45.8 0.6 collective-permute-done.17
  46.4 2.7 %collective-permute-done.16 = bf16[32,2048]{1,0:T(8,128)(2,1)S(1)} collective-permute-done((bf16[32,2048]{1,0:T(8,128)(2,1)S(1)}, bf16[32,2048]{1,0:T(8,128)(2,1)S(1)}, u32[]{:S(2)}, u32[]{:S(2)}) %collective-permute-start.16) | collective-permute-done | bytes 131104 | tf_op jit(solution)/shard_map/ppermute | solution.py:255
  49.2 0.1 fusion.5.refs_5_
  49.2 0.5 collective-permute-start.18
  49.8 2.6 %collective-permute-start.20 = (bf16[32,2048]{1,0:T(8,128)(2,1)S(1)}, bf16[32,2048]{1,0:T(8,128)(2,1)S(1)}, u32[]{:S(2)}, u32[]{:S(2)}) collective-permute-start(bf16[32,2048]{1,0:T(8,128)(2,1)S(1)} %fusion.5.refs_5_), channel_id=1, source_target_pairs={{0,2},{1,3},{2,0},{3,1},{4,6},{5,7},{6,4},{7,5},{8,10},{9,11},{10,... | collective-permute-start | bytes 393224 | tf_op jit(solution)/shard_map/ppermute | solution.py:255
  52.4 4.2 %collective-permute-done.18.refs_3_ = bf16[32,2048]{1,0:T(8,128)(2,1)S(1)} collective-permute-done((bf16[32,2048]{1,0:T(8,128)(2,1)S(1)}, bf16[32,2048]{1,0:T(8,128)(2,1)S(1)}, u32[]{:S(2)}, u32[]{:S(2)}) %collective-permute-start.18) | collective-permute-done | bytes 131104 | tf_op jit(solution)/shard_map/ppermute | solution.py:255
  56.5 0.2 collective-permute-done.20.refs_4_
  56.7 0.3 collective-permute-start.21
  57.0 0.3 collective-permute-start.26
  57.3 0.5 collective-permute-done.19.refs_0_
  57.9 0.2 collective-permute-done.21.refs_1_
  58.1 1.8 %shard_map.109 = (f32[192,512]{1,0:T(8,128)S(1)}, bf16[192,512]{1,0:T(8,128)(2,1)S(1)}, bf16[192,512]{1,0:T(8,128)(2,1)S(1)}, bf16[192,512]{1,0:T(8,128)(2,1)S(1)}, bf16[192,2048]{1,0:T(8,128)(2,1)S(1)}) custom-call(bf16[32,2048]{1,0:T(8,128)(2,1)S(1)} %collective-permute-done.19.refs_0_, bf16[32,2048]{1,0:T(8,128)(2,1)S(1)} %collective-permute-done.21.refs_1_, ...), custom_call_target="tpu_custom_call" | custom-call | flops 1610612736 | bytes 8388608 | tf_op jit(solution)/shard_map/pallas_call | solution.py:385
  59.9 2.2 %collective-permute-start.23 = (bf16[192,512]{1,0:T(8,128)(2,1)S(1)}, bf16[192,512]{1,0:T(8,128)(2,1)S(1)}, u32[]{:S(2)}, u32[]{:S(2)}) collective-permute-start(bf16[192,512]{1,0:T(8,128)(2,1)S(1)} %get-tuple-element.63), channel_id=1, source_target_pairs={{0,24},{8,16},{16,8},{24,0},{1,25},{9,17},{17,9},{25,1},{2,26},{10... | collective-permute-start | bytes 589832 | tf_op jit(solution)/shard_map/ppermute | solution.py:258
  62.1 0.5 collective-permute-done.26.refs_1_
  62.6 0.7 collective-permute-start.24
  63.3 2.0 %collective-permute-start.25 = (bf16[192,512]{1,0:T(8,128)(2,1)S(1)}, bf16[192,512]{1,0:T(8,128)(2,1)S(1)}, u32[]{:S(2)}, u32[]{:S(2)}) collective-permute-start(bf16[192,512]{1,0:T(8,128)(2,1)S(1)} %get-tuple-element.65), channel_id=1, source_target_pairs={{0,8},{8,0},{16,24},{24,16},{1,9},{9,1},{17,25},{25,17},{2,10},{10... | collective-permute-start | bytes 589832 | tf_op jit(solution)/shard_map/ppermute | solution.py:258
  65.4 1.6 %shard_map.110 = (f32[64,512]{1,0:T(8,128)S(1)}, bf16[64,512]{1,0:T(8,128)(2,1)S(1)}, bf16[64,512]{1,0:T(8,128)(2,1)S(1)}, bf16[64,512]{1,0:T(8,128)(2,1)S(1)}, bf16[64,2048]{1,0:T(8,128)(2,1)S(1)}) custom-call(bf16[32,2048]{1,0:T(8,128)(2,1)S(1)} %collective-permute-done.27.refs_0_, bf16[32,2048]{1,0:T(8,128)(2,1)S(1)} %collective-permute-done.26.refs_1_, ...), custom_call_target="tpu_custom_call" | custom-call | flops 536870912 | bytes 8388608 | tf_op jit(solution)/shard_map/pallas_call | solution.py:385
  66.9 0.8 %collective-permute-start.28 = (bf16[64,512]{1,0:T(8,128)(2,1)S(1)}, bf16[64,512]{1,0:T(8,128)(2,1)S(1)}, u32[]{:S(2)}, u32[]{:S(2)}) collective-permute-start(bf16[64,512]{1,0:T(8,128)(2,1)S(1)} %get-tuple-element.68), channel_id=1, source_target_pairs={{0,24},{8,16},{16,8},{24,0},{1,25},{9,17},{17,9},{25,1},{2,26},{10... | collective-permute-start | bytes 196616 | tf_op jit(solution)/shard_map/ppermute | solution.py:258
  67.8 0.7 collective-permute-start.29
  68.5 0.1 collective-permute-done.23.refs_0_
  68.6 1.9 %collective-permute-start.30 = (bf16[64,512]{1,0:T(8,128)(2,1)S(1)}, bf16[64,512]{1,0:T(8,128)(2,1)S(1)}, u32[]{:S(2)}, u32[]{:S(2)}) collective-permute-start(bf16[64,512]{1,0:T(8,128)(2,1)S(1)} %get-tuple-element.70), channel_id=1, source_target_pairs={{0,8},{8,0},{16,24},{24,16},{1,9},{9,1},{17,25},{25,17},{2,10},{10... | collective-permute-start | bytes 196616 | tf_op jit(solution)/shard_map/ppermute | solution.py:258
  70.5 4.7 %shard_map.112 = (bf16[4,512,2048]{2,1,0:T(8,128)(2,1)}, f32[1,2048]{1,0:T(1,128)}) custom-call(bf16[256,2048]{1,0:T(8,128)(2,1)S(1)} %get-tuple-element.59.acts, f32[4,512]{1,0:T(4,128)S(1)} %get-tuple-element.60.norms, bf16[192,2048]{1,0:T(8,128)(2,1)S(1)} %get-tuple-element.74.main_rows, bf16[64,2048]{1,0:T(8,128)(2,1)S(1)} %get-tuple-element.75.last_rows, ...), custom_call_target="tpu_custom_call" | custom-call | flops 2147483648 | bytes 16777216 | tf_op jit(solution)/shard_map/pallas_call | solution.py:405
  75.2 2.4 %shard_map.111 = (bf16[2048,512]{1,0:T(8,128)(2,1)}, f32[1,512]{1,0:T(1,128)}) custom-call(bf16[2048,256]{1,0:T(8,128)(2,1)S(1)} %get-tuple-element.58.ordered, bf16[256,2048]{1,0:T(8,128)(2,1)S(1)} %get-tuple-element.59.acts, f32[4,512]{1,0:T(4,128)S(1)} %get-tuple-element.60.norms, bf16[192,512]{1,0:T(8,128)(2,1)S(1)} %collective-permute-done.23.refs_0_, ...), custom_call_target="tpu_custom_call" | custom-call | flops 536870912 | bytes 2097152 | tf_op jit(solution)/shard_map/pallas_call | solution.py:420
  (31 shorter events, 0.1 us)
Async XLA Ops:
  0.6 10.7 %collective-permute-start = (bf16[32,2048]{1,0:T(8,128)(2,1)}, bf16[32,2048]{1,0:T(8,128)(2,1)S(1)}, u32[]{:S(2)}, u32[]{:S(2)}) collective-permute-start(bf16[32,2048]{1,0:T(8,128)(2,1)} %bitcast.18), channel_id=1, source_target_pairs={{0,4},{1,5},{2,6},{3,7},{4,0},{5,1},{6,2},{7,3},{8,12},{9,13},{10,... | collective-permute-start | bytes 393224 | tf_op jit(solution)/shard_map/ppermute | solution.py:255
  4.7 6.8 %collective-permute-start.2 = (bf16[32,2048]{1,0:T(8,128)(2,1)}, bf16[32,2048]{1,0:T(8,128)(2,1)S(1)}, u32[]{:S(2)}, u32[]{:S(2)}) collective-permute-start(bf16[32,2048]{1,0:T(8,128)(2,1)} %bitcast.19), channel_id=1, source_target_pairs={{0,2},{1,3},{2,0},{3,1},{4,6},{5,7},{6,4},{7,5},{8,10},{9,11},{10,... | collective-permute-start | bytes 393224 | tf_op jit(solution)/shard_map/ppermute | solution.py:255
  6.3 9.8 %slice-start = ((s8[8388608]{0:T(1024)(128)(4,1)}), s8[4194304]{0:T(1024)(128)(4,1)S(1)}, s32[]{:S(2)}) async-start(s8[8388608]{0:T(1024)(128)(4,1)} %bitcast.10), calls=%async_computation | async-start | bytes 8388608
  6.3 0.8 %copy-start.3 = (s32[256]{0:T(256)S(1)}, s32[256]{0:T(256)}, u32[]{:S(2)}) copy-start(s32[256]{0:T(256)} %param.9) | copy-start | bytes 3076
  7.1 1.1 %copy-start.1 = (bf16[1,32,2048]{2,1,0:T(8,128)(2,1)S(1)}, bf16[1,32,2048]{2,1,0:T(8,128)(2,1)}, u32[]{:S(2)}) copy-start(bf16[1,32,2048]{2,1,0:T(8,128)(2,1)} %param.7) | copy-start | bytes 393220
  7.1 5.9 %copy-start = (bf16[1,2048,512]{2,1,0:T(8,128)(2,1)S(1)}, bf16[1,2048,512]{2,1,0:T(8,128)(2,1)}, u32[]{:S(2)}) copy-start(bf16[1,2048,512]{2,1,0:T(8,128)(2,1)} %param.10) | copy-start | bytes 6291460
  7.1 5.9 %copy-start.2 = (f32[1,512]{1,0:T(1,128)S(1)}, f32[1,512]{1,0:T(1,128)}, u32[]{:S(2)}) copy-start(f32[1,512]{1,0:T(1,128)} %refs_3_.1) | copy-start | bytes 6148
  7.1 9.0 %slice-start.1 = ((s8[8388608]{0:T(1024)(128)(4,1)}), s8[4194304]{0:T(1024)(128)(4,1)S(1)}, s32[]{:S(2)}) async-start(s8[8388608]{0:T(1024)(128)(4,1)} %bitcast.10), calls=%async_computation.1 | async-start | bytes 8388608
  8.2 4.8 %collective-permute-start.4 = (bf16[32,2048]{1,0:T(8,128)(2,1)S(1)}, bf16[32,2048]{1,0:T(8,128)(2,1)S(1)}, u32[]{:S(2)}, u32[]{:S(2)}) collective-permute-start(bf16[32,2048]{1,0:T(8,128)(2,1)S(1)} %bitcast.20), channel_id=1, source_target_pairs={{0,1},{1,0},{2,3},{3,2},{4,5},{5,4},{6,7},{7,6},{8,9},{9,8},{10,11... | collective-permute-start | bytes 393224 | tf_op jit(solution)/shard_map/ppermute | solution.py:255
  11.4 1.6 %collective-permute-start.1 = (bf16[32,2048]{1,0:T(8,128)(2,1)S(1)}, bf16[32,2048]{1,0:T(8,128)(2,1)S(1)}, u32[]{:S(2)}, u32[]{:S(2)}) collective-permute-start(bf16[32,2048]{1,0:T(8,128)(2,1)S(1)} %collective-permute-done.refs_3_.refs_2_), channel_id=1, source_target_pairs={{0,1},{1,0},{2,3},{3,2},{4,5},{5,4},{6,7},{7,6},{8,9},{9,8},{10,11... | collective-permute-start | bytes 393224 | tf_op jit(solution)/shard_map/ppermute | solution.py:255
  11.6 1.4 %collective-permute-start.3 = (bf16[32,2048]{1,0:T(8,128)(2,1)S(1)}, bf16[32,2048]{1,0:T(8,128)(2,1)S(1)}, u32[]{:S(2)}, u32[]{:S(2)}) collective-permute-start(bf16[32,2048]{1,0:T(8,128)(2,1)S(1)} %collective-permute-done.2.refs_4_.refs_1_), channel_id=1, source_target_pairs={{0,1},{1,0},{2,3},{3,2},{4,5},{5,4},{6,7},{7,6},{8,9},{9,8},{10,11... | collective-permute-start | bytes 393224 | tf_op jit(solution)/shard_map/ppermute | solution.py:255
  11.9 6.2 %collective-permute-start.8 = (bf16[32,2048]{1,0:T(8,128)(2,1)S(1)}, bf16[32,2048]{1,0:T(8,128)(2,1)S(1)}, u32[]{:S(2)}, u32[]{:S(2)}) collective-permute-start(bf16[32,2048]{1,0:T(8,128)(2,1)S(1)} %collective-permute-done.refs_3_.refs_2_), channel_id=1, source_target_pairs={{0,2},{1,3},{2,0},{3,1},{4,6},{5,7},{6,4},{7,5},{8,10},{9,11},{10,... | collective-permute-start | bytes 393224 | tf_op jit(solution)/shard_map/ppermute | solution.py:255
  13.6 9.5 %collective-permute-start.5 = (bf16[192,512]{1,0:T(8,128)(2,1)S(1)}, bf16[192,512]{1,0:T(8,128)(2,1)S(1)}, u32[]{:S(2)}, u32[]{:S(2)}) collective-permute-start(bf16[192,512]{1,0:T(8,128)(2,1)S(1)} %shard_map.103.refs_3_.after), channel_id=1, source_target_pairs={{0,24},{8,16},{16,8},{24,0},{1,25},{9,17},{17,9},{25,1},{2,26},{10... | collective-permute-start | bytes 589832 | tf_op jit(solution)/shard_map/ppermute | solution.py:258
  18.1 2.5 %collective-permute-start.9 = (bf16[32,2048]{1,0:T(8,128)(2,1)S(1)}, bf16[32,2048]{1,0:T(8,128)(2,1)S(1)}, u32[]{:S(2)}, u32[]{:S(2)}) collective-permute-start(bf16[32,2048]{1,0:T(8,128)(2,1)S(1)} %collective-permute-done.8.refs_0_.refs_6_), channel_id=1, source_target_pairs={{0,1},{1,0},{2,3},{3,2},{4,5},{5,4},{6,7},{7,6},{8,9},{9,8},{10,11... | collective-permute-start | bytes 393224 | tf_op jit(solution)/shard_map/ppermute | solution.py:255
  18.1 7.9 %collective-permute-start.6 = (bf16[192,512]{1,0:T(8,128)(2,1)S(1)}, bf16[192,512]{1,0:T(8,128)(2,1)S(1)}, u32[]{:S(2)}, u32[]{:S(2)}) collective-permute-start(bf16[192,512]{1,0:T(8,128)(2,1)S(1)} %shard_map.103.refs_3_.after), channel_id=1, source_target_pairs={{0,16},{8,24},{16,0},{24,8},{1,17},{9,25},{17,1},{25,9},{2,18},{10... | collective-permute-start | bytes 589832 | tf_op jit(solution)/shard_map/ppermute | solution.py:258
  19.0 7.7 %collective-permute-start.7 = (bf16[192,512]{1,0:T(8,128)(2,1)S(1)}, bf16[192,512]{1,0:T(8,128)(2,1)S(1)}, u32[]{:S(2)}, u32[]{:S(2)}) collective-permute-start(bf16[192,512]{1,0:T(8,128)(2,1)S(1)} %shard_map.103.refs_3_.after), channel_id=1, source_target_pairs={{0,8},{8,0},{16,24},{24,16},{1,9},{9,1},{17,25},{25,17},{2,10},{10... | collective-permute-start | bytes 589832 | tf_op jit(solution)/shard_map/ppermute | solution.py:258
  21.0 8.1 %collective-permute-start.10 = (bf16[80,512]{1,0:T(8,128)(2,1)S(1)}, bf16[80,512]{1,0:T(8,128)(2,1)S(1)}, u32[]{:S(2)}, u32[]{:S(2)}) collective-permute-start(bf16[80,512]{1,0:T(8,128)(2,1)S(1)} %shard_map.106.refs_3_), channel_id=1, source_target_pairs={{0,24},{8,16},{16,8},{24,0},{1,25},{9,17},{17,9},{25,1},{2,26},{10... | collective-permute-start | bytes 245768 | tf_op jit(solution)/shard_map/ppermute | solution.py:258
  22.2 7.1 %collective-permute-start.11 = (bf16[80,512]{1,0:T(8,128)(2,1)S(1)}, bf16[80,512]{1,0:T(8,128)(2,1)S(1)}, u32[]{:S(2)}, u32[]{:S(2)}) collective-permute-start(bf16[80,512]{1,0:T(8,128)(2,1)S(1)} %shard_map.106.refs_3_), channel_id=1, source_target_pairs={{0,16},{8,24},{16,0},{24,8},{1,17},{9,25},{17,1},{25,9},{2,18},{10... | collective-permute-start | bytes 245768 | tf_op jit(solution)/shard_map/ppermute | solution.py:258
  23.1 6.5 %collective-permute-start.12 = (bf16[80,512]{1,0:T(8,128)(2,1)S(1)}, bf16[80,512]{1,0:T(8,128)(2,1)S(1)}, u32[]{:S(2)}, u32[]{:S(2)}) collective-permute-start(bf16[80,512]{1,0:T(8,128)(2,1)S(1)} %shard_map.106.refs_3_), channel_id=1, source_target_pairs={{0,8},{8,0},{16,24},{24,16},{1,9},{9,1},{17,25},{25,17},{2,10},{10... | collective-permute-start | bytes 245768 | tf_op jit(solution)/shard_map/ppermute | solution.py:258
  32.4 16.8 %copy-start.4 = (bf16[1,32,2048]{2,1,0:T(8,128)(2,1)S(1)}, bf16[1,32,2048]{2,1,0:T(8,128)(2,1)}, u32[]{:S(2)}) copy-start(bf16[1,32,2048]{2,1,0:T(8,128)(2,1)} %param.8) | copy-start | bytes 393220
  32.4 16.8 %copy-start.5 = (f32[1,2048]{1,0:T(1,128)S(1)}, f32[1,2048]{1,0:T(1,128)}, u32[]{:S(2)}) copy-start(f32[1,2048]{1,0:T(1,128)} %param.13) | copy-start | bytes 24580
  32.4 1.4 %collective-permute-start.14 = (bf16[32,2048]{1,0:T(8,128)(2,1)S(1)}, bf16[32,2048]{1,0:T(8,128)(2,1)S(1)}, u32[]{:S(2)}, u32[]{:S(2)}) collective-permute-start(bf16[32,2048]{1,0:T(8,128)(2,1)S(1)} %get-tuple-element.46), channel_id=1, source_target_pairs={{0,1},{1,0},{2,3},{3,2},{4,5},{5,4},{6,7},{7,6},{8,9},{9,8},{10,11... | collective-permute-start | bytes 393224 | tf_op jit(solution)/shard_map/ppermute | solution.py:255
  32.5 2.8 %collective-permute-start.13 = (bf16[96,2048]{1,0:T(8,128)(2,1)S(1)}, bf16[96,2048]{1,0:T(8,128)(2,1)S(1)}, u32[]{:S(2)}, u32[]{:S(2)}) collective-permute-start(bf16[96,2048]{1,0:T(8,128)(2,1)S(1)} %get-tuple-element.44), channel_id=1, source_target_pairs={{0,1},{1,0},{2,3},{3,2},{4,5},{5,4},{6,7},{7,6},{8,9},{9,8},{10,11... | collective-permute-start | bytes 1179656 | tf_op jit(solution)/shard_map/ppermute | solution.py:255
  33.8 5.6 %collective-permute-start.15 = (bf16[32,2048]{1,0:T(8,128)(2,1)S(1)}, bf16[32,2048]{1,0:T(8,128)(2,1)S(1)}, u32[]{:S(2)}, u32[]{:S(2)}) collective-permute-start(bf16[32,2048]{1,0:T(8,128)(2,1)S(1)} %add_convert_fusion), channel_id=1, source_target_pairs={{0,2},{1,3},{2,0},{3,1},{4,6},{5,7},{6,4},{7,5},{8,10},{9,11},{10,... | collective-permute-start | bytes 393224 | tf_op jit(solution)/shard_map/ppermute | solution.py:255
  39.5 7.0 %collective-permute-start.17 = (bf16[32,2048]{1,0:T(8,128)(2,1)S(1)}, bf16[32,2048]{1,0:T(8,128)(2,1)S(1)}, u32[]{:S(2)}, u32[]{:S(2)}) collective-permute-start(bf16[32,2048]{1,0:T(8,128)(2,1)S(1)} %slice.31), channel_id=1, source_target_pairs={{0,2},{1,3},{2,0},{3,1},{4,6},{5,7},{6,4},{7,5},{8,10},{9,11},{10,... | collective-permute-start | bytes 393224 | tf_op jit(solution)/shard_map/ppermute | solution.py:255
  40.9 8.2 %collective-permute-start.16 = (bf16[32,2048]{1,0:T(8,128)(2,1)S(1)}, bf16[32,2048]{1,0:T(8,128)(2,1)S(1)}, u32[]{:S(2)}, u32[]{:S(2)}) collective-permute-start(bf16[32,2048]{1,0:T(8,128)(2,1)S(1)} %fusion), channel_id=1, source_target_pairs={{0,4},{1,5},{2,6},{3,7},{4,0},{5,1},{6,2},{7,3},{8,12},{9,13},{10,... | collective-permute-start | bytes 393224 | tf_op jit(solution)/shard_map/ppermute | solution.py:255
  49.2 7.3 %collective-permute-start.18 = (bf16[32,2048]{1,0:T(8,128)(2,1)S(1)}, bf16[32,2048]{1,0:T(8,128)(2,1)S(1)}, u32[]{:S(2)}, u32[]{:S(2)}) collective-permute-start(bf16[32,2048]{1,0:T(8,128)(2,1)S(1)} %fusion.5.refs_5_), channel_id=1, source_target_pairs={{0,4},{1,5},{2,6},{3,7},{4,0},{5,1},{6,2},{7,3},{8,12},{9,13},{10,... | collective-permute-start | bytes 393224 | tf_op jit(solution)/shard_map/ppermute | solution.py:255
  49.8 6.9 %collective-permute-start.20 = (bf16[32,2048]{1,0:T(8,128)(2,1)S(1)}, bf16[32,2048]{1,0:T(8,128)(2,1)S(1)}, u32[]{:S(2)}, u32[]{:S(2)}) collective-permute-start(bf16[32,2048]{1,0:T(8,128)(2,1)S(1)} %fusion.5.refs_5_), channel_id=1, source_target_pairs={{0,2},{1,3},{2,0},{3,1},{4,6},{5,7},{6,4},{7,5},{8,10},{9,11},{10,... | collective-permute-start | bytes 393224 | tf_op jit(solution)/shard_map/ppermute | solution.py:255
  52.4 5.0 %collective-permute-start.22 = (bf16[32,2048]{1,0:T(8,128)(2,1)S(1)}, bf16[32,2048]{1,0:T(8,128)(2,1)S(1)}, u32[]{:S(2)}, u32[]{:S(2)}) collective-permute-start(bf16[32,2048]{1,0:T(8,128)(2,1)S(1)} %fusion.5.refs_5_), channel_id=1, source_target_pairs={{0,1},{1,0},{2,3},{3,2},{4,5},{5,4},{6,7},{7,6},{8,9},{9,8},{10,11... | collective-permute-start | bytes 393224 | tf_op jit(solution)/shard_map/ppermute | solution.py:255
  56.5 1.3 %collective-permute-start.19 = (bf16[32,2048]{1,0:T(8,128)(2,1)S(1)}, bf16[32,2048]{1,0:T(8,128)(2,1)S(1)}, u32[]{:S(2)}, u32[]{:S(2)}) collective-permute-start(bf16[32,2048]{1,0:T(8,128)(2,1)S(1)} %collective-permute-done.18.refs_3_), channel_id=1, source_target_pairs={{0,1},{1,0},{2,3},{3,2},{4,5},{5,4},{6,7},{7,6},{8,9},{9,8},{10,11... | collective-permute-start | bytes 393224 | tf_op jit(solution)/shard_map/ppermute | solution.py:255
  56.7 1.4 %collective-permute-start.21 = (bf16[32,2048]{1,0:T(8,128)(2,1)S(1)}, bf16[32,2048]{1,0:T(8,128)(2,1)S(1)}, u32[]{:S(2)}, u32[]{:S(2)}) collective-permute-start(bf16[32,2048]{1,0:T(8,128)(2,1)S(1)} %collective-permute-done.20.refs_4_), channel_id=1, source_target_pairs={{0,1},{1,0},{2,3},{3,2},{4,5},{5,4},{6,7},{7,6},{8,9},{9,8},{10,11... | collective-permute-start | bytes 393224 | tf_op jit(solution)/shard_map/ppermute | solution.py:255
  57.0 5.6 %collective-permute-start.26 = (bf16[32,2048]{1,0:T(8,128)(2,1)S(1)}, bf16[32,2048]{1,0:T(8,128)(2,1)S(1)}, u32[]{:S(2)}, u32[]{:S(2)}) collective-permute-start(bf16[32,2048]{1,0:T(8,128)(2,1)S(1)} %collective-permute-done.18.refs_3_), channel_id=1, source_target_pairs={{0,2},{1,3},{2,0},{3,1},{4,6},{5,7},{6,4},{7,5},{8,10},{9,11},{10,... | collective-permute-start | bytes 393224 | tf_op jit(solution)/shard_map/ppermute | solution.py:255
  59.9 8.7 %collective-permute-start.23 = (bf16[192,512]{1,0:T(8,128)(2,1)S(1)}, bf16[192,512]{1,0:T(8,128)(2,1)S(1)}, u32[]{:S(2)}, u32[]{:S(2)}) collective-permute-start(bf16[192,512]{1,0:T(8,128)(2,1)S(1)} %get-tuple-element.63), channel_id=1, source_target_pairs={{0,24},{8,16},{16,8},{24,0},{1,25},{9,17},{17,9},{25,1},{2,26},{10... | collective-permute-start | bytes 589832 | tf_op jit(solution)/shard_map/ppermute | solution.py:258
  62.6 2.8 %collective-permute-start.27 = (bf16[32,2048]{1,0:T(8,128)(2,1)S(1)}, bf16[32,2048]{1,0:T(8,128)(2,1)S(1)}, u32[]{:S(2)}, u32[]{:S(2)}) collective-permute-start(bf16[32,2048]{1,0:T(8,128)(2,1)S(1)} %collective-permute-done.26.refs_1_), channel_id=1, source_target_pairs={{0,1},{1,0},{2,3},{3,2},{4,5},{5,4},{6,7},{7,6},{8,9},{9,8},{10,11... | collective-permute-start | bytes 393224 | tf_op jit(solution)/shard_map/ppermute | solution.py:255
  62.6 12.6 %collective-permute-start.24 = (bf16[192,512]{1,0:T(8,128)(2,1)S(1)}, bf16[192,512]{1,0:T(8,128)(2,1)S(1)}, u32[]{:S(2)}, u32[]{:S(2)}) collective-permute-start(bf16[192,512]{1,0:T(8,128)(2,1)S(1)} %get-tuple-element.64), channel_id=1, source_target_pairs={{0,16},{8,24},{16,0},{24,8},{1,17},{9,25},{17,1},{25,9},{2,18},{10... | collective-permute-start | bytes 589832 | tf_op jit(solution)/shard_map/ppermute | solution.py:258
  63.3 11.9 %collective-permute-start.25 = (bf16[192,512]{1,0:T(8,128)(2,1)S(1)}, bf16[192,512]{1,0:T(8,128)(2,1)S(1)}, u32[]{:S(2)}, u32[]{:S(2)}) collective-permute-start(bf16[192,512]{1,0:T(8,128)(2,1)S(1)} %get-tuple-element.65), channel_id=1, source_target_pairs={{0,8},{8,0},{16,24},{24,16},{1,9},{9,1},{17,25},{25,17},{2,10},{10... | collective-permute-start | bytes 589832 | tf_op jit(solution)/shard_map/ppermute | solution.py:258
  66.9 8.3 %collective-permute-start.28 = (bf16[64,512]{1,0:T(8,128)(2,1)S(1)}, bf16[64,512]{1,0:T(8,128)(2,1)S(1)}, u32[]{:S(2)}, u32[]{:S(2)}) collective-permute-start(bf16[64,512]{1,0:T(8,128)(2,1)S(1)} %get-tuple-element.68), channel_id=1, source_target_pairs={{0,24},{8,16},{16,8},{24,0},{1,25},{9,17},{17,9},{25,1},{2,26},{10... | collective-permute-start | bytes 196616 | tf_op jit(solution)/shard_map/ppermute | solution.py:258
  67.8 7.5 %collective-permute-start.29 = (bf16[64,512]{1,0:T(8,128)(2,1)S(1)}, bf16[64,512]{1,0:T(8,128)(2,1)S(1)}, u32[]{:S(2)}, u32[]{:S(2)}) collective-permute-start(bf16[64,512]{1,0:T(8,128)(2,1)S(1)} %get-tuple-element.69), channel_id=1, source_target_pairs={{0,16},{8,24},{16,0},{24,8},{1,17},{9,25},{17,1},{25,9},{2,18},{10... | collective-permute-start | bytes 196616 | tf_op jit(solution)/shard_map/ppermute | solution.py:258
  68.6 6.6 %collective-permute-start.30 = (bf16[64,512]{1,0:T(8,128)(2,1)S(1)}, bf16[64,512]{1,0:T(8,128)(2,1)S(1)}, u32[]{:S(2)}, u32[]{:S(2)}) collective-permute-start(bf16[64,512]{1,0:T(8,128)(2,1)S(1)} %get-tuple-element.70), channel_id=1, source_target_pairs={{0,8},{8,0},{16,24},{24,16},{1,9},{9,1},{17,25},{25,17},{2,10},{10... | collective-permute-start | bytes 196616 | tf_op jit(solution)/shard_map/ppermute | solution.py:258

commit v6 on v5

--- a/solution.py
+++ b/solution.py
@@ -357,8 +357,6 @@
     for line in reversed(range(1, lines)):
         low = line & -line
         blocks[line] = parts[line].astype(BF16)
-        if low == 1 and line + 1 in blocks:
-            blocks[line], _ = lax.optimization_barrier((blocks[line], blocks[line + 1]))
         arrived = swap_tok(blocks[line], 2 * low)
         parts[line ^ low] = parts[line ^ low] + arrived.astype(F32)
     resid_full = (

time: 78 us -> 78 us (level)
  waiting for transfers between devices: 21.8 us -> 20.2 us
  starting transfers between devices: 33.7 us -> 35.2 us
    ppermute x19, waiting for transfers between devices: 17.1 us -> 15.6 us  [swap_tok(): return lax.ppermute(value, 'tok', [(i, i ^ step) for i in range(ranks)])]
    ppermute x19, starting transfers between devices: 16.8 us -> 18.3 us  [swap_tok(): return lax.ppermute(value, 'tok', [(i, i ^ step) for i in range(ranks)])]
  transfers between devices with their start and end apart: 31 -> 31, of which waited for: 17 -> 13; matrix products, arithmetic and copies ran while one was open for 0% -> 0% of each run, Pallas kernels for 18% -> 18%
where the time goes in v6:
time: 78 us; the launch traced here: 77.8 us
  starting transfers between devices  35.2 us (45%)
  waiting for transfers between devices  20.2 us (26%)
  Pallas kernels  19.3 us (25%)
  local copies, waits for them, and re-layouts  1.83 us (2%)
  between operations  1.03 us (1%)
    ppermute x19, starting transfers between devices, swap_tok(): return lax.ppermute(value, 'tok', [(i, i ^ step) for i in range(ranks)])  18.3 us
    ppermute x12, starting transfers between devices, swap_layer(): return lax.ppermute(value, 'layer', [(i, i ^ step) for i in range(layers)])  16.9 us
    ppermute x19, waiting for transfers between devices, swap_tok(): return lax.ppermute(value, 'tok', [(i, i ^ step) for i in range(ranks)])  15.6 us
    pallas_call x1, Pallas kernels, on_device(): call(functools.partial(decoder_grad_kernel, loss_scale), (struct((layers,...  4.69 us
    ppermute x12, waiting for transfers between devices, swap_layer(): return lax.ppermute(value, 'layer', [(i, i ^ step) for i in range(layers)])  4.59 us
    pallas_call x2, Pallas kernels, grad_acts(): call(functools.partial(grad_kernel, layers, len(pieces)), (*[struct((coun...  3.37 us
    pallas_call x1, Pallas kernels, on_device(): call(functools.partial(decode_kernel, layers, last, columns), (struct((ro...  2.77 us
    pallas_call x1, Pallas kernels, on_device(): call(functools.partial(order_kernel, len(late)), (struct((width, row_tota...  2.49 us
  transfers between devices with their start and end apart: 31, of which 13 were waited for; matrix products, arithmetic and copies ran while one was open for 0% of the time, Pallas kernels for 18%

profile of v6, /device:TPU:0, one launch (start us, length us, event | category | flops | bytes accessed | tf_op | source)
XLA Modules:
  0.0 77.8 jit_solution(12056227208585505480)
XLA Ops:
  0.6 4.1 %collective-permute-start = (bf16[32,2048]{1,0:T(8,128)(2,1)}, bf16[32,2048]{1,0:T(8,128)(2,1)S(1)}, u32[]{:S(2)}, u32[]{:S(2)}) collective-permute-start(bf16[32,2048]{1,0:T(8,128)(2,1)} %bitcast.18), channel_id=1, source_target_pairs={{0,4},{1,5},{2,6},{3,7},{4,0},{5,1},{6,2},{7,3},{8,12},{9,13},{10,... | collective-permute-start | bytes 393224 | tf_op jit(solution)/shard_map/ppermute | solution.py:255
  4.7 1.6 %collective-permute-start.2 = (bf16[32,2048]{1,0:T(8,128)(2,1)}, bf16[32,2048]{1,0:T(8,128)(2,1)S(1)}, u32[]{:S(2)}, u32[]{:S(2)}) collective-permute-start(bf16[32,2048]{1,0:T(8,128)(2,1)} %bitcast.19), channel_id=1, source_target_pairs={{0,2},{1,3},{2,0},{3,1},{4,6},{5,7},{6,4},{7,5},{8,10},{9,11},{10,... | collective-permute-start | bytes 393224 | tf_op jit(solution)/shard_map/ppermute | solution.py:255
  6.3 0.8 %copy-done.3 = s32[256]{0:T(256)S(1)} copy-done((s32[256]{0:T(256)S(1)}, s32[256]{0:T(256)}, u32[]{:S(2)}) %copy-start.3) | copy-done | bytes 1048
  7.2 0.1 shard_map.102.order.order_ref.refs_8_
  7.3 1.0 %copy-done.1 = bf16[1,32,2048]{2,1,0:T(8,128)(2,1)S(1)} copy-done((bf16[1,32,2048]{2,1,0:T(8,128)(2,1)S(1)}, bf16[1,32,2048]{2,1,0:T(8,128)(2,1)}, u32[]{:S(2)}) %copy-start.1) | copy-done | bytes 131096
  8.2 3.1 %collective-permute-done.refs_3_.refs_2_ = bf16[32,2048]{1,0:T(8,128)(2,1)S(1)} collective-permute-done((bf16[32,2048]{1,0:T(8,128)(2,1)}, bf16[32,2048]{1,0:T(8,128)(2,1)S(1)}, u32[]{:S(2)}, u32[]{:S(2)}) %collective-permute-start) | collective-permute-done | bytes 131104 | tf_op jit(solution)/shard_map/ppermute | solution.py:255
  11.4 0.0 collective-permute-start.1
  11.4 0.2 collective-permute-done.2.refs_4_.refs_1_
  11.6 0.3 collective-permute-start.3
  11.9 1.1 %collective-permute-start.8 = (bf16[32,2048]{1,0:T(8,128)(2,1)S(1)}, bf16[32,2048]{1,0:T(8,128)(2,1)S(1)}, u32[]{:S(2)}, u32[]{:S(2)}) collective-permute-start(bf16[32,2048]{1,0:T(8,128)(2,1)S(1)} %collective-permute-done.refs_3_.refs_2_), channel_id=1, source_target_pairs={{0,2},{1,3},{2,0},{3,1},{4,6},{5,7},{6,4},{7,5},{8,10},{9,11},{10,... | collective-permute-start | bytes 393224 | tf_op jit(solution)/shard_map/ppermute | solution.py:255
  13.0 0.0 collective-permute-done.3.refs_1_.refs_4_
  13.0 0.6 shard_map.103.refs_3_.after
  13.6 2.5 %collective-permute-start.5 = (bf16[192,512]{1,0:T(8,128)(2,1)S(1)}, bf16[192,512]{1,0:T(8,128)(2,1)S(1)}, u32[]{:S(2)}, u32[]{:S(2)}) collective-permute-start(bf16[192,512]{1,0:T(8,128)(2,1)S(1)} %shard_map.103.refs_3_.after), channel_id=1, source_target_pairs={{0,24},{8,16},{16,8},{24,0},{1,25},{9,17},{17,9},{25,1},{2,26},{10... | collective-permute-start | bytes 589832 | tf_op jit(solution)/shard_map/ppermute | solution.py:258
  16.1 1.9 %shard_map.105.refs_4_ = f32[4,512]{1,0:T(4,128)S(1)} custom-call(bf16[4,512,2048]{2,1,0:T(8,128)(2,1)S(1)} %bitcast.12, bf16[192,512]{1,0:T(8,128)(2,1)S(1)} %shard_map.103.refs_3_.after), custom_call_target="tpu_custom_call" | custom-call | flops 16777216 | bytes 8388608 | tf_op jit(solution)/shard_map/pallas_call | solution.py:306
  18.1 0.0 collective-permute-done.8.refs_0_.refs_6_
  18.1 0.1 collective-permute-start.9
  18.1 0.9 %collective-permute-start.6 = (bf16[192,512]{1,0:T(8,128)(2,1)S(1)}, bf16[192,512]{1,0:T(8,128)(2,1)S(1)}, u32[]{:S(2)}, u32[]{:S(2)}) collective-permute-start(bf16[192,512]{1,0:T(8,128)(2,1)S(1)} %shard_map.103.refs_3_.after), channel_id=1, source_target_pairs={{0,16},{8,24},{16,0},{24,8},{1,17},{9,25},{17,1},{25,9},{2,18},{10... | collective-permute-start | bytes 589832 | tf_op jit(solution)/shard_map/ppermute | solution.py:258
  19.0 1.5 %collective-permute-start.7 = (bf16[192,512]{1,0:T(8,128)(2,1)S(1)}, bf16[192,512]{1,0:T(8,128)(2,1)S(1)}, u32[]{:S(2)}, u32[]{:S(2)}) collective-permute-start(bf16[192,512]{1,0:T(8,128)(2,1)S(1)} %shard_map.103.refs_3_.after), channel_id=1, source_target_pairs={{0,8},{8,0},{16,24},{24,16},{1,9},{9,1},{17,25},{25,17},{2,10},{10... | collective-permute-start | bytes 589832 | tf_op jit(solution)/shard_map/ppermute | solution.py:258
  20.5 0.0 collective-permute-done.9.refs_1_.refs_7_
  20.5 0.5 shard_map.106.refs_3_
  21.0 1.2 %collective-permute-start.10 = (bf16[80,512]{1,0:T(8,128)(2,1)S(1)}, bf16[80,512]{1,0:T(8,128)(2,1)S(1)}, u32[]{:S(2)}, u32[]{:S(2)}) collective-permute-start(bf16[80,512]{1,0:T(8,128)(2,1)S(1)} %shard_map.106.refs_3_), channel_id=1, source_target_pairs={{0,24},{8,16},{16,8},{24,0},{1,25},{9,17},{17,9},{25,1},{2,26},{10... | collective-permute-start | bytes 245768 | tf_op jit(solution)/shard_map/ppermute | solution.py:258
  22.2 0.9 %collective-permute-start.11 = (bf16[80,512]{1,0:T(8,128)(2,1)S(1)}, bf16[80,512]{1,0:T(8,128)(2,1)S(1)}, u32[]{:S(2)}, u32[]{:S(2)}) collective-permute-start(bf16[80,512]{1,0:T(8,128)(2,1)S(1)} %shard_map.106.refs_3_), channel_id=1, source_target_pairs={{0,16},{8,24},{16,0},{24,8},{1,17},{9,25},{17,1},{25,9},{2,18},{10... | collective-permute-start | bytes 245768 | tf_op jit(solution)/shard_map/ppermute | solution.py:258
  23.1 0.0 collective-permute-done.5.refs_0_
  23.1 1.5 %collective-permute-start.12 = (bf16[80,512]{1,0:T(8,128)(2,1)S(1)}, bf16[80,512]{1,0:T(8,128)(2,1)S(1)}, u32[]{:S(2)}, u32[]{:S(2)}) collective-permute-start(bf16[80,512]{1,0:T(8,128)(2,1)S(1)} %shard_map.106.refs_3_), channel_id=1, source_target_pairs={{0,8},{8,0},{16,24},{24,16},{1,9},{9,1},{17,25},{25,17},{2,10},{10... | collective-permute-start | bytes 245768 | tf_op jit(solution)/shard_map/ppermute | solution.py:258
  24.6 1.5 %collective-permute-done.6.refs_1_ = bf16[192,512]{1,0:T(8,128)(2,1)S(1)} collective-permute-done((bf16[192,512]{1,0:T(8,128)(2,1)S(1)}, bf16[192,512]{1,0:T(8,128)(2,1)S(1)}, u32[]{:S(2)}, u32[]{:S(2)}) %collective-permute-start.6) | collective-permute-done | bytes 196640 | tf_op jit(solution)/shard_map/ppermute | solution.py:258
  26.1 0.7 collective-permute-done.7.refs_2_
  26.8 0.4 shard_map.104.first_sorted
  27.2 2.0 %collective-permute-done.10.refs_0_ = bf16[80,512]{1,0:T(8,128)(2,1)S(1)} collective-permute-done((bf16[80,512]{1,0:T(8,128)(2,1)S(1)}, bf16[80,512]{1,0:T(8,128)(2,1)S(1)}, u32[]{:S(2)}, u32[]{:S(2)}) %collective-permute-start.10) | collective-permute-done | bytes 81952 | tf_op jit(solution)/shard_map/ppermute | solution.py:258
  29.2 0.2 collective-permute-done.11.refs_1_
  29.4 0.2 collective-permute-done.12.refs_2_
  29.6 2.8 %shard_map.107 = (bf16[256,2048]{1,0:T(8,128)(2,1)S(1)}, bf16[96,2048]{1,0:T(8,128)(2,1)S(1)}, bf16[96,2048]{1,0:T(8,128)(2,1)S(1)}, bf16[32,2048]{1,0:T(8,128)(...) custom-call(bf16[256,256]{1,0:T(8,128)(2,1)S(1)} %shard_map.102.order.order_ref.refs_8_, ...), custom_call_target="tpu_custom_call" | custom-call | flops 2147483648 | bytes 8388608 | tf_op jit(solution)/shard_map/pallas_call | solution.py:338
  32.4 0.0 copy-start.4
  32.4 0.0 copy-start.5
  32.4 0.1 collective-permute-start.14
  32.5 0.5 collective-permute-start.13
  33.0 0.8 %collective-permute-done.14 = bf16[32,2048]{1,0:T(8,128)(2,1)S(1)} collective-permute-done((bf16[32,2048]{1,0:T(8,128)(2,1)S(1)}, bf16[32,2048]{1,0:T(8,128)(2,1)S(1)}, u32[]{:S(2)}, u32[]{:S(2)}) %collective-permute-start.14) | collective-permute-done | bytes 131104 | tf_op jit(solution)/shard_map/ppermute | solution.py:255
  33.8 1.5 %collective-permute-start.15 = (bf16[32,2048]{1,0:T(8,128)(2,1)S(1)}, bf16[32,2048]{1,0:T(8,128)(2,1)S(1)}, u32[]{:S(2)}, u32[]{:S(2)}) collective-permute-start(bf16[32,2048]{1,0:T(8,128)(2,1)S(1)} %add_convert_fusion), channel_id=1, source_target_pairs={{0,2},{1,3},{2,0},{3,1},{4,6},{5,7},{6,4},{7,5},{8,10},{9,11},{10,... | collective-permute-start | bytes 393224 | tf_op jit(solution)/shard_map/ppermute | solution.py:255
  35.3 0.1 convert_add_fusion
  35.4 0.7 collective-permute-start.17
  36.1 4.1 %collective-permute-done.15 = bf16[32,2048]{1,0:T(8,128)(2,1)S(1)} collective-permute-done((bf16[32,2048]{1,0:T(8,128)(2,1)S(1)}, bf16[32,2048]{1,0:T(8,128)(2,1)S(1)}, u32[]{:S(2)}, u32[]{:S(2)}) %collective-permute-start.15) | collective-permute-done | bytes 131104 | tf_op jit(solution)/shard_map/ppermute | solution.py:255
  40.3 2.5 %collective-permute-start.16 = (bf16[32,2048]{1,0:T(8,128)(2,1)S(1)}, bf16[32,2048]{1,0:T(8,128)(2,1)S(1)}, u32[]{:S(2)}, u32[]{:S(2)}) collective-permute-start(bf16[32,2048]{1,0:T(8,128)(2,1)S(1)} %fusion), channel_id=1, source_target_pairs={{0,4},{1,5},{2,6},{3,7},{4,0},{5,1},{6,2},{7,3},{8,12},{9,13},{10,... | collective-permute-start | bytes 393224 | tf_op jit(solution)/shard_map/ppermute | solution.py:255
  42.8 2.5 %shard_map.108 = (bf16[2048,256]{1,0:T(8,128)(2,1)S(1)}, bf16[4,2048,512]{2,1,0:T(8,128)(2,1)S(1)}) custom-call(bf16[32,2048]{1,0:T(8,128)(2,1)S(1)} %bitcast.22, bf16[32,2048]{1,0:T(8,128)(2,1)S(1)} %collective-permute-done.2.refs_4_.refs_1_, bf16[32,2048]{1,0:T(8,128)(2,1)S(1)} %collective-permute-done.refs_3_.refs_2_, ...), custom_call_target="tpu_custom_call" | custom-call | flops 268435456 | bytes 16777216 | tf_op jit(solution)/shard_map/pallas_call | solution.py:367
  45.3 0.0 collective-permute-done.17
  45.3 3.6 %collective-permute-done.16 = bf16[32,2048]{1,0:T(8,128)(2,1)S(1)} collective-permute-done((bf16[32,2048]{1,0:T(8,128)(2,1)S(1)}, bf16[32,2048]{1,0:T(8,128)(2,1)S(1)}, u32[]{:S(2)}, u32[]{:S(2)}) %collective-permute-start.16) | collective-permute-done | bytes 131104 | tf_op jit(solution)/shard_map/ppermute | solution.py:255
  48.9 0.1 fusion.5.refs_5_
  49.0 0.1 collective-permute-start.18
  49.1 4.3 %collective-permute-start.20 = (bf16[32,2048]{1,0:T(8,128)(2,1)S(1)}, bf16[32,2048]{1,0:T(8,128)(2,1)S(1)}, u32[]{:S(2)}, u32[]{:S(2)}) collective-permute-start(bf16[32,2048]{1,0:T(8,128)(2,1)S(1)} %fusion.5.refs_5_), channel_id=1, source_target_pairs={{0,2},{1,3},{2,0},{3,1},{4,6},{5,7},{6,4},{7,5},{8,10},{9,11},{10,... | collective-permute-start | bytes 393224 | tf_op jit(solution)/shard_map/ppermute | solution.py:255
  53.3 0.0 collective-permute-start.22
  53.4 3.1 %collective-permute-done.18.refs_3_ = bf16[32,2048]{1,0:T(8,128)(2,1)S(1)} collective-permute-done((bf16[32,2048]{1,0:T(8,128)(2,1)S(1)}, bf16[32,2048]{1,0:T(8,128)(2,1)S(1)}, u32[]{:S(2)}, u32[]{:S(2)}) %collective-permute-start.18) | collective-permute-done | bytes 131104 | tf_op jit(solution)/shard_map/ppermute | solution.py:255
  56.5 0.0 collective-permute-start.19
  56.5 0.4 collective-permute-done.20.refs_4_
  56.8 0.2 collective-permute-start.21
  57.0 1.4 %collective-permute-start.26 = (bf16[32,2048]{1,0:T(8,128)(2,1)S(1)}, bf16[32,2048]{1,0:T(8,128)(2,1)S(1)}, u32[]{:S(2)}, u32[]{:S(2)}) collective-permute-start(bf16[32,2048]{1,0:T(8,128)(2,1)S(1)} %collective-permute-done.18.refs_3_), channel_id=1, source_target_pairs={{0,2},{1,3},{2,0},{3,1},{4,6},{5,7},{6,4},{7,5},{8,10},{9,11},{10,... | collective-permute-start | bytes 393224 | tf_op jit(solution)/shard_map/ppermute | solution.py:255
  58.3 1.8 %shard_map.109 = (f32[192,512]{1,0:T(8,128)S(1)}, bf16[192,512]{1,0:T(8,128)(2,1)S(1)}, bf16[192,512]{1,0:T(8,128)(2,1)S(1)}, bf16[192,512]{1,0:T(8,128)(2,1)S(1)}, bf16[192,2048]{1,0:T(8,128)(2,1)S(1)}) custom-call(bf16[32,2048]{1,0:T(8,128)(2,1)S(1)} %collective-permute-done.19.refs_0_, bf16[32,2048]{1,0:T(8,128)(2,1)S(1)} %collective-permute-done.21.refs_1_, ...), custom_call_target="tpu_custom_call" | custom-call | flops 1610612736 | bytes 8388608 | tf_op jit(solution)/shard_map/pallas_call | solution.py:383
  60.2 2.3 %collective-permute-start.23 = (bf16[192,512]{1,0:T(8,128)(2,1)S(1)}, bf16[192,512]{1,0:T(8,128)(2,1)S(1)}, u32[]{:S(2)}, u32[]{:S(2)}) collective-permute-start(bf16[192,512]{1,0:T(8,128)(2,1)S(1)} %get-tuple-element.61), channel_id=1, source_target_pairs={{0,24},{8,16},{16,8},{24,0},{1,25},{9,17},{17,9},{25,1},{2,26},{10... | collective-permute-start | bytes 589832 | tf_op jit(solution)/shard_map/ppermute | solution.py:258
  62.5 0.2 collective-permute-done.26.refs_1_
  62.7 1.6 %collective-permute-start.24 = (bf16[192,512]{1,0:T(8,128)(2,1)S(1)}, bf16[192,512]{1,0:T(8,128)(2,1)S(1)}, u32[]{:S(2)}, u32[]{:S(2)}) collective-permute-start(bf16[192,512]{1,0:T(8,128)(2,1)S(1)} %get-tuple-element.62), channel_id=1, source_target_pairs={{0,16},{8,24},{16,0},{24,8},{1,17},{9,25},{17,1},{25,9},{2,18},{10... | collective-permute-start | bytes 589832 | tf_op jit(solution)/shard_map/ppermute | solution.py:258
  64.4 1.0 %collective-permute-start.25 = (bf16[192,512]{1,0:T(8,128)(2,1)S(1)}, bf16[192,512]{1,0:T(8,128)(2,1)S(1)}, u32[]{:S(2)}, u32[]{:S(2)}) collective-permute-start(bf16[192,512]{1,0:T(8,128)(2,1)S(1)} %get-tuple-element.63), channel_id=1, source_target_pairs={{0,8},{8,0},{16,24},{24,16},{1,9},{9,1},{17,25},{25,17},{2,10},{10... | collective-permute-start | bytes 589832 | tf_op jit(solution)/shard_map/ppermute | solution.py:258
  65.3 1.6 %shard_map.110 = (f32[64,512]{1,0:T(8,128)S(1)}, bf16[64,512]{1,0:T(8,128)(2,1)S(1)}, bf16[64,512]{1,0:T(8,128)(2,1)S(1)}, bf16[64,512]{1,0:T(8,128)(2,1)S(1)}, bf16[64,2048]{1,0:T(8,128)(2,1)S(1)}) custom-call(bf16[32,2048]{1,0:T(8,128)(2,1)S(1)} %collective-permute-done.27.refs_0_, bf16[32,2048]{1,0:T(8,128)(2,1)S(1)} %collective-permute-done.26.refs_1_, ...), custom_call_target="tpu_custom_call" | custom-call | flops 536870912 | bytes 8388608 | tf_op jit(solution)/shard_map/pallas_call | solution.py:383
  66.9 1.0 %collective-permute-start.28 = (bf16[64,512]{1,0:T(8,128)(2,1)S(1)}, bf16[64,512]{1,0:T(8,128)(2,1)S(1)}, u32[]{:S(2)}, u32[]{:S(2)}) collective-permute-start(bf16[64,512]{1,0:T(8,128)(2,1)S(1)} %get-tuple-element.66), channel_id=1, source_target_pairs={{0,24},{8,16},{16,8},{24,0},{1,25},{9,17},{17,9},{25,1},{2,26},{10... | collective-permute-start | bytes 196616 | tf_op jit(solution)/shard_map/ppermute | solution.py:258
  67.8 1.6 %collective-permute-start.29 = (bf16[64,512]{1,0:T(8,128)(2,1)S(1)}, bf16[64,512]{1,0:T(8,128)(2,1)S(1)}, u32[]{:S(2)}, u32[]{:S(2)}) collective-permute-start(bf16[64,512]{1,0:T(8,128)(2,1)S(1)} %get-tuple-element.67), channel_id=1, source_target_pairs={{0,16},{8,24},{16,0},{24,8},{1,17},{9,25},{17,1},{25,9},{2,18},{10... | collective-permute-start | bytes 196616 | tf_op jit(solution)/shard_map/ppermute | solution.py:258
  69.5 1.0 %collective-permute-start.30 = (bf16[64,512]{1,0:T(8,128)(2,1)S(1)}, bf16[64,512]{1,0:T(8,128)(2,1)S(1)}, u32[]{:S(2)}, u32[]{:S(2)}) collective-permute-start(bf16[64,512]{1,0:T(8,128)(2,1)S(1)} %get-tuple-element.68), channel_id=1, source_target_pairs={{0,8},{8,0},{16,24},{24,16},{1,9},{9,1},{17,25},{25,17},{2,10},{10... | collective-permute-start | bytes 196616 | tf_op jit(solution)/shard_map/ppermute | solution.py:258
  70.4 4.7 %shard_map.112 = (bf16[4,512,2048]{2,1,0:T(8,128)(2,1)}, f32[1,2048]{1,0:T(1,128)}) custom-call(bf16[256,2048]{1,0:T(8,128)(2,1)S(1)} %get-tuple-element.57.acts, f32[4,512]{1,0:T(4,128)S(1)} %get-tuple-element.58.norms, bf16[192,2048]{1,0:T(8,128)(2,1)S(1)} %get-tuple-element.72.main_rows, bf16[64,2048]{1,0:T(8,128)(2,1)S(1)} %get-tuple-element.73.last_rows, ...), custom_call_target="tpu_custom_call" | custom-call | flops 2147483648 | bytes 16777216 | tf_op jit(solution)/shard_map/pallas_call | solution.py:403
  75.2 2.4 %shard_map.111 = (bf16[2048,512]{1,0:T(8,128)(2,1)}, f32[1,512]{1,0:T(1,128)}) custom-call(bf16[2048,256]{1,0:T(8,128)(2,1)S(1)} %get-tuple-element.56.ordered, bf16[256,2048]{1,0:T(8,128)(2,1)S(1)} %get-tuple-element.57.acts, f32[4,512]{1,0:T(4,128)S(1)} %get-tuple-element.58.norms, bf16[192,512]{1,0:T(8,128)(2,1)S(1)} %collective-permute-done.23.refs_0_, ...), custom_call_target="tpu_custom_call" | custom-call | flops 536870912 | bytes 2097152 | tf_op jit(solution)/shard_map/pallas_call | solution.py:418
  (31 shorter events, 0.1 us)
Async XLA Ops:
  0.6 10.7 %collective-permute-start = (bf16[32,2048]{1,0:T(8,128)(2,1)}, bf16[32,2048]{1,0:T(8,128)(2,1)S(1)}, u32[]{:S(2)}, u32[]{:S(2)}) collective-permute-start(bf16[32,2048]{1,0:T(8,128)(2,1)} %bitcast.18), channel_id=1, source_target_pairs={{0,4},{1,5},{2,6},{3,7},{4,0},{5,1},{6,2},{7,3},{8,12},{9,13},{10,... | collective-permute-start | bytes 393224 | tf_op jit(solution)/shard_map/ppermute | solution.py:255
  4.7 6.8 %collective-permute-start.2 = (bf16[32,2048]{1,0:T(8,128)(2,1)}, bf16[32,2048]{1,0:T(8,128)(2,1)S(1)}, u32[]{:S(2)}, u32[]{:S(2)}) collective-permute-start(bf16[32,2048]{1,0:T(8,128)(2,1)} %bitcast.19), channel_id=1, source_target_pairs={{0,2},{1,3},{2,0},{3,1},{4,6},{5,7},{6,4},{7,5},{8,10},{9,11},{10,... | collective-permute-start | bytes 393224 | tf_op jit(solution)/shard_map/ppermute | solution.py:255
  6.3 9.8 %slice-start = ((s8[8388608]{0:T(1024)(128)(4,1)}), s8[4194304]{0:T(1024)(128)(4,1)S(1)}, s32[]{:S(2)}) async-start(s8[8388608]{0:T(1024)(128)(4,1)} %bitcast.10), calls=%async_computation | async-start | bytes 8388608
  6.3 0.8 %copy-start.3 = (s32[256]{0:T(256)S(1)}, s32[256]{0:T(256)}, u32[]{:S(2)}) copy-start(s32[256]{0:T(256)} %param.9) | copy-start | bytes 3076
  7.1 1.1 %copy-start.1 = (bf16[1,32,2048]{2,1,0:T(8,128)(2,1)S(1)}, bf16[1,32,2048]{2,1,0:T(8,128)(2,1)}, u32[]{:S(2)}) copy-start(bf16[1,32,2048]{2,1,0:T(8,128)(2,1)} %param.7) | copy-start | bytes 393220
  7.1 5.9 %copy-start = (bf16[1,2048,512]{2,1,0:T(8,128)(2,1)S(1)}, bf16[1,2048,512]{2,1,0:T(8,128)(2,1)}, u32[]{:S(2)}) copy-start(bf16[1,2048,512]{2,1,0:T(8,128)(2,1)} %param.10) | copy-start | bytes 6291460
  7.1 5.9 %copy-start.2 = (f32[1,512]{1,0:T(1,128)S(1)}, f32[1,512]{1,0:T(1,128)}, u32[]{:S(2)}) copy-start(f32[1,512]{1,0:T(1,128)} %refs_3_.1) | copy-start | bytes 6148
  7.1 9.0 %slice-start.1 = ((s8[8388608]{0:T(1024)(128)(4,1)}), s8[4194304]{0:T(1024)(128)(4,1)S(1)}, s32[]{:S(2)}) async-start(s8[8388608]{0:T(1024)(128)(4,1)} %bitcast.10), calls=%async_computation.1 | async-start | bytes 8388608
  8.2 4.8 %collective-permute-start.4 = (bf16[32,2048]{1,0:T(8,128)(2,1)S(1)}, bf16[32,2048]{1,0:T(8,128)(2,1)S(1)}, u32[]{:S(2)}, u32[]{:S(2)}) collective-permute-start(bf16[32,2048]{1,0:T(8,128)(2,1)S(1)} %bitcast.20), channel_id=1, source_target_pairs={{0,1},{1,0},{2,3},{3,2},{4,5},{5,4},{6,7},{7,6},{8,9},{9,8},{10,11... | collective-permute-start | bytes 393224 | tf_op jit(solution)/shard_map/ppermute | solution.py:255
  11.4 1.6 %collective-permute-start.1 = (bf16[32,2048]{1,0:T(8,128)(2,1)S(1)}, bf16[32,2048]{1,0:T(8,128)(2,1)S(1)}, u32[]{:S(2)}, u32[]{:S(2)}) collective-permute-start(bf16[32,2048]{1,0:T(8,128)(2,1)S(1)} %collective-permute-done.refs_3_.refs_2_), channel_id=1, source_target_pairs={{0,1},{1,0},{2,3},{3,2},{4,5},{5,4},{6,7},{7,6},{8,9},{9,8},{10,11... | collective-permute-start | bytes 393224 | tf_op jit(solution)/shard_map/ppermute | solution.py:255
  11.6 1.4 %collective-permute-start.3 = (bf16[32,2048]{1,0:T(8,128)(2,1)S(1)}, bf16[32,2048]{1,0:T(8,128)(2,1)S(1)}, u32[]{:S(2)}, u32[]{:S(2)}) collective-permute-start(bf16[32,2048]{1,0:T(8,128)(2,1)S(1)} %collective-permute-done.2.refs_4_.refs_1_), channel_id=1, source_target_pairs={{0,1},{1,0},{2,3},{3,2},{4,5},{5,4},{6,7},{7,6},{8,9},{9,8},{10,11... | collective-permute-start | bytes 393224 | tf_op jit(solution)/shard_map/ppermute | solution.py:255
  11.9 6.2 %collective-permute-start.8 = (bf16[32,2048]{1,0:T(8,128)(2,1)S(1)}, bf16[32,2048]{1,0:T(8,128)(2,1)S(1)}, u32[]{:S(2)}, u32[]{:S(2)}) collective-permute-start(bf16[32,2048]{1,0:T(8,128)(2,1)S(1)} %collective-permute-done.refs_3_.refs_2_), channel_id=1, source_target_pairs={{0,2},{1,3},{2,0},{3,1},{4,6},{5,7},{6,4},{7,5},{8,10},{9,11},{10,... | collective-permute-start | bytes 393224 | tf_op jit(solution)/shard_map/ppermute | solution.py:255
  13.6 9.5 %collective-permute-start.5 = (bf16[192,512]{1,0:T(8,128)(2,1)S(1)}, bf16[192,512]{1,0:T(8,128)(2,1)S(1)}, u32[]{:S(2)}, u32[]{:S(2)}) collective-permute-start(bf16[192,512]{1,0:T(8,128)(2,1)S(1)} %shard_map.103.refs_3_.after), channel_id=1, source_target_pairs={{0,24},{8,16},{16,8},{24,0},{1,25},{9,17},{17,9},{25,1},{2,26},{10... | collective-permute-start | bytes 589832 | tf_op jit(solution)/shard_map/ppermute | solution.py:258
  18.1 2.5 %collective-permute-start.9 = (bf16[32,2048]{1,0:T(8,128)(2,1)S(1)}, bf16[32,2048]{1,0:T(8,128)(2,1)S(1)}, u32[]{:S(2)}, u32[]{:S(2)}) collective-permute-start(bf16[32,2048]{1,0:T(8,128)(2,1)S(1)} %collective-permute-done.8.refs_0_.refs_6_), channel_id=1, source_target_pairs={{0,1},{1,0},{2,3},{3,2},{4,5},{5,4},{6,7},{7,6},{8,9},{9,8},{10,11... | collective-permute-start | bytes 393224 | tf_op jit(solution)/shard_map/ppermute | solution.py:255
  18.1 7.9 %collective-permute-start.6 = (bf16[192,512]{1,0:T(8,128)(2,1)S(1)}, bf16[192,512]{1,0:T(8,128)(2,1)S(1)}, u32[]{:S(2)}, u32[]{:S(2)}) collective-permute-start(bf16[192,512]{1,0:T(8,128)(2,1)S(1)} %shard_map.103.refs_3_.after), channel_id=1, source_target_pairs={{0,16},{8,24},{16,0},{24,8},{1,17},{9,25},{17,1},{25,9},{2,18},{10... | collective-permute-start | bytes 589832 | tf_op jit(solution)/shard_map/ppermute | solution.py:258
  19.0 7.7 %collective-permute-start.7 = (bf16[192,512]{1,0:T(8,128)(2,1)S(1)}, bf16[192,512]{1,0:T(8,128)(2,1)S(1)}, u32[]{:S(2)}, u32[]{:S(2)}) collective-permute-start(bf16[192,512]{1,0:T(8,128)(2,1)S(1)} %shard_map.103.refs_3_.after), channel_id=1, source_target_pairs={{0,8},{8,0},{16,24},{24,16},{1,9},{9,1},{17,25},{25,17},{2,10},{10... | collective-permute-start | bytes 589832 | tf_op jit(solution)/shard_map/ppermute | solution.py:258
  21.0 8.1 %collective-permute-start.10 = (bf16[80,512]{1,0:T(8,128)(2,1)S(1)}, bf16[80,512]{1,0:T(8,128)(2,1)S(1)}, u32[]{:S(2)}, u32[]{:S(2)}) collective-permute-start(bf16[80,512]{1,0:T(8,128)(2,1)S(1)} %shard_map.106.refs_3_), channel_id=1, source_target_pairs={{0,24},{8,16},{16,8},{24,0},{1,25},{9,17},{17,9},{25,1},{2,26},{10... | collective-permute-start | bytes 245768 | tf_op jit(solution)/shard_map/ppermute | solution.py:258
  22.2 7.1 %collective-permute-start.11 = (bf16[80,512]{1,0:T(8,128)(2,1)S(1)}, bf16[80,512]{1,0:T(8,128)(2,1)S(1)}, u32[]{:S(2)}, u32[]{:S(2)}) collective-permute-start(bf16[80,512]{1,0:T(8,128)(2,1)S(1)} %shard_map.106.refs_3_), channel_id=1, source_target_pairs={{0,16},{8,24},{16,0},{24,8},{1,17},{9,25},{17,1},{25,9},{2,18},{10... | collective-permute-start | bytes 245768 | tf_op jit(solution)/shard_map/ppermute | solution.py:258
  23.1 6.5 %collective-permute-start.12 = (bf16[80,512]{1,0:T(8,128)(2,1)S(1)}, bf16[80,512]{1,0:T(8,128)(2,1)S(1)}, u32[]{:S(2)}, u32[]{:S(2)}) collective-permute-start(bf16[80,512]{1,0:T(8,128)(2,1)S(1)} %shard_map.106.refs_3_), channel_id=1, source_target_pairs={{0,8},{8,0},{16,24},{24,16},{1,9},{9,1},{17,25},{25,17},{2,10},{10... | collective-permute-start | bytes 245768 | tf_op jit(solution)/shard_map/ppermute | solution.py:258
  32.4 16.5 %copy-start.4 = (bf16[1,32,2048]{2,1,0:T(8,128)(2,1)S(1)}, bf16[1,32,2048]{2,1,0:T(8,128)(2,1)}, u32[]{:S(2)}) copy-start(bf16[1,32,2048]{2,1,0:T(8,128)(2,1)} %param.8) | copy-start | bytes 393220
  32.4 16.5 %copy-start.5 = (f32[1,2048]{1,0:T(1,128)S(1)}, f32[1,2048]{1,0:T(1,128)}, u32[]{:S(2)}) copy-start(f32[1,2048]{1,0:T(1,128)} %param.13) | copy-start | bytes 24580
  32.4 1.4 %collective-permute-start.14 = (bf16[32,2048]{1,0:T(8,128)(2,1)S(1)}, bf16[32,2048]{1,0:T(8,128)(2,1)S(1)}, u32[]{:S(2)}, u32[]{:S(2)}) collective-permute-start(bf16[32,2048]{1,0:T(8,128)(2,1)S(1)} %get-tuple-element.45), channel_id=1, source_target_pairs={{0,1},{1,0},{2,3},{3,2},{4,5},{5,4},{6,7},{7,6},{8,9},{9,8},{10,11... | collective-permute-start | bytes 393224 | tf_op jit(solution)/shard_map/ppermute | solution.py:255
  32.5 2.8 %collective-permute-start.13 = (bf16[96,2048]{1,0:T(8,128)(2,1)S(1)}, bf16[96,2048]{1,0:T(8,128)(2,1)S(1)}, u32[]{:S(2)}, u32[]{:S(2)}) collective-permute-start(bf16[96,2048]{1,0:T(8,128)(2,1)S(1)} %get-tuple-element.43), channel_id=1, source_target_pairs={{0,1},{1,0},{2,3},{3,2},{4,5},{5,4},{6,7},{7,6},{8,9},{9,8},{10,11... | collective-permute-start | bytes 1179656 | tf_op jit(solution)/shard_map/ppermute | solution.py:255
  33.8 6.4 %collective-permute-start.15 = (bf16[32,2048]{1,0:T(8,128)(2,1)S(1)}, bf16[32,2048]{1,0:T(8,128)(2,1)S(1)}, u32[]{:S(2)}, u32[]{:S(2)}) collective-permute-start(bf16[32,2048]{1,0:T(8,128)(2,1)S(1)} %add_convert_fusion), channel_id=1, source_target_pairs={{0,2},{1,3},{2,0},{3,1},{4,6},{5,7},{6,4},{7,5},{8,10},{9,11},{10,... | collective-permute-start | bytes 393224 | tf_op jit(solution)/shard_map/ppermute | solution.py:255
  35.4 9.9 %collective-permute-start.17 = (bf16[32,2048]{1,0:T(8,128)(2,1)S(1)}, bf16[32,2048]{1,0:T(8,128)(2,1)S(1)}, u32[]{:S(2)}, u32[]{:S(2)}) collective-permute-start(bf16[32,2048]{1,0:T(8,128)(2,1)S(1)} %slice.31), channel_id=1, source_target_pairs={{0,2},{1,3},{2,0},{3,1},{4,6},{5,7},{6,4},{7,5},{8,10},{9,11},{10,... | collective-permute-start | bytes 393224 | tf_op jit(solution)/shard_map/ppermute | solution.py:255
  40.3 8.6 %collective-permute-start.16 = (bf16[32,2048]{1,0:T(8,128)(2,1)S(1)}, bf16[32,2048]{1,0:T(8,128)(2,1)S(1)}, u32[]{:S(2)}, u32[]{:S(2)}) collective-permute-start(bf16[32,2048]{1,0:T(8,128)(2,1)S(1)} %fusion), channel_id=1, source_target_pairs={{0,4},{1,5},{2,6},{3,7},{4,0},{5,1},{6,2},{7,3},{8,12},{9,13},{10,... | collective-permute-start | bytes 393224 | tf_op jit(solution)/shard_map/ppermute | solution.py:255
  49.0 7.4 %collective-permute-start.18 = (bf16[32,2048]{1,0:T(8,128)(2,1)S(1)}, bf16[32,2048]{1,0:T(8,128)(2,1)S(1)}, u32[]{:S(2)}, u32[]{:S(2)}) collective-permute-start(bf16[32,2048]{1,0:T(8,128)(2,1)S(1)} %fusion.5.refs_5_), channel_id=1, source_target_pairs={{0,4},{1,5},{2,6},{3,7},{4,0},{5,1},{6,2},{7,3},{8,12},{9,13},{10,... | collective-permute-start | bytes 393224 | tf_op jit(solution)/shard_map/ppermute | solution.py:255
  49.1 7.7 %collective-permute-start.20 = (bf16[32,2048]{1,0:T(8,128)(2,1)S(1)}, bf16[32,2048]{1,0:T(8,128)(2,1)S(1)}, u32[]{:S(2)}, u32[]{:S(2)}) collective-permute-start(bf16[32,2048]{1,0:T(8,128)(2,1)S(1)} %fusion.5.refs_5_), channel_id=1, source_target_pairs={{0,2},{1,3},{2,0},{3,1},{4,6},{5,7},{6,4},{7,5},{8,10},{9,11},{10,... | collective-permute-start | bytes 393224 | tf_op jit(solution)/shard_map/ppermute | solution.py:255
  53.3 5.0 %collective-permute-start.22 = (bf16[32,2048]{1,0:T(8,128)(2,1)S(1)}, bf16[32,2048]{1,0:T(8,128)(2,1)S(1)}, u32[]{:S(2)}, u32[]{:S(2)}) collective-permute-start(bf16[32,2048]{1,0:T(8,128)(2,1)S(1)} %fusion.5.refs_5_), channel_id=1, source_target_pairs={{0,1},{1,0},{2,3},{3,2},{4,5},{5,4},{6,7},{7,6},{8,9},{9,8},{10,11... | collective-permute-start | bytes 393224 | tf_op jit(solution)/shard_map/ppermute | solution.py:255
  56.5 1.9 %collective-permute-start.19 = (bf16[32,2048]{1,0:T(8,128)(2,1)S(1)}, bf16[32,2048]{1,0:T(8,128)(2,1)S(1)}, u32[]{:S(2)}, u32[]{:S(2)}) collective-permute-start(bf16[32,2048]{1,0:T(8,128)(2,1)S(1)} %collective-permute-done.18.refs_3_), channel_id=1, source_target_pairs={{0,1},{1,0},{2,3},{3,2},{4,5},{5,4},{6,7},{7,6},{8,9},{9,8},{10,11... | collective-permute-start | bytes 393224 | tf_op jit(solution)/shard_map/ppermute | solution.py:255
  56.8 1.5 %collective-permute-start.21 = (bf16[32,2048]{1,0:T(8,128)(2,1)S(1)}, bf16[32,2048]{1,0:T(8,128)(2,1)S(1)}, u32[]{:S(2)}, u32[]{:S(2)}) collective-permute-start(bf16[32,2048]{1,0:T(8,128)(2,1)S(1)} %collective-permute-done.20.refs_4_), channel_id=1, source_target_pairs={{0,1},{1,0},{2,3},{3,2},{4,5},{5,4},{6,7},{7,6},{8,9},{9,8},{10,11... | collective-permute-start | bytes 393224 | tf_op jit(solution)/shard_map/ppermute | solution.py:255
  57.0 5.8 %collective-permute-start.26 = (bf16[32,2048]{1,0:T(8,128)(2,1)S(1)}, bf16[32,2048]{1,0:T(8,128)(2,1)S(1)}, u32[]{:S(2)}, u32[]{:S(2)}) collective-permute-start(bf16[32,2048]{1,0:T(8,128)(2,1)S(1)} %collective-permute-done.18.refs_3_), channel_id=1, source_target_pairs={{0,2},{1,3},{2,0},{3,1},{4,6},{5,7},{6,4},{7,5},{8,10},{9,11},{10,... | collective-permute-start | bytes 393224 | tf_op jit(solution)/shard_map/ppermute | solution.py:255
  60.2 9.3 %collective-permute-start.23 = (bf16[192,512]{1,0:T(8,128)(2,1)S(1)}, bf16[192,512]{1,0:T(8,128)(2,1)S(1)}, u32[]{:S(2)}, u32[]{:S(2)}) collective-permute-start(bf16[192,512]{1,0:T(8,128)(2,1)S(1)} %get-tuple-element.61), channel_id=1, source_target_pairs={{0,24},{8,16},{16,8},{24,0},{1,25},{9,17},{17,9},{25,1},{2,26},{10... | collective-permute-start | bytes 589832 | tf_op jit(solution)/shard_map/ppermute | solution.py:258
  62.7 2.6 %collective-permute-start.27 = (bf16[32,2048]{1,0:T(8,128)(2,1)S(1)}, bf16[32,2048]{1,0:T(8,128)(2,1)S(1)}, u32[]{:S(2)}, u32[]{:S(2)}) collective-permute-start(bf16[32,2048]{1,0:T(8,128)(2,1)S(1)} %collective-permute-done.26.refs_1_), channel_id=1, source_target_pairs={{0,1},{1,0},{2,3},{3,2},{4,5},{5,4},{6,7},{7,6},{8,9},{9,8},{10,11... | collective-permute-start | bytes 393224 | tf_op jit(solution)/shard_map/ppermute | solution.py:255
  62.7 12.4 %collective-permute-start.24 = (bf16[192,512]{1,0:T(8,128)(2,1)S(1)}, bf16[192,512]{1,0:T(8,128)(2,1)S(1)}, u32[]{:S(2)}, u32[]{:S(2)}) collective-permute-start(bf16[192,512]{1,0:T(8,128)(2,1)S(1)} %get-tuple-element.62), channel_id=1, source_target_pairs={{0,16},{8,24},{16,0},{24,8},{1,17},{9,25},{17,1},{25,9},{2,18},{10... | collective-permute-start | bytes 589832 | tf_op jit(solution)/shard_map/ppermute | solution.py:258
  64.4 10.8 %collective-permute-start.25 = (bf16[192,512]{1,0:T(8,128)(2,1)S(1)}, bf16[192,512]{1,0:T(8,128)(2,1)S(1)}, u32[]{:S(2)}, u32[]{:S(2)}) collective-permute-start(bf16[192,512]{1,0:T(8,128)(2,1)S(1)} %get-tuple-element.63), channel_id=1, source_target_pairs={{0,8},{8,0},{16,24},{24,16},{1,9},{9,1},{17,25},{25,17},{2,10},{10... | collective-permute-start | bytes 589832 | tf_op jit(solution)/shard_map/ppermute | solution.py:258
  66.9 8.3 %collective-permute-start.28 = (bf16[64,512]{1,0:T(8,128)(2,1)S(1)}, bf16[64,512]{1,0:T(8,128)(2,1)S(1)}, u32[]{:S(2)}, u32[]{:S(2)}) collective-permute-start(bf16[64,512]{1,0:T(8,128)(2,1)S(1)} %get-tuple-element.66), channel_id=1, source_target_pairs={{0,24},{8,16},{16,8},{24,0},{1,25},{9,17},{17,9},{25,1},{2,26},{10... | collective-permute-start | bytes 196616 | tf_op jit(solution)/shard_map/ppermute | solution.py:258
  67.8 7.3 %collective-permute-start.29 = (bf16[64,512]{1,0:T(8,128)(2,1)S(1)}, bf16[64,512]{1,0:T(8,128)(2,1)S(1)}, u32[]{:S(2)}, u32[]{:S(2)}) collective-permute-start(bf16[64,512]{1,0:T(8,128)(2,1)S(1)} %get-tuple-element.67), channel_id=1, source_target_pairs={{0,16},{8,24},{16,0},{24,8},{1,17},{9,25},{17,1},{25,9},{2,18},{10... | collective-permute-start | bytes 196616 | tf_op jit(solution)/shard_map/ppermute | solution.py:258
  69.5 5.7 %collective-permute-start.30 = (bf16[64,512]{1,0:T(8,128)(2,1)S(1)}, bf16[64,512]{1,0:T(8,128)(2,1)S(1)}, u32[]{:S(2)}, u32[]{:S(2)}) collective-permute-start(bf16[64,512]{1,0:T(8,128)(2,1)S(1)} %get-tuple-element.68), channel_id=1, source_target_pairs={{0,8},{8,0},{16,24},{24,16},{1,9},{9,1},{17,25},{25,17},{2,10},{10... | collective-permute-start | bytes 196616 | tf_op jit(solution)/shard_map/ppermute | solution.py:258
